TPU v7x, 32 devices: a whole 2x2x4 slice. The times are simulated.
32 devices in a mesh: tm: 4 (over y, core), space: 8 (over z, x).
Axes of the slice: x: 2, y: 2, z: 4, core: 2. Of those that a mesh axis runs over, the one named last changes fastest.
Arguments:
- queries: bfloat16 [4, 8, 384, 1536], P('tm', 'space'), may hold values from -7 to 7
- keys: bfloat16 [4, 8, 384, 1536], P('tm', 'space'), may hold values from -7 to 7
- values: bfloat16 [4, 8, 384, 1536], P('tm', 'space'), may hold values from -2 to 2
- outputs: bfloat16 [4, 8, 384, 1536], P('tm', 'space'), may hold values from -2 to 2
- out_grads: bfloat16 [4, 8, 384, 1536], P('tm', 'space'), may hold values from -6 to 6
- log_sums: float32 [4, 8, 12, 384], P('tm', 'space'), may hold values from 8 to 9.5
- window_mask: int32 [4, 8, 9], P('tm', 'space'), may hold values 0 or 1
Outputs:
- query_grads: bfloat16 [4, 8, 384, 1536], P('tm', 'space')
- key_grads: bfloat16 [4, 8, 384, 1536], P('tm', 'space')
- value_grads: bfloat16 [4, 8, 384, 1536], P('tm', 'space')
All inputs are finite; a program needn't handle non-finite values. No bound on the sum of `window_mask` on one device may be relied on, other than what follows from the above.
Results may differ from a plain program's by a relative error of at most 0.0065.
Values may be sent and summed in bfloat16 or wider, within the bound.
No kernel may reach another device: no remote copies, remote signals or barrier semaphores. Data moves between devices by JAX's collectives and lax.ppermute only.
A program may use at most 192 MiB of HBM per device.

v0:
```python
import jax
import jax.numpy as jnp
from jax import lax
from jax.sharding import PartitionSpec as P


def with_halo(shard, sides, width):
    for axis, dim in sides:
        peers, length = (lax.axis_size(axis), shard.shape[dim])
        up = [(i, (i + 1) % peers) for i in range(peers - 1)]
        down = [(j, i) for i, j in up]
        last = lax.slice_in_dim(shard, length - width, length, axis=dim)
        initial = lax.slice_in_dim(shard, 0, width, axis=dim)
        before = lax.ppermute(last, axis, up)
        after = lax.ppermute(initial, axis, down)
        shard = jnp.concatenate([before, shard, after], axis=dim)
    return shard


def from_behind(value, axis, steps):
    count = lax.axis_size(axis)
    initial, last = (max(0, -steps), min(count, count - steps))
    return lax.ppermute(value, axis, [(source, source + steps) for source in range(initial, last)])


def round_keep(value):
    return lax.optimization_barrier(value.astype(jnp.bfloat16)).astype(jnp.float32)


def pair_terms(query_rows, grad_rows, sum_rows, delta_rows, flags, key_rows, value_rows):
    num_tiles, tile_len, full_width = query_rows.shape
    head_count = sum_rows.shape[1]
    head_width = full_width // head_count
    factor = head_width ** (-0.5)
    shape_four = (num_tiles, tile_len, head_count, head_width)
    query_heads = query_rows.reshape(shape_four)
    grad_heads = grad_rows.reshape(shape_four)
    key_heads = key_rows.reshape(shape_four)
    value_heads = value_rows.reshape(shape_four)
    scores = (
        jnp.einsum("nqhd,nkhd->nhqk", query_heads, key_heads, preferred_element_type=jnp.float32)
        * factor
    )
    weights = jnp.exp(scores - sum_rows[..., None]) * flags[:, None, None, None]
    weights_low = weights.astype(jnp.bfloat16)
    grad_prob = jnp.einsum(
        "nqhd,nkhd->nhqk", grad_heads, value_heads, preferred_element_type=jnp.float32
    )
    grad_score = (weights * (grad_prob - delta_rows[..., None])).astype(jnp.bfloat16)
    query_term = (
        jnp.einsum("nhqk,nkhd->nqhd", grad_score, key_heads, preferred_element_type=jnp.float32)
        * factor
    )
    key_term = (
        jnp.einsum("nhqk,nqhd->nkhd", grad_score, query_heads, preferred_element_type=jnp.float32)
        * factor
    )
    value_term = jnp.einsum(
        "nhqk,nqhd->nkhd", weights_low, grad_heads, preferred_element_type=jnp.float32
    )
    flat = (num_tiles, tile_len, full_width)
    return (query_term.reshape(flat), key_term.reshape(flat), value_term.reshape(flat))


def spread(minus, centre, plus, axis_dim):
    count = centre.shape[axis_dim]
    zero_shape = list(centre.shape)
    zero_shape[axis_dim] = 1
    zero_row = jnp.zeros(tuple(zero_shape), centre.dtype)
    lower = jnp.concatenate((lax.slice_in_dim(minus, 1, count, 1, axis_dim), zero_row), axis_dim)
    upper = jnp.concatenate((zero_row, lax.slice_in_dim(plus, 0, count - 1, 1, axis_dim)), axis_dim)
    interior = centre + lower + upper
    rim_before = lax.index_in_dim(minus, 0, axis_dim, False)
    rim_after = lax.index_in_dim(plus, count - 1, axis_dim, False)
    return (interior, rim_before, rim_after)


def per_device(queries, keys, values, outputs, out_grads, log_sums, window_mask):
    time_tiles, row_tiles, tile_len, full_width = queries.shape
    head_count = log_sums.shape[2]
    head_width = full_width // head_count
    num_tiles = time_tiles * row_tiles
    all_times = time_tiles * lax.axis_size("tm")
    all_rows = row_tiles * lax.axis_size("space")
    first_time = lax.axis_index("tm") * time_tiles
    first_row = lax.axis_index("space") * row_tiles
    products = out_grads.astype(jnp.float32) * outputs.astype(jnp.float32)
    deltas = (
        products.reshape(time_tiles, row_tiles, tile_len, head_count, head_width)
        .sum(-1)
        .transpose(0, 1, 3, 2)
    )
    flat = (num_tiles, tile_len, full_width)
    query_flat = queries.reshape(flat)
    grad_flat = out_grads.reshape(flat)
    sums_flat = log_sums.reshape(num_tiles, head_count, tile_len)
    deltas_flat = deltas.reshape(num_tiles, head_count, tile_len)
    pair_kv = with_halo(jnp.stack((keys, values)), (("tm", 1), ("space", 2)), 1)
    times_here = first_time + jnp.arange(time_tiles, dtype=jnp.int32)
    rows_here = first_row + jnp.arange(row_tiles, dtype=jnp.int32)
    query_total = jnp.zeros(flat, jnp.float32)
    interiors = []
    befores = []
    afters = []
    for time_off in (-1, 0, 1):
        pieces = []
        for row_off in (-1, 0, 1):
            slab = pair_kv[
                :, 1 + time_off : 1 + time_off + time_tiles, 1 + row_off : 1 + row_off + row_tiles
            ]
            slab = slab.reshape((2,) + flat)
            time_inside = jnp.logical_and(
                times_here + time_off >= 0, times_here + time_off < all_times
            )
            row_inside = jnp.logical_and(rows_here + row_off >= 0, rows_here + row_off < all_rows)
            inside = jnp.logical_and(time_inside[:, None], row_inside[None, :])
            slot_index = (time_off + 1) * 3 + row_off + 1
            if slot_index == 4:
                picked = inside
            else:
                picked = jnp.logical_and(inside, window_mask[:, :, slot_index] > 0)
            query_term, key_term, value_term = pair_terms(
                query_flat,
                grad_flat,
                sums_flat,
                deltas_flat,
                picked.astype(jnp.float32).reshape(num_tiles),
                slab[0],
                slab[1],
            )
            query_total = query_total + query_term
            pieces.append(
                round_keep(jnp.stack((key_term, value_term))).reshape(
                    2, time_tiles, row_tiles, tile_len, full_width
                )
            )
        interior, rim_before, rim_after = spread(pieces[0], pieces[1], pieces[2], 2)
        interiors.append(interior)
        befores.append(rim_before)
        afters.append(rim_after)
    rim_before = jnp.stack(befores, 1).astype(jnp.bfloat16)
    rim_after = jnp.stack(afters, 1).astype(jnp.bfloat16)
    from_before = from_behind(rim_after, "space", 1)
    from_after = from_behind(rim_before, "space", -1)
    own_rows = jnp.stack(interiors, 1)
    own_rows = own_rows.at[:, :, :, 0].add(from_before.astype(jnp.float32))
    own_rows = own_rows.at[:, :, :, row_tiles - 1].add(from_after.astype(jnp.float32))
    grouped = own_rows.astype(jnp.bfloat16)
    own_times, edge_before, edge_after = spread(
        grouped[:, 0].astype(jnp.float32),
        grouped[:, 1].astype(jnp.float32),
        grouped[:, 2].astype(jnp.float32),
        1,
    )
    from_past = from_behind(edge_after.astype(jnp.bfloat16), "tm", 1)
    from_future = from_behind(edge_before.astype(jnp.bfloat16), "tm", -1)
    own_times = own_times.at[:, 0].add(from_past.astype(jnp.float32))
    own_times = own_times.at[:, time_tiles - 1].add(from_future.astype(jnp.float32))
    key_grads = own_times[0].astype(jnp.bfloat16)
    value_grads = own_times[1].astype(jnp.bfloat16)
    query_grads = query_total.astype(jnp.bfloat16).reshape(
        time_tiles, row_tiles, tile_len, full_width
    )
    return (query_grads, key_grads, value_grads)


def solution(mesh):
    return jax.shard_map(
        per_device,
        mesh=mesh,
        in_specs=(
            P("tm", "space", None, None),
            P("tm", "space", None, None),
            P("tm", "space", None, None),
            P("tm", "space", None, None),
            P("tm", "space", None, None),
            P("tm", "space", None, None),
            P("tm", "space", None),
        ),
        out_specs=(
            P("tm", "space", None, None),
            P("tm", "space", None, None),
            P("tm", "space", None, None),
        ),
        check_vma=False,
    )
```

profile of v0, /device:TPU:9, one launch (start us, length us, event | category | flops | bytes accessed | tf_op | source)
XLA Modules:
  0.0 733.2 jit_solution(4486389191350155131)
XLA Ops:
  3.5 2.7 collective-permute-start.1
  6.2 3.0 collective-permute-start
  9.3 25.0 %collective-permute-done.1 = bf16[2,1,1,384,1536]{3,4,2,1,0:T(8,128)(2,1)S(1)} collective-permute-done((bf16[2,1,1,384,1536]{3,4,2,1,0:T(8,128)(2,1)S(1)}, bf16[2,1,1,384,1536]{3,4,2,1,0:T(8,128)(2,1)S(1)}, u32[]{:S(2)}, u32[]{:S(2)}) %collective-permute-start.1) | collective-permute-done | bytes 2359328 | tf_op jit(solution)/shard_map/ppermute | solution.py:15
  35.1 3.7 pad_maximum_fusion
  38.8 3.0 collective-permute-start.3
  55.3 3.3 fusion.74
  60.9 2.9 convert_multiply_fusion
  66.2 5.5 multiply_convert_fusion.8
  76.3 3.4 pad_maximum_fusion.5
  79.7 2.6 fusion.111
  84.7 240.2 %collective-permute-done.3 = bf16[2,3,1,384,1536]{3,4,2,1,0:T(8,128)(2,1)} collective-permute-done((bf16[2,3,1,384,1536]{3,4,2,1,0:T(8,128)(2,1)}, bf16[2,3,1,384,1536]{3,4,2,1,0:T(8,128)(2,1)}, u32[]{:S(2)}, u32[]{:S(2)}) %collective-permute-start.3) | collective-permute-done | bytes 7077920 | tf_op jit(solution)/shard_map/ppermute | solution.py:15
  324.9 5.5 fusion.98
  331.6 3.3 fusion.86
  337.4 5.3 multiply_convert_fusion
  347.4 3.3 pad_maximum_fusion.9
  351.9 3.3 fusion.77
  357.6 5.3 multiply_convert_fusion.3
  367.8 3.3 pad_maximum_fusion.8
  372.2 3.3 fusion.68
  378.0 5.1 multiply_convert_fusion.5
  390.5 3.4 pad_maximum_fusion.1
  395.9 5.2 fusion.99
  402.2 2.7 fusion.80
  405.0 4.0 multiply_convert_fusion.2
  408.9 2.7 copy.138
  411.7 4.2 multiply_convert_fusion.9
  418.3 3.2 pad_maximum_fusion.12
  422.7 2.7 fusion.71
  425.4 4.0 multiply_convert_fusion.4
  431.8 4.3 multiply_convert_fusion.10
  438.6 3.4 pad_maximum_fusion.11
  443.1 2.7 fusion.62
  458.1 3.4 pad_maximum_fusion.2
  461.5 4.3 collective-permute-start.5
  468.2 3.2 fusion.65
  471.5 2.6 copy.122
  474.1 5.3 multiply_convert_fusion.6
  484.1 3.4 pad_maximum_fusion.4
  489.9 3.4 fusion.83
  495.7 5.3 multiply_convert_fusion.1
  513.2 165.8 %collective-permute-done.4 = bf16[2,3,1,384,1536]{4,3,0,1,2:T(8,128)(2,1)} collective-permute-done((bf16[2,3,1,384,1536]{4,3,0,1,2:T(8,128)(2,1)}, bf16[2,3,1,384,1536]{4,3,0,1,2:T(8,128)(2,1)}, u32[]{:S(2)}, u32[]{:S(2)}) %collective-permute-start.4) | collective-permute-done | bytes 7077920 | tf_op jit(solution)/shard_map/ppermute | solution.py:23
  679.0 3.3 collective-permute-done.5
  682.3 6.7 fusion
  691.6 2.9 copy-done.2
  696.5 4.1 collective-permute-start.7
  712.3 10.3 %collective-permute-done.6 = bf16[2,1,384,1536]{3,2,0,1:T(8,128)(2,1)} collective-permute-done((bf16[2,1,384,1536]{3,2,0,1:T(8,128)(2,1)}, bf16[2,1,384,1536]{3,2,0,1:T(8,128)(2,1)}, u32[]{:S(2)}, u32[]{:S(2)}) %collective-permute-start.6) | collective-permute-done | bytes 2359328 | tf_op jit(solution)/shard_map/ppermute | solution.py:23
  722.5 4.7 collective-permute-done.7
  727.2 4.0 fusion.10
  (200 shorter events, 117.7 us)
Async XLA Ops:
  3.2 31.9 %copy-start.9 = (bf16[1,1,384,1536]{2,3,1,0:T(8,128)(2,1)}, bf16[1,1,384,1536]{2,3,1,0:T(8,128)(2,1)S(1)}, u32[]{:S(2)}) copy-start(bf16[1,1,384,1536]{2,3,1,0:T(8,128)(2,1)S(1)} %copy.78) | copy-start | bytes 3538948
  3.5 38.3 %copy-start.67 = (s32[1,1,9]{2,1,0:T(1,128)S(1)}, s32[1,1,9]{2,1,0:T(1,128)}, u32[]{:S(2)}) copy-start(s32[1,1,9]{2,1,0:T(1,128)} %param.21) | copy-start | bytes 112
  3.5 44.2 %copy-start.68 = (f32[1,1,12,384]{3,1,2,0:T(1,128)S(1)}, f32[1,1,12,384]{3,1,2,0:T(1,128)}, u32[]{:S(2)}) copy-start(f32[1,1,12,384]{3,1,2,0:T(1,128)} %param.20) | copy-start | bytes 55300
  3.5 30.8 %collective-permute-start.1 = (bf16[2,1,1,384,1536]{3,4,2,1,0:T(8,128)(2,1)S(1)}, bf16[2,1,1,384,1536]{3,4,2,1,0:T(8,128)(2,1)S(1)}, u32[]{:S(2)}, u32[]{:S(2)}) collective-permute-start(bf16[2,1,1,384,1536]{3,4,2,1,0:T(8,128)(2,1)S(1)} %pad_maximum_fusion.3), channel_id=1, source_target_pairs={{8,0},{16,8},{24,16},{9,1},{17,9},{25,17},{10,2},{18,10},{26,18},{... | collective-permute-start | bytes 7077896 | tf_op jit(solution)/shard_map/ppermute | solution.py:15
  6.2 28.8 %collective-permute-start = (bf16[2,1,1,384,1536]{3,4,2,1,0:T(8,128)(2,1)S(1)}, bf16[2,1,1,384,1536]{3,4,2,1,0:T(8,128)(2,1)S(1)}, u32[]{:S(2)}, u32[]{:S(2)}) collective-permute-start(bf16[2,1,1,384,1536]{3,4,2,1,0:T(8,128)(2,1)S(1)} %pad_maximum_fusion.3), channel_id=1, source_target_pairs={{0,8},{8,16},{16,24},{1,9},{9,17},{17,25},{2,10},{10,18},{18,26},{... | collective-permute-start | bytes 7077896 | tf_op jit(solution)/shard_map/ppermute | solution.py:14
  34.3 4.5 copy-start.41
  35.1 3.7 copy-start.43
  38.8 286.2 %collective-permute-start.3 = (bf16[2,3,1,384,1536]{3,4,2,1,0:T(8,128)(2,1)}, bf16[2,3,1,384,1536]{3,4,2,1,0:T(8,128)(2,1)}, u32[]{:S(2)}, u32[]{:S(2)}) collective-permute-start(bf16[2,3,1,384,1536]{3,4,2,1,0:T(8,128)(2,1)} %pad_maximum_fusion), channel_id=1, source_target_pairs={{1,0},{2,1},{3,2},{4,3},{5,4},{6,5},{7,6},{9,8},{10,9},{11,10},{12... | collective-permute-start | bytes 21233672 | tf_op jit(solution)/shard_map/ppermute | solution.py:15
  55.2 3.3 copy-start.3
  76.3 3.4 copy-start.1
  82.3 313.6 %collective-permute-start.2 = (bf16[2,3,1,384,1536]{3,4,2,1,0:T(8,128)(2,1)}, bf16[2,3,1,384,1536]{3,4,2,1,0:T(8,128)(2,1)}, u32[]{:S(2)}, u32[]{:S(2)}) collective-permute-start(bf16[2,3,1,384,1536]{3,4,2,1,0:T(8,128)(2,1)} %pad_maximum_fusion), channel_id=1, source_target_pairs={{0,1},{1,2},{2,3},{3,4},{4,5},{5,6},{6,7},{8,9},{9,10},{10,11},{11... | collective-permute-start | bytes 21233672 | tf_op jit(solution)/shard_map/ppermute | solution.py:14
  330.5 40.5 %copy-start.24 = (bf16[1,1,1,384,1536]{3,4,2,1,0:T(8,128)(2,1)}, bf16[1,1,1,384,1536]{3,4,2,1,0:T(8,128)(2,1)S(1)}, u32[]{:S(2)}) copy-start(bf16[1,1,1,384,1536]{3,4,2,1,0:T(8,128)(2,1)S(1)} %get-tuple-element.64) | copy-start | bytes 3538948
  331.6 3.3 copy-start.7
  347.4 3.3 copy-start.26
  351.9 3.3 copy-start.8
  372.2 3.3 copy-start.5
  375.5 2.5 copy-start.49
  385.3 2.5 copy-start.53
  387.8 2.7 copy-start.47
  394.0 285.1 %collective-permute-start.4 = (bf16[2,3,1,384,1536]{4,3,0,1,2:T(8,128)(2,1)}, bf16[2,3,1,384,1536]{4,3,0,1,2:T(8,128)(2,1)}, u32[]{:S(2)}, u32[]{:S(2)}) collective-permute-start(bf16[2,3,1,384,1536]{4,3,0,1,2:T(8,128)(2,1)} %pad_maximum_fusion.1), channel_id=1, source_target_pairs={{0,1},{1,2},{2,3},{3,4},{4,5},{5,6},{6,7},{8,9},{9,10},{10,11},{11... | collective-permute-start | bytes 21233672 | tf_op jit(solution)/shard_map/ppermute | solution.py:23
  402.2 2.8 copy-start.63
  422.7 2.7 copy-start.51
  422.7 2.7 copy-start.64
  438.6 3.4 copy-start.30
  443.1 2.7 copy-start.50
  443.1 2.7 copy-start.65
  455.0 2.4 copy-start.46
  455.0 3.1 copy-start.48
  458.1 7.7 %copy-start.44 = (bf16[2,1,1,384,1536]{3,4,2,1,0:T(8,128)(2,1)S(1)}, bf16[2,1,1,384,1536]{3,4,2,1,0:T(8,128)(2,1)}, u32[]{:S(2)}) copy-start(bf16[2,1,1,384,1536]{3,4,2,1,0:T(8,128)(2,1)} %copy-done.43) | copy-start | bytes 7077892
  461.5 220.8 %collective-permute-start.5 = (bf16[2,3,1,384,1536]{4,3,0,1,2:T(8,128)(2,1)}, bf16[2,3,1,384,1536]{4,3,0,1,2:T(8,128)(2,1)}, u32[]{:S(2)}, u32[]{:S(2)}) collective-permute-start(bf16[2,3,1,384,1536]{4,3,0,1,2:T(8,128)(2,1)} %pad_maximum_fusion.2), channel_id=1, source_target_pairs={{1,0},{2,1},{3,2},{4,3},{5,4},{6,5},{7,6},{9,8},{10,9},{11,10},{12... | collective-permute-start | bytes 21233672 | tf_op jit(solution)/shard_map/ppermute | solution.py:23
  468.2 3.2 copy-start.6
  484.1 3.4 copy-start.42
  489.9 3.4 copy-start.4
  505.3 2.3 copy-start.35
  507.6 2.3 copy-start.37
  509.9 2.3 copy-start.29
  512.3 170.0 %copy-start.39 = (bf16[2,1,384,1536]{3,2,0,1:T(8,128)(2,1)S(1)}, bf16[2,1,384,1536]{3,2,0,1:T(8,128)(2,1)}, u32[]{:S(2)}) copy-start(bf16[2,1,384,1536]{3,2,0,1:T(8,128)(2,1)} %pad_maximum_fusion.5) | copy-start | bytes 7077892
  512.3 170.0 %copy-start.40 = (bf16[2,1,384,1536]{3,2,0,1:T(8,128)(2,1)S(1)}, bf16[2,1,384,1536]{3,2,0,1:T(8,128)(2,1)}, u32[]{:S(2)}) copy-start(bf16[2,1,384,1536]{3,2,0,1:T(8,128)(2,1)} %pad_maximum_fusion.4) | copy-start | bytes 7077892
  689.0 5.5 copy-start.2
  689.1 11.5 %copy-start.11 = (bf16[12,384,384]{2,1,0:T(8,128)(2,1)S(1)}, bf16[12,384,384]{2,1,0:T(8,128)(2,1)}, u32[]{:S(2)}) copy-start(bf16[12,384,384]{2,1,0:T(8,128)(2,1)} %copy-done.10) | copy-start | bytes 10616836
  689.1 11.5 %copy-start.27 = (bf16[1,1,1,384,1536]{3,4,2,1,0:T(8,128)(2,1)S(1)}, bf16[1,1,1,384,1536]{3,4,2,1,0:T(8,128)(2,1)}, u32[]{:S(2)}) copy-start(bf16[1,1,1,384,1536]{3,4,2,1,0:T(8,128)(2,1)} %get-tuple-element.62) | copy-start | bytes 3538948
  694.5 28.0 %collective-permute-start.6 = (bf16[2,1,384,1536]{3,2,0,1:T(8,128)(2,1)}, bf16[2,1,384,1536]{3,2,0,1:T(8,128)(2,1)}, u32[]{:S(2)}, u32[]{:S(2)}) collective-permute-start(bf16[2,1,384,1536]{3,2,0,1:T(8,128)(2,1)} %get-tuple-element.57), channel_id=1, source_target_pairs={{0,8},{8,16},{16,24},{1,9},{9,17},{17,25},{2,10},{10,18},{18,26},{... | collective-permute-start | bytes 7077896 | tf_op jit(solution)/shard_map/ppermute | solution.py:23
  696.5 5.1 copy-start.13
  696.5 5.1 copy-start.25
  696.5 30.7 %collective-permute-start.7 = (bf16[2,1,384,1536]{3,2,0,1:T(8,128)(2,1)}, bf16[2,1,384,1536]{3,2,0,1:T(8,128)(2,1)}, u32[]{:S(2)}, u32[]{:S(2)}) collective-permute-start(bf16[2,1,384,1536]{3,2,0,1:T(8,128)(2,1)} %get-tuple-element.58), channel_id=1, source_target_pairs={{8,0},{16,8},{24,16},{9,1},{17,9},{25,17},{10,2},{18,10},{26,18},{... | collective-permute-start | bytes 7077896 | tf_op jit(solution)/shard_map/ppermute | solution.py:23
  701.6 2.3 copy-start.33
  703.9 2.3 copy-start.31
  706.2 2.7 copy-start.38
  (29 other events, 48.4 us)
where the time goes:
time: 741 us; the launch traced here: 733 us
  waiting for transfers between devices  450 us (61%)
  matrix products  115 us (16%)
  local copies, waits for them, and re-layouts  86.8 us (12%)
  other arithmetic  50.7 us (7%)
  starting transfers between devices  23.3 us (3%)
    ppermute x2, waiting for transfers between devices, with_halo(): after = lax.ppermute(initial, axis, down)  265 us
    ppermute x4, waiting for transfers between devices, from_behind(): lax.ppermute(value, axis, [(source, source + steps) for source in range(i...  184 us
    another operation x18, local copies, waits for them, and re-layouts, per_device(): jnp.stack((key_term, value_term))  43.7 us
    dot_general x9, matrix products, pair_terms(): jnp.einsum('nqhd,nkhd->nhqk', grad_heads, value_heads, preferred_element_...  42 us
    dot_general x9, matrix products, pair_terms(): jnp.einsum('nhqk,nqhd->nkhd', weights_low, grad_heads, preferred_element_...  28 us
    unnamed x145, local copies, waits for them, and re-layouts  25.1 us
    dot_general x9, matrix products, pair_terms(): jnp.einsum('nhqk,nqhd->nkhd', grad_score, query_heads, preferred_element_...  24.1 us
    another operation x9, other arithmetic, per_device(): jnp.stack((key_term, value_term))  23.8 us
  transfers between devices with their start and end apart: 8, of which 7 were waited for; matrix products, arithmetic and copies ran while one was open for 30% of the time, Pallas kernels for 0%

commit v1 on v0

v1 whole, which is shorter than its diff:
```python
import functools
import math

import jax
import jax.numpy as jnp
from jax import lax
from jax.experimental import pallas as pl
from jax.experimental.pallas import tpu as pltpu
from jax.sharding import PartitionSpec as P

F32 = jnp.float32
BF16 = jnp.bfloat16
LOG2E = math.log2(math.e)
FAR = 1e30
CHUNKS = (4, 4, 4)


def dot(a, b, dims):
    return lax.dot_general(a, b, (dims, ((), ())), preferred_element_type=F32)


def prep_kernel(chunks, q_ref, g_ref, o_ref, lse_ref, flag_ref, *outs):
    stat_ref = outs[-1]
    h = pl.program_id(0)
    heads = pl.num_programs(0)
    prod = g_ref[...].astype(F32) * o_ref[...].astype(F32)
    stat_ref[h, 1:2, :] = jnp.sum(prod.T, axis=0, keepdims=True)
    stat_ref[h, 0:1, :] = lse_ref[pl.ds(h, 1), :] * LOG2E

    @pl.when(h == 0)
    def _():
        stat_ref[heads, :, :] = flag_ref[...]

    first = 0
    for count, out in zip(chunks, outs):

        @pl.when((h >= first) & (h < first + count))
        def _(out=out):
            out[0] = q_ref[...]
            out[1] = g_ref[...]

        first += count


def prep(chunks, head_width, q, g, o, lse, flags):
    tile, full = q.shape
    heads = full // head_width
    cols = pl.BlockSpec((tile, head_width), lambda h: (0, h))

    def chunk_spec(first, count):
        return pl.BlockSpec(
            (2, tile, head_width), lambda h: (0, 0, jnp.clip(h - first, 0, count - 1))
        )

    specs, shapes, first = ([], [], 0)
    for count in chunks:
        specs.append(chunk_spec(first, count))
        shapes.append(jax.ShapeDtypeStruct((2, tile, count * head_width), BF16))
        first += count
    return pl.pallas_call(
        functools.partial(prep_kernel, chunks),
        grid=(heads,),
        in_specs=[
            cols,
            cols,
            cols,
            pl.BlockSpec((heads, tile), lambda h: (0, 0)),
            pl.BlockSpec((2, tile), lambda h: (0, 0)),
        ],
        out_specs=specs + [pl.BlockSpec((heads + 1, 2, tile), lambda h: (0, 0, 0))],
        out_shape=shapes + [jax.ShapeDtypeStruct((heads + 1, 2, tile), F32)],
        cost_estimate=pl.CostEstimate(
            flops=2 * tile * full, bytes_accessed=10 * tile * full, transcendentals=0
        ),
        name="prep",
    )(q, g, o, lse, flags)


def pair_kernel(
    first, heads, factor, far_ref,
    q_ref, g_ref, x_ref, z_ref, k_ref, v_ref, kn_ref, vn_ref, kf_ref, vf_ref,
    so_ref, sx_ref, sz_ref,
    dq_own, dq_partner, dq_outer, dkv_own, dkv_near, dkv_far, acc,
):
    h = pl.program_id(0) + first
    queries = (z_ref.at[0], q_ref, x_ref.at[0])
    grads = (z_ref.at[1], g_ref, x_ref.at[1])
    stats = (sz_ref, so_ref, sx_ref)

    def key_slot(slot, key, value):
        dk = None
        dv = None
        for j in range(3):
            qj = queries[j][...]
            gj = grads[j][...]
            lane = 3 * j + slot
            flag = stats[j][heads, 0:1, lane : lane + 1]
            shift = jnp.where(flag > 0, stats[j][h, 0:1, :], FAR)
            delta = stats[j][h, 1:2, :]
            scores = dot(key, qj, ((1,), (1,)))
            weights = jnp.exp2(scores * (factor * LOG2E) - shift)
            grad_prob = dot(value, gj, ((1,), (1,)))
            grad_score = (weights * (grad_prob - delta)).astype(BF16)
            term_v = dot(weights.astype(BF16), gj, ((1,), (0,)))
            term_k = dot(grad_score, qj, ((1,), (0,)))
            term_q = dot(grad_score, key, ((0,), (0,)))
            dv = term_v if dv is None else dv + term_v
            dk = term_k if dk is None else dk + term_k
            acc[j] = term_q if slot == 0 else acc[j] + term_q
        return (dk * factor, dv)

    dk, dv = key_slot(0, k_ref[...], v_ref[...])
    dkv_own[0] = dk
    dkv_own[1] = dv
    dk, dv = key_slot(1, kn_ref[...], vn_ref[...])
    dkv_near[0] = dk.astype(BF16)
    dkv_near[1] = dv.astype(BF16)

    @pl.when(far_ref[0] > 0)
    def _():
        dk, dv = key_slot(2, kf_ref[...], vf_ref[...])
        dkv_far[0] = dk.astype(BF16)
        dkv_far[1] = dv.astype(BF16)

    @pl.when(far_ref[0] == 0)
    def _():
        dkv_far[...] = jnp.zeros_like(dkv_far)

    dq_outer[...] = (acc[0] * factor).astype(BF16)
    dq_own[...] = acc[1] * factor
    dq_partner[...] = acc[2] * factor


def pair_call(first, count, head_width, far, q, g, x, z, kv, near, far_kv, so, sx, sz):
    tile, full = q.shape
    heads = full // head_width
    wide = count * head_width
    cols = pl.BlockSpec((tile, head_width), lambda h, *_: (0, h + first))
    part = pl.BlockSpec((2, tile, head_width), lambda h, *_: (0, 0, h))
    stat = pl.BlockSpec((heads + 1, 2, tile), lambda h, *_: (0, 0, 0))
    one = pl.BlockSpec((tile, head_width), lambda h, *_: (0, h))
    two = lambda kind: jax.ShapeDtypeStruct((2, tile, wide), kind)
    single = lambda kind: jax.ShapeDtypeStruct((tile, wide), kind)
    pairs = 9 * count
    return pl.pallas_call(
        functools.partial(pair_kernel, first, heads, head_width**-0.5),
        grid_spec=pltpu.PrefetchScalarGridSpec(
            num_scalar_prefetch=1,
            grid=(count,),
            in_specs=[cols, cols, part, part] + [cols] * 6 + [stat] * 3,
            out_specs=[one, one, one, part, part, part],
            scratch_shapes=[pltpu.VMEM((3, tile, head_width), F32)],
        ),
        out_shape=[single(F32), single(F32), single(BF16), two(F32), two(BF16), two(BF16)],
        compiler_params=pltpu.CompilerParams(vmem_limit_bytes=40 * 1024 * 1024),
        cost_estimate=pl.CostEstimate(
            flops=20 * pairs * tile * tile * head_width,
            bytes_accessed=40 * tile * wide,
            transcendentals=pairs * tile * tile,
        ),
        name="pairs",
    )(far, q, g, x, z, *kv, *near, *far_kv, so, sx, sz)


def finish_kernel(own_q, back_q, own_kv, near, far, *rest):
    out_q, out_k, out_v = rest[-3:]
    out_q[...] = (own_q[...] + back_q[...].astype(F32)).astype(BF16)
    sums = own_kv[...] + near[...].astype(F32) + far[...].astype(F32)
    out_k[...] = sums[0].astype(BF16)
    out_v[...] = sums[1].astype(BF16)


def finish(first, count, head_width, full, parts, so_far):
    tile = parts[0].shape[0]
    one = pl.BlockSpec((tile, head_width), lambda h: (0, h))
    two = pl.BlockSpec((2, tile, head_width), lambda h: (0, 0, h))
    cols = pl.BlockSpec((tile, head_width), lambda h: (0, h + first))
    kept = [] if so_far is None else list(so_far)
    return pl.pallas_call(
        finish_kernel,
        grid=(count,),
        in_specs=[one, one, two, two, two] + [pl.BlockSpec(memory_space=pl.ANY)] * len(kept),
        out_specs=[cols] * 3,
        out_shape=[jax.ShapeDtypeStruct((tile, full), BF16)] * 3,
        input_output_aliases={5 + i: i for i in range(len(kept))},
        cost_estimate=pl.CostEstimate(
            flops=8 * tile * count * head_width,
            bytes_accessed=30 * tile * count * head_width,
            transcendentals=0,
        ),
        name="finish",
    )(*parts, *kept)


def pair_flags(window_mask, tile):
    mask = window_mask.reshape(9)
    frames, rows = (lax.axis_size("tm"), lax.axis_size("space"))
    frame, row = (lax.axis_index("tm"), lax.axis_index("space"))
    toward = 1 - 2 * lax.rem(row, 2)
    near = 1 - 2 * lax.rem(frame, 2)
    lane = jnp.arange(9, dtype=jnp.int32)
    row_off = (lane // 3 - 1) * toward
    slot = lane % 3
    frame_off = jnp.where(slot == 1, near, jnp.where(slot == 2, -near, 0))
    inside = (
        (row + row_off >= 0)
        & (row + row_off < rows)
        & (frame + frame_off >= 0)
        & (frame + frame_off < frames)
    )
    index = 3 * (frame_off + 1) + row_off + 1
    picked = jnp.sum(
        jnp.where(index[:, None] == lane[None, :], mask[None, :], 0), axis=1
    )
    flags = (inside & ((picked > 0) | (index == 4))).astype(F32)
    return jnp.zeros((2, tile), F32).at[0, :9].set(flags)


def per_device(queries, keys, values, outputs, out_grads, log_sums, window_mask):
    tile, full = queries.shape[2:]
    heads = log_sums.shape[2]
    head_width = full // heads
    frames, rows = (lax.axis_size("tm"), lax.axis_size("space"))
    q, k, v, o, g = (
        a.reshape(tile, full) for a in (queries, keys, values, outputs, out_grads)
    )
    partner = [(i, i ^ 1) for i in range(rows)]
    onward = [(i, i + 2) for i in range(0, rows - 2, 2)]
    onward += [(i, i - 2) for i in range(3, rows, 2)]
    homeward = [(b, a) for a, b in onward]
    near_pairs = [(i, i ^ 1) for i in range(frames)]
    far_pairs = [(i, i + 1) for i in range(1, frames - 1, 2)]
    far_pairs += [(b, a) for a, b in far_pairs]

    frame = lax.axis_index("tm")
    far_frame = frame - 1 + 2 * lax.rem(frame, 2)
    has_far = ((far_frame >= 0) & (far_frame < frames)).astype(jnp.int32).reshape(1)

    flags = pair_flags(window_mask, tile)
    *packed, stats = prep(
        CHUNKS, head_width, q, g, o, log_sums.reshape(heads, tile), flags
    )
    near_kv = [lax.ppermute(a, "tm", near_pairs) for a in (k, v)]
    far_kv = [lax.ppermute(a, "tm", far_pairs) for a in (k, v)]
    stats_x = lax.ppermute(stats, "space", partner)
    stats_z = lax.ppermute(stats_x, "space", onward)
    from_partner = [lax.ppermute(a, "space", partner) for a in packed]
    from_outer = [lax.ppermute(a, "space", onward) for a in from_partner]

    out = None
    first = 0
    for count, x, z in zip(CHUNKS, from_partner, from_outer):
        dq_own, dq_partner, dq_outer, dkv_own, dkv_near, dkv_far = pair_call(
            first, count, head_width, has_far, q, g, x, z,
            (k, v), near_kv, far_kv, stats, stats_x, stats_z,
        )
        home = lax.ppermute(dq_outer, "space", homeward)
        dq_back = lax.ppermute(
            (dq_partner + home.astype(F32)).astype(BF16), "space", partner
        )
        near_back = lax.ppermute(dkv_near, "tm", near_pairs)
        far_back = lax.ppermute(dkv_far, "tm", far_pairs)
        out = finish(
            first, count, head_width, full,
            (dq_own, dq_back, dkv_own, near_back, far_back), out,
        )
        first += count
    return tuple(a.reshape(queries.shape) for a in out)


def solution(mesh):
    tile = P("tm", "space", None, None)
    return jax.shard_map(
        per_device,
        mesh=mesh,
        in_specs=(tile,) * 6 + (P("tm", "space", None),),
        out_specs=(tile,) * 3,
        check_vma=False,
    )
```

time: 741 us -> 221 us (0.30)
  waiting for transfers between devices: 450 us -> 76.8 us
  matrix products: 115 us -> 0 us
  Pallas kernels: 0 us -> 82.8 us
  local copies, waits for them, and re-layouts: 86.8 us -> 10.3 us
  other arithmetic: 50.7 us -> 2.62 us
  starting transfers between devices: 23.3 us -> 45.1 us
    ppermute x8 -> x24, waiting for transfers between devices: 450 us -> 76.8 us  [the longest x1 50.4 us: per_device(): stats_x = lax.ppermute(stats, 'space', partner)]
    dot_general x45 -> x0, matrix products: 115 us -> none  [the longest x9 42 us: pair_terms(): jnp.einsum('nqhd,nkhd->nhqk', grad_heads, value_heads, preferred_element_...]
    pallas_call x0 -> x7, Pallas kernels: none -> 82.8 us  [the longest x3 61.3 us: pair_call(): pl.pallas_call(functools.partial(pair_kernel, first, heads, head_width **...]
    another operation x18 -> x0, local copies, waits for them, and re-layouts: 43.7 us -> none  [per_device(): jnp.stack((key_term, value_term))]
    another operation x13 -> x0, other arithmetic: 35 us -> none  [the longest x9 23.8 us: per_device(): jnp.stack((key_term, value_term))]
    ppermute x8 -> x24, starting transfers between devices: 23.3 us -> 45.1 us  [the longest x3 8.61 us: per_device(): far_back = lax.ppermute(dkv_far, 'tm', far_pairs)]
    unnamed x145 -> x49, local copies, waits for them, and re-layouts: 25.1 us -> 10.3 us
    slice x5 -> x0, local copies, waits for them, and re-layouts: 13.9 us -> none  [the longest x4 13.2 us: per_device(): slab[1]]
  transfers between devices with their start and end apart: 8 -> 24, of which waited for: 7 -> 5; matrix products, arithmetic and copies ran while one was open for 30% -> 1% of each run, Pallas kernels for 0% -> 32%
where the time goes in v1:
time: 221 us; the launch traced here: 219 us
  Pallas kernels  82.8 us (37%)
  waiting for transfers between devices  76.8 us (35%)
  starting transfers between devices  45.1 us (20%)
  local copies, waits for them, and re-layouts  10.3 us (5%)
  other arithmetic  2.62 us (1%)
    pallas_call x3, Pallas kernels, pair_call(): pl.pallas_call(functools.partial(pair_kernel, first, heads, head_width **...  61.3 us
    ppermute x1, waiting for transfers between devices, per_device(): stats_x = lax.ppermute(stats, 'space', partner)  50.4 us
    ppermute x2, waiting for transfers between devices, per_device(): far_kv = [lax.ppermute(a, 'tm', far_pairs) for a in (k, v)]  16.5 us
    pallas_call x3, Pallas kernels, finish(): pl.pallas_call(finish_kernel, grid=(count,), in_specs=[one, one, two, two...  12.3 us
    unnamed x49, local copies, waits for them, and re-layouts  10.3 us
    pallas_call x1, Pallas kernels, prep(): pl.pallas_call(functools.partial(prep_kernel, chunks), grid=(heads,), in_...  9.16 us
    ppermute x3, starting transfers between devices, per_device(): far_back = lax.ppermute(dkv_far, 'tm', far_pairs)  8.61 us
    ppermute x3, starting transfers between devices, per_device(): from_outer = [lax.ppermute(a, 'space', onward) for a in from_partner]  8.34 us
  transfers between devices with their start and end apart: 24, of which 5 were waited for; matrix products, arithmetic and copies ran while one was open for 1% of the time, Pallas kernels for 32%

profile of v1, /device:TPU:9, one launch (start us, length us, event | category | flops | bytes accessed | tf_op | source)
XLA Modules:
  0.0 218.5 jit_solution(900897895677029755)
XLA Ops:
  0.7 0.8 select_reduce_fusion
  1.5 0.6 pad_convert_fusion.flag_ref
  2.1 1.3 copy.18
  3.5 9.2 %prep.1 = (bf16[2,384,512]{2,1,0:T(8,128)(2,1)}, bf16[2,384,512]{2,1,0:T(8,128)(2,1)}, bf16[2,384,512]{2,1,0:T(8,128)(2,1)}, f32[13,2,384]{2,1,0:T(2,128)}) custom-call(bf16[384,1536]{1,0:T(8,128)(2,1)} %bitcast.17, bf16[384,1536]{1,0:T(8,128)(2,1)} %bitcast.21, bf16[384,1536]{1,0:T(8,128)(2,1)} %bitcast.38, f32[12,384]{1,0:T(8,128)} %bitcast.39, ...), custom_call_target="tpu_custom_call" | custom-call | flops 1179648 | bytes 5898240 | tf_op jit(solution)/shard_map/prep/pallas_call | solution.py:60
  12.6 1.3 collective-permute-start.18
  13.9 0.3 collective-permute-start.12
  14.2 1.2 collective-permute-start
  15.4 0.3 collective-permute-start.6
  15.6 50.4 %collective-permute-done.6.sx_ref = f32[13,2,384]{2,1,0:T(2,128)S(1)} collective-permute-done((f32[13,2,384]{2,1,0:T(2,128)}, f32[13,2,384]{2,1,0:T(2,128)S(1)}, u32[]{:S(2)}, u32[]{:S(2)}) %collective-permute-start.6) | collective-permute-done | bytes 39968 | tf_op jit(solution)/shard_map/ppermute | solution.py:245
  66.0 3.2 %collective-permute-start.7 = (f32[13,2,384]{2,1,0:T(2,128)S(1)}, f32[13,2,384]{2,1,0:T(2,128)S(1)}, u32[]{:S(2)}, u32[]{:S(2)}) collective-permute-start(f32[13,2,384]{2,1,0:T(2,128)S(1)} %collective-permute-done.6.sx_ref), channel_id=1, source_target_pairs={{0,2},{2,4},{4,6},{3,1},{5,3},{7,5},{8,10},{10,12},{12,14},{11,9},... | collective-permute-start | bytes 119816 | tf_op jit(solution)/shard_map/ppermute | solution.py:246
  69.2 0.6 copy-done.10
  69.8 1.7 collective-permute-start.2
  71.5 0.6 copy-done.13
  72.1 1.8 collective-permute-start.3
  73.9 3.0 %collective-permute-start.4 = (bf16[384,1536]{1,0:T(8,128)(2,1)S(1)}, bf16[384,1536]{1,0:T(8,128)(2,1)}, u32[]{:S(2)}, u32[]{:S(2)}) collective-permute-start(bf16[384,1536]{1,0:T(8,128)(2,1)S(1)} %bitcast.26), channel_id=1, source_target_pairs={{8,16},{16,8},{9,17},{17,9},{10,18},{18,10},{11,19},{19,11},{12,20... | collective-permute-start | bytes 3538952 | tf_op jit(solution)/shard_map/ppermute | solution.py:244
  77.0 2.5 %collective-permute-start.5 = (bf16[384,1536]{1,0:T(8,128)(2,1)}, bf16[384,1536]{1,0:T(8,128)(2,1)}, u32[]{:S(2)}, u32[]{:S(2)}) collective-permute-start(bf16[384,1536]{1,0:T(8,128)(2,1)} %bitcast.31), channel_id=1, source_target_pairs={{8,16},{16,8},{9,17},{17,9},{10,18},{18,10},{11,19},{19,11},{12,20... | collective-permute-start | bytes 3538952 | tf_op jit(solution)/shard_map/ppermute | solution.py:244
  79.5 3.2 %collective-permute-start.19 = (bf16[2,384,512]{2,1,0:T(8,128)(2,1)}, bf16[2,384,512]{2,1,0:T(8,128)(2,1)}, u32[]{:S(2)}, u32[]{:S(2)}) collective-permute-start(bf16[2,384,512]{2,1,0:T(8,128)(2,1)} %collective-permute-done.18.x_ref), channel_id=1, source_target_pairs={{0,2},{2,4},{4,6},{3,1},{5,3},{7,5},{8,10},{10,12},{12,14},{11,9},... | collective-permute-start | bytes 2359304 | tf_op jit(solution)/shard_map/ppermute | solution.py:248
  82.8 3.2 %collective-permute-start.13 = (bf16[2,384,512]{2,1,0:T(8,128)(2,1)}, bf16[2,384,512]{2,1,0:T(8,128)(2,1)S(1)}, u32[]{:S(2)}, u32[]{:S(2)}) collective-permute-start(bf16[2,384,512]{2,1,0:T(8,128)(2,1)} %collective-permute-done.12.x_ref), channel_id=1, source_target_pairs={{0,2},{2,4},{4,6},{3,1},{5,3},{7,5},{8,10},{10,12},{12,14},{11,9},... | collective-permute-start | bytes 2359304 | tf_op jit(solution)/shard_map/ppermute | solution.py:248
  86.0 1.9 collective-permute-start.1
  87.9 3.9 %collective-permute-done.4.kf_ref = bf16[384,1536]{1,0:T(8,128)(2,1)} collective-permute-done((bf16[384,1536]{1,0:T(8,128)(2,1)S(1)}, bf16[384,1536]{1,0:T(8,128)(2,1)}, u32[]{:S(2)}, u32[]{:S(2)}) %collective-permute-start.4) | collective-permute-done | bytes 1179680 | tf_op jit(solution)/shard_map/ppermute | solution.py:244
  91.8 12.5 %collective-permute-done.5.vf_ref = bf16[384,1536]{1,0:T(8,128)(2,1)} collective-permute-done((bf16[384,1536]{1,0:T(8,128)(2,1)}, bf16[384,1536]{1,0:T(8,128)(2,1)}, u32[]{:S(2)}, u32[]{:S(2)}) %collective-permute-start.5) | collective-permute-done | bytes 1179680 | tf_op jit(solution)/shard_map/ppermute | solution.py:244
  104.4 1.3 copy-done.6
  105.7 0.8 copy-done.8
  106.4 0.8 copy-done.11
  107.2 0.8 copy-done.14
  108.0 20.5 %pairs.5 = (f32[384,512]{1,0:T(8,128)S(1)}, f32[384,512]{1,0:T(8,128)S(1)}, bf16[384,512]{1,0:T(8,128)(2,1)S(1)}, f32[2,384,512]{2,1,0:T(8,128)}, bf16[2,384,512...) custom-call(s32[1]{0:T(128)} %bitcast.far_ref, bf16[384,1536]{1,0:T(8,128)(2,1)S(1)} %bitcast.18, ...), custom_call_target="tpu_custom_call" | custom-call | flops 13589544960 | bytes 7864320 | tf_op jit(solution)/shard_map/pairs/pallas_call | solution.py:145
  128.5 0.9 copy-done.2
  129.4 1.9 collective-permute-start.20
  131.4 2.8 %collective-permute-start.23 = (bf16[2,384,512]{2,1,0:T(8,128)(2,1)S(1)}, bf16[2,384,512]{2,1,0:T(8,128)(2,1)S(1)}, u32[]{:S(2)}, u32[]{:S(2)}) collective-permute-start(bf16[2,384,512]{2,1,0:T(8,128)(2,1)S(1)} %get-tuple-element.67), channel_id=1, source_target_pairs={{8,16},{16,8},{9,17},{17,9},{10,18},{18,10},{11,19},{19,11},{12,20... | collective-permute-start | bytes 2359304 | tf_op jit(solution)/shard_map/ppermute | solution.py:262
  134.3 20.4 %pairs.4 = (f32[384,512]{1,0:T(8,128)S(1)}, f32[384,512]{1,0:T(8,128)S(1)}, bf16[384,512]{1,0:T(8,128)(2,1)S(1)}, f32[2,384,512]{2,1,0:T(8,128)}, bf16[2,384,512...) custom-call(s32[1]{0:T(128)} %bitcast.far_ref, bf16[384,1536]{1,0:T(8,128)(2,1)S(1)} %bitcast.19, ...), custom_call_target="tpu_custom_call" | custom-call | flops 13589544960 | bytes 7864320 | tf_op jit(solution)/shard_map/pairs/pallas_call | solution.py:145
  154.7 0.9 copy-done.4
  155.6 2.1 collective-permute-start.14
  157.7 20.5 %pairs.3 = (f32[384,512]{1,0:T(8,128)S(1)}, f32[384,512]{1,0:T(8,128)S(1)}, bf16[384,512]{1,0:T(8,128)(2,1)S(1)}, f32[2,384,512]{2,1,0:T(8,128)}, bf16[2,384,512...) custom-call(s32[1]{0:T(128)} %bitcast.far_ref, bf16[384,1536]{1,0:T(8,128)(2,1)S(1)} %bitcast.20, ...), custom_call_target="tpu_custom_call" | custom-call | flops 13589544960 | bytes 7864320 | tf_op jit(solution)/shard_map/pairs/pallas_call | solution.py:145
  178.2 1.9 collective-permute-start.8
  180.2 2.9 %collective-permute-start.21 = (bf16[384,512]{1,0:T(8,128)(2,1)S(1)}, bf16[384,512]{1,0:T(8,128)(2,1)S(1)}, u32[]{:S(2)}, u32[]{:S(2)}) collective-permute-start(bf16[384,512]{1,0:T(8,128)(2,1)S(1)} %add_convert_fusion), channel_id=1, source_target_pairs={{0,1},{1,0},{2,3},{3,2},{4,5},{5,4},{6,7},{7,6},{8,9},{9,8},{10,11... | collective-permute-start | bytes 1179656 | tf_op jit(solution)/shard_map/ppermute | solution.py:258
  183.1 3.9 %collective-permute-done.8 = bf16[384,512]{1,0:T(8,128)(2,1)S(1)} collective-permute-done((bf16[384,512]{1,0:T(8,128)(2,1)S(1)}, bf16[384,512]{1,0:T(8,128)(2,1)S(1)}, u32[]{:S(2)}, u32[]{:S(2)}) %collective-permute-start.8) | collective-permute-done | bytes 393248 | tf_op jit(solution)/shard_map/ppermute | solution.py:257
  187.0 3.6 %collective-permute-start.17 = (bf16[2,384,512]{2,1,0:T(8,128)(2,1)}, bf16[2,384,512]{2,1,0:T(8,128)(2,1)S(1)}, u32[]{:S(2)}, u32[]{:S(2)}) collective-permute-start(bf16[2,384,512]{2,1,0:T(8,128)(2,1)} %get-tuple-element.60), channel_id=1, source_target_pairs={{8,16},{16,8},{9,17},{17,9},{10,18},{18,10},{11,19},{19,11},{12,20... | collective-permute-start | bytes 2359304 | tf_op jit(solution)/shard_map/ppermute | solution.py:262
  190.8 2.8 %collective-permute-start.15 = (bf16[384,512]{1,0:T(8,128)(2,1)S(1)}, bf16[384,512]{1,0:T(8,128)(2,1)S(1)}, u32[]{:S(2)}, u32[]{:S(2)}) collective-permute-start(bf16[384,512]{1,0:T(8,128)(2,1)S(1)} %add_convert_fusion.1), channel_id=1, source_target_pairs={{0,1},{1,0},{2,3},{3,2},{4,5},{5,4},{6,7},{7,6},{8,9},{9,8},{10,11... | collective-permute-start | bytes 1179656 | tf_op jit(solution)/shard_map/ppermute | solution.py:258
  193.7 2.2 %collective-permute-start.11 = (bf16[2,384,512]{2,1,0:T(8,128)(2,1)}, bf16[2,384,512]{2,1,0:T(8,128)(2,1)S(1)}, u32[]{:S(2)}, u32[]{:S(2)}) collective-permute-start(bf16[2,384,512]{2,1,0:T(8,128)(2,1)} %get-tuple-element.53), channel_id=1, source_target_pairs={{8,16},{16,8},{9,17},{17,9},{10,18},{18,10},{11,19},{19,11},{12,20... | collective-permute-start | bytes 2359304 | tf_op jit(solution)/shard_map/ppermute | solution.py:262
  195.9 0.9 add_convert_fusion.2
  196.8 6.0 %collective-permute-done.15.back_q = bf16[384,512]{1,0:T(8,128)(2,1)S(1)} collective-permute-done((bf16[384,512]{1,0:T(8,128)(2,1)S(1)}, bf16[384,512]{1,0:T(8,128)(2,1)S(1)}, u32[]{:S(2)}, u32[]{:S(2)}) %collective-permute-start.15) | collective-permute-done | bytes 393248 | tf_op jit(solution)/shard_map/ppermute | solution.py:258
  202.8 1.1 collective-permute-start.9
  203.9 4.1 %finish.3 = (bf16[384,1536]{1,0:T(8,128)(2,1)}, bf16[384,1536]{1,0:T(8,128)(2,1)}, bf16[384,1536]{1,0:T(8,128)(2,1)}) custom-call(f32[384,512]{1,0:T(8,128)} %copy-done.2, bf16[384,512]{1,0:T(8,128)(2,1)} %copy-done.22, f32[2,384,512]{2,1,0:T(8,128)} %get-tuple-element.65.own_kv, bf16[2,384,512]{2,1,0:T(8,128)(2,1)} %copy-done.16, ...), custom_call_target="tpu_custom_call" | custom-call | flops 1572864 | bytes 5898240 | tf_op jit(solution)/shard_map/finish/pallas_call | solution.py:179
  208.1 0.9 copy-done.19
  208.9 0.3 copy-done.20
  209.2 4.1 %finish.4 = (bf16[384,1536]{1,0:T(8,128)(2,1)}, bf16[384,1536]{1,0:T(8,128)(2,1)}, bf16[384,1536]{1,0:T(8,128)(2,1)}) custom-call(f32[384,512]{1,0:T(8,128)} %copy-done.4, bf16[384,512]{1,0:T(8,128)(2,1)} %copy-done.23, f32[2,384,512]{2,1,0:T(8,128)} %get-tuple-element.58.own_kv, ...), custom_call_target="tpu_custom_call", output_to_operand_aliasing={{0}: (5, {}), {1}: (6, {}), {2}: (7, {})} | custom-call | flops 1572864 | bytes 5898240 | tf_op jit(solution)/shard_map/finish/pallas_call | solution.py:179
  213.3 0.9 copy-done.18
  214.4 4.1 %finish.5 = (bf16[384,1536]{1,0:T(8,128)(2,1)}, bf16[384,1536]{1,0:T(8,128)(2,1)}, bf16[384,1536]{1,0:T(8,128)(2,1)}) custom-call(f32[384,512]{1,0:T(8,128)} %copy-done.3, bf16[384,512]{1,0:T(8,128)(2,1)} %collective-permute-done.9.back_q, f32[2,384,512]{2,1,0:T(8,128)} %get-tuple-element.51.own_kv, ...), custom_call_target="tpu_custom_call", output_to_operand_aliasing={{0}: (5, {}), {1}: (6, {}), {2}: (7, {})} | custom-call | flops 1572864 | bytes 5898240 | tf_op jit(solution)/shard_map/finish/pallas_call | solution.py:179
  (63 shorter events, 0.8 us)
Async XLA Ops:
  3.5 66.3 %copy-start.5 = (bf16[1,1,384,1536]{3,2,1,0:T(8,128)(2,1)S(1)}, bf16[1,1,384,1536]{3,2,1,0:T(8,128)(2,1)}, u32[]{:S(2)}) copy-start(bf16[1,1,384,1536]{3,2,1,0:T(8,128)(2,1)} %param.10) | copy-start | bytes 3538948
  3.5 100.9 %copy-start = (bf16[1,1,384,1536]{3,2,1,0:T(8,128)(2,1)S(1)}, bf16[1,1,384,1536]{3,2,1,0:T(8,128)(2,1)}, u32[]{:S(2)}) copy-start(bf16[1,1,384,1536]{3,2,1,0:T(8,128)(2,1)} %param.9) | copy-start | bytes 3538948
  3.5 100.9 %copy-start.1 = (bf16[1,1,384,1536]{3,2,1,0:T(8,128)(2,1)S(1)}, bf16[1,1,384,1536]{3,2,1,0:T(8,128)(2,1)}, u32[]{:S(2)}) copy-start(bf16[1,1,384,1536]{3,2,1,0:T(8,128)(2,1)} %param.13) | copy-start | bytes 3538948
  12.6 61.3 %collective-permute-start.18 = (bf16[2,384,512]{2,1,0:T(8,128)(2,1)}, bf16[2,384,512]{2,1,0:T(8,128)(2,1)}, u32[]{:S(2)}, u32[]{:S(2)}) collective-permute-start(bf16[2,384,512]{2,1,0:T(8,128)(2,1)} %get-tuple-element.61), channel_id=1, source_target_pairs={{0,1},{1,0},{2,3},{3,2},{4,5},{5,4},{6,7},{7,6},{8,9},{9,8},{10,11... | collective-permute-start | bytes 2359304 | tf_op jit(solution)/shard_map/ppermute | solution.py:247
  13.9 63.1 %collective-permute-start.12 = (bf16[2,384,512]{2,1,0:T(8,128)(2,1)}, bf16[2,384,512]{2,1,0:T(8,128)(2,1)}, u32[]{:S(2)}, u32[]{:S(2)}) collective-permute-start(bf16[2,384,512]{2,1,0:T(8,128)(2,1)} %get-tuple-element.54), channel_id=1, source_target_pairs={{0,1},{1,0},{2,3},{3,2},{4,5},{5,4},{6,7},{7,6},{8,9},{9,8},{10,11... | collective-permute-start | bytes 2359304 | tf_op jit(solution)/shard_map/ppermute | solution.py:247
  14.2 65.3 %collective-permute-start = (bf16[2,384,512]{2,1,0:T(8,128)(2,1)}, bf16[2,384,512]{2,1,0:T(8,128)(2,1)}, u32[]{:S(2)}, u32[]{:S(2)}) collective-permute-start(bf16[2,384,512]{2,1,0:T(8,128)(2,1)} %get-tuple-element.46), channel_id=1, source_target_pairs={{0,1},{1,0},{2,3},{3,2},{4,5},{5,4},{6,7},{7,6},{8,9},{9,8},{10,11... | collective-permute-start | bytes 2359304 | tf_op jit(solution)/shard_map/ppermute | solution.py:247
  15.4 50.6 %collective-permute-start.6 = (f32[13,2,384]{2,1,0:T(2,128)}, f32[13,2,384]{2,1,0:T(2,128)S(1)}, u32[]{:S(2)}, u32[]{:S(2)}) collective-permute-start(f32[13,2,384]{2,1,0:T(2,128)} %get-tuple-element.47.so_ref), channel_id=1, source_target_pairs={{0,1},{1,0},{2,3},{3,2},{4,5},{5,4},{6,7},{7,6},{8,9},{9,8},{10,11... | collective-permute-start | bytes 119816 | tf_op jit(solution)/shard_map/ppermute | solution.py:245
  66.0 5.5 %collective-permute-start.7 = (f32[13,2,384]{2,1,0:T(2,128)S(1)}, f32[13,2,384]{2,1,0:T(2,128)S(1)}, u32[]{:S(2)}, u32[]{:S(2)}) collective-permute-start(f32[13,2,384]{2,1,0:T(2,128)S(1)} %collective-permute-done.6.sx_ref), channel_id=1, source_target_pairs={{0,2},{2,4},{4,6},{3,1},{5,3},{7,5},{8,10},{10,12},{12,14},{11,9},... | collective-permute-start | bytes 119816 | tf_op jit(solution)/shard_map/ppermute | solution.py:246
  69.2 0.6 copy-start.10
  69.8 13.0 %collective-permute-start.2 = (bf16[384,1536]{1,0:T(8,128)(2,1)S(1)}, bf16[384,1536]{1,0:T(8,128)(2,1)}, u32[]{:S(2)}, u32[]{:S(2)}) collective-permute-start(bf16[384,1536]{1,0:T(8,128)(2,1)S(1)} %bitcast.25), channel_id=1, source_target_pairs={{0,8},{8,0},{16,24},{24,16},{1,9},{9,1},{17,25},{25,17},{2,10},{10... | collective-permute-start | bytes 3538952 | tf_op jit(solution)/shard_map/ppermute | solution.py:243
  71.5 0.6 copy-start.13
  72.1 13.8 %collective-permute-start.3 = (bf16[384,1536]{1,0:T(8,128)(2,1)}, bf16[384,1536]{1,0:T(8,128)(2,1)}, u32[]{:S(2)}, u32[]{:S(2)}) collective-permute-start(bf16[384,1536]{1,0:T(8,128)(2,1)} %bitcast.30), channel_id=1, source_target_pairs={{0,8},{8,0},{16,24},{24,16},{1,9},{9,1},{17,25},{25,17},{2,10},{10... | collective-permute-start | bytes 3538952 | tf_op jit(solution)/shard_map/ppermute | solution.py:243
  73.9 17.9 %collective-permute-start.4 = (bf16[384,1536]{1,0:T(8,128)(2,1)S(1)}, bf16[384,1536]{1,0:T(8,128)(2,1)}, u32[]{:S(2)}, u32[]{:S(2)}) collective-permute-start(bf16[384,1536]{1,0:T(8,128)(2,1)S(1)} %bitcast.26), channel_id=1, source_target_pairs={{8,16},{16,8},{9,17},{17,9},{10,18},{18,10},{11,19},{19,11},{12,20... | collective-permute-start | bytes 3538952 | tf_op jit(solution)/shard_map/ppermute | solution.py:244
  77.0 27.4 %collective-permute-start.5 = (bf16[384,1536]{1,0:T(8,128)(2,1)}, bf16[384,1536]{1,0:T(8,128)(2,1)}, u32[]{:S(2)}, u32[]{:S(2)}) collective-permute-start(bf16[384,1536]{1,0:T(8,128)(2,1)} %bitcast.31), channel_id=1, source_target_pairs={{8,16},{16,8},{9,17},{17,9},{10,18},{18,10},{11,19},{19,11},{12,20... | collective-permute-start | bytes 3538952 | tf_op jit(solution)/shard_map/ppermute | solution.py:244
  79.5 24.9 %collective-permute-start.19 = (bf16[2,384,512]{2,1,0:T(8,128)(2,1)}, bf16[2,384,512]{2,1,0:T(8,128)(2,1)}, u32[]{:S(2)}, u32[]{:S(2)}) collective-permute-start(bf16[2,384,512]{2,1,0:T(8,128)(2,1)} %collective-permute-done.18.x_ref), channel_id=1, source_target_pairs={{0,2},{2,4},{4,6},{3,1},{5,3},{7,5},{8,10},{10,12},{12,14},{11,9},... | collective-permute-start | bytes 2359304 | tf_op jit(solution)/shard_map/ppermute | solution.py:248
  82.8 51.5 %collective-permute-start.13 = (bf16[2,384,512]{2,1,0:T(8,128)(2,1)}, bf16[2,384,512]{2,1,0:T(8,128)(2,1)S(1)}, u32[]{:S(2)}, u32[]{:S(2)}) collective-permute-start(bf16[2,384,512]{2,1,0:T(8,128)(2,1)} %collective-permute-done.12.x_ref), channel_id=1, source_target_pairs={{0,2},{2,4},{4,6},{3,1},{5,3},{7,5},{8,10},{10,12},{12,14},{11,9},... | collective-permute-start | bytes 2359304 | tf_op jit(solution)/shard_map/ppermute | solution.py:248
  86.0 71.7 %collective-permute-start.1 = (bf16[2,384,512]{2,1,0:T(8,128)(2,1)}, bf16[2,384,512]{2,1,0:T(8,128)(2,1)S(1)}, u32[]{:S(2)}, u32[]{:S(2)}) collective-permute-start(bf16[2,384,512]{2,1,0:T(8,128)(2,1)} %collective-permute-done.x_ref), channel_id=1, source_target_pairs={{0,2},{2,4},{4,6},{3,1},{5,3},{7,5},{8,10},{10,12},{12,14},{11,9},... | collective-permute-start | bytes 2359304 | tf_op jit(solution)/shard_map/ppermute | solution.py:248
  104.4 1.3 copy-start.6
  105.7 0.8 copy-start.8
  106.4 0.8 copy-start.11
  107.2 0.8 copy-start.14
  108.0 26.3 %copy-start.7 = (bf16[1,1,384,1536]{3,2,1,0:T(8,128)(2,1)S(1)}, bf16[1,1,384,1536]{3,2,1,0:T(8,128)(2,1)}, u32[]{:S(2)}) copy-start(bf16[1,1,384,1536]{3,2,1,0:T(8,128)(2,1)} %param.11) | copy-start | bytes 3538948
  108.0 26.3 %copy-start.9 = (f32[13,2,384]{2,1,0:T(2,128)S(1)}, f32[13,2,384]{2,1,0:T(2,128)}, u32[]{:S(2)}) copy-start(f32[13,2,384]{2,1,0:T(2,128)} %get-tuple-element.47.so_ref) | copy-start | bytes 119812
  108.0 26.3 %copy-start.12 = (f32[13,2,384]{2,1,0:T(2,128)S(1)}, f32[13,2,384]{2,1,0:T(2,128)}, u32[]{:S(2)}) copy-start(f32[13,2,384]{2,1,0:T(2,128)} %copy-done.10) | copy-start | bytes 119812
  108.0 26.3 %copy-start.15 = (f32[13,2,384]{2,1,0:T(2,128)S(1)}, f32[13,2,384]{2,1,0:T(2,128)}, u32[]{:S(2)}) copy-start(f32[13,2,384]{2,1,0:T(2,128)} %copy-done.13) | copy-start | bytes 119812
  128.5 0.9 copy-start.2
  129.4 50.7 %collective-permute-start.20 = (bf16[384,512]{1,0:T(8,128)(2,1)S(1)}, bf16[384,512]{1,0:T(8,128)(2,1)S(1)}, u32[]{:S(2)}, u32[]{:S(2)}) collective-permute-start(bf16[384,512]{1,0:T(8,128)(2,1)S(1)} %get-tuple-element.64), channel_id=1, source_target_pairs={{2,0},{4,2},{6,4},{1,3},{3,5},{5,7},{10,8},{12,10},{14,12},{9,11},... | collective-permute-start | bytes 1179656 | tf_op jit(solution)/shard_map/ppermute | solution.py:257
  131.3 59.5 %collective-permute-start.22 = (bf16[2,384,512]{2,1,0:T(8,128)(2,1)S(1)}, bf16[2,384,512]{2,1,0:T(8,128)(2,1)S(1)}, u32[]{:S(2)}, u32[]{:S(2)}) collective-permute-start(bf16[2,384,512]{2,1,0:T(8,128)(2,1)S(1)} %get-tuple-element.66), channel_id=1, source_target_pairs={{0,8},{8,0},{16,24},{24,16},{1,9},{9,1},{17,25},{25,17},{2,10},{10... | collective-permute-start | bytes 2359304 | tf_op jit(solution)/shard_map/ppermute | solution.py:261
  131.4 62.3 %collective-permute-start.23 = (bf16[2,384,512]{2,1,0:T(8,128)(2,1)S(1)}, bf16[2,384,512]{2,1,0:T(8,128)(2,1)S(1)}, u32[]{:S(2)}, u32[]{:S(2)}) collective-permute-start(bf16[2,384,512]{2,1,0:T(8,128)(2,1)S(1)} %get-tuple-element.67), channel_id=1, source_target_pairs={{8,16},{16,8},{9,17},{17,9},{10,18},{18,10},{11,19},{19,11},{12,20... | collective-permute-start | bytes 2359304 | tf_op jit(solution)/shard_map/ppermute | solution.py:262
  154.7 0.9 copy-start.4
  155.6 27.5 %collective-permute-start.14 = (bf16[384,512]{1,0:T(8,128)(2,1)S(1)}, bf16[384,512]{1,0:T(8,128)(2,1)S(1)}, u32[]{:S(2)}, u32[]{:S(2)}) collective-permute-start(bf16[384,512]{1,0:T(8,128)(2,1)S(1)} %get-tuple-element.57), channel_id=1, source_target_pairs={{2,0},{4,2},{6,4},{1,3},{3,5},{5,7},{10,8},{12,10},{14,12},{9,11},... | collective-permute-start | bytes 1179656 | tf_op jit(solution)/shard_map/ppermute | solution.py:257
  178.2 12.5 %copy-start.3 = (f32[384,512]{1,0:T(8,128)}, f32[384,512]{1,0:T(8,128)S(1)}, u32[]{:S(2)}) copy-start(f32[384,512]{1,0:T(8,128)S(1)} %get-tuple-element.48.own_q) | copy-start | bytes 2359300
  178.2 8.8 %collective-permute-start.8 = (bf16[384,512]{1,0:T(8,128)(2,1)S(1)}, bf16[384,512]{1,0:T(8,128)(2,1)S(1)}, u32[]{:S(2)}, u32[]{:S(2)}) collective-permute-start(bf16[384,512]{1,0:T(8,128)(2,1)S(1)} %get-tuple-element.50), channel_id=1, source_target_pairs={{2,0},{4,2},{6,4},{1,3},{3,5},{5,7},{10,8},{12,10},{14,12},{9,11},... | collective-permute-start | bytes 1179656 | tf_op jit(solution)/shard_map/ppermute | solution.py:257
  180.2 10.5 %collective-permute-start.21 = (bf16[384,512]{1,0:T(8,128)(2,1)S(1)}, bf16[384,512]{1,0:T(8,128)(2,1)S(1)}, u32[]{:S(2)}, u32[]{:S(2)}) collective-permute-start(bf16[384,512]{1,0:T(8,128)(2,1)S(1)} %add_convert_fusion), channel_id=1, source_target_pairs={{0,1},{1,0},{2,3},{3,2},{4,5},{5,4},{6,7},{7,6},{8,9},{9,8},{10,11... | collective-permute-start | bytes 1179656 | tf_op jit(solution)/shard_map/ppermute | solution.py:258
  183.1 24.9 %collective-permute-start.16 = (bf16[2,384,512]{2,1,0:T(8,128)(2,1)}, bf16[2,384,512]{2,1,0:T(8,128)(2,1)S(1)}, u32[]{:S(2)}, u32[]{:S(2)}) collective-permute-start(bf16[2,384,512]{2,1,0:T(8,128)(2,1)} %get-tuple-element.59), channel_id=1, source_target_pairs={{0,8},{8,0},{16,24},{24,16},{1,9},{9,1},{17,25},{25,17},{2,10},{10... | collective-permute-start | bytes 2359304 | tf_op jit(solution)/shard_map/ppermute | solution.py:261
  187.0 21.1 %collective-permute-start.17 = (bf16[2,384,512]{2,1,0:T(8,128)(2,1)}, bf16[2,384,512]{2,1,0:T(8,128)(2,1)S(1)}, u32[]{:S(2)}, u32[]{:S(2)}) collective-permute-start(bf16[2,384,512]{2,1,0:T(8,128)(2,1)} %get-tuple-element.60), channel_id=1, source_target_pairs={{8,16},{16,8},{9,17},{17,9},{10,18},{18,10},{11,19},{19,11},{12,20... | collective-permute-start | bytes 2359304 | tf_op jit(solution)/shard_map/ppermute | solution.py:262
  190.7 13.2 %copy-start.22 = (bf16[384,512]{1,0:T(8,128)(2,1)}, bf16[384,512]{1,0:T(8,128)(2,1)S(1)}, u32[]{:S(2)}) copy-start(bf16[384,512]{1,0:T(8,128)(2,1)S(1)} %collective-permute-done.21.back_q) | copy-start | bytes 1179652
  190.7 22.6 %collective-permute-start.10 = (bf16[2,384,512]{2,1,0:T(8,128)(2,1)}, bf16[2,384,512]{2,1,0:T(8,128)(2,1)S(1)}, u32[]{:S(2)}, u32[]{:S(2)}) collective-permute-start(bf16[2,384,512]{2,1,0:T(8,128)(2,1)} %get-tuple-element.52), channel_id=1, source_target_pairs={{0,8},{8,0},{16,24},{24,16},{1,9},{9,1},{17,25},{25,17},{2,10},{10... | collective-permute-start | bytes 2359304 | tf_op jit(solution)/shard_map/ppermute | solution.py:261
  190.8 5.9 %copy-start.16 = (bf16[2,384,512]{2,1,0:T(8,128)(2,1)}, bf16[2,384,512]{2,1,0:T(8,128)(2,1)S(1)}, u32[]{:S(2)}) copy-start(bf16[2,384,512]{2,1,0:T(8,128)(2,1)S(1)} %collective-permute-done.22.near) | copy-start | bytes 2359300
  190.8 11.9 %collective-permute-start.15 = (bf16[384,512]{1,0:T(8,128)(2,1)S(1)}, bf16[384,512]{1,0:T(8,128)(2,1)S(1)}, u32[]{:S(2)}, u32[]{:S(2)}) collective-permute-start(bf16[384,512]{1,0:T(8,128)(2,1)S(1)} %add_convert_fusion.1), channel_id=1, source_target_pairs={{0,1},{1,0},{2,3},{3,2},{4,5},{5,4},{6,7},{7,6},{8,9},{9,8},{10,11... | collective-permute-start | bytes 1179656 | tf_op jit(solution)/shard_map/ppermute | solution.py:258
  193.7 9.1 %copy-start.17 = (bf16[2,384,512]{2,1,0:T(8,128)(2,1)}, bf16[2,384,512]{2,1,0:T(8,128)(2,1)S(1)}, u32[]{:S(2)}) copy-start(bf16[2,384,512]{2,1,0:T(8,128)(2,1)S(1)} %collective-permute-done.23.far) | copy-start | bytes 2359300
  193.7 19.7 %collective-permute-start.11 = (bf16[2,384,512]{2,1,0:T(8,128)(2,1)}, bf16[2,384,512]{2,1,0:T(8,128)(2,1)S(1)}, u32[]{:S(2)}, u32[]{:S(2)}) collective-permute-start(bf16[2,384,512]{2,1,0:T(8,128)(2,1)} %get-tuple-element.53), channel_id=1, source_target_pairs={{8,16},{16,8},{9,17},{17,9},{10,18},{18,10},{11,19},{19,11},{12,20... | collective-permute-start | bytes 2359304 | tf_op jit(solution)/shard_map/ppermute | solution.py:262
  202.8 1.1 copy-start.23
  202.8 10.5 %collective-permute-start.9 = (bf16[384,512]{1,0:T(8,128)(2,1)}, bf16[384,512]{1,0:T(8,128)(2,1)}, u32[]{:S(2)}, u32[]{:S(2)}) collective-permute-start(bf16[384,512]{1,0:T(8,128)(2,1)} %add_convert_fusion.2), channel_id=1, source_target_pairs={{0,1},{1,0},{2,3},{3,2},{4,5},{5,4},{6,7},{7,6},{8,9},{9,8},{10,11... | collective-permute-start | bytes 1179656 | tf_op jit(solution)/shard_map/ppermute | solution.py:258
  208.0 0.9 copy-start.19
  208.1 1.1 copy-start.20
  213.3 0.9 copy-start.18
  213.3 1.1 copy-start.21

commit v2 on v1

v2 whole, which is shorter than its diff:
```python
import functools
import math

import jax
import jax.numpy as jnp
from jax import lax
from jax.experimental import pallas as pl
from jax.experimental.pallas import tpu as pltpu
from jax.sharding import PartitionSpec as P

F32 = jnp.float32
BF16 = jnp.bfloat16
LOG2E = math.log2(math.e)
FAR_AWAY = 1e30

OUTER, OWN, PARTNER = (0, 1, 2)
HERE, NEAR, FAR = (0, 1, 2)
CHUNKS = (3, 3, 3, 3)
STAGES = (
    ((HERE, (OWN, PARTNER)), (NEAR, (OWN, PARTNER))),
    ((HERE, (OUTER,)), (NEAR, (OUTER,)), (FAR, (OWN, PARTNER, OUTER))),
)
EXTRA = 32


def dot(a, b, dims):
    return lax.dot_general(a, b, (dims, ((), ())), preferred_element_type=F32)


def three_terms(row):
    terms = []
    for _ in range(3):
        term = row.astype(BF16).astype(F32)
        terms.append(term)
        row = row - term
    return terms


def fold(row):
    lanes = 128
    return [row[:, i : i + lanes] for i in range(0, row.shape[1], lanes)]


def prep_kernel(first, count, q_ref, g_ref, o_ref, lse_ref, flag_ref, out):
    tile = q_ref.shape[0]
    width = q_ref.shape[1] // count
    out[0:tile, :] = q_ref[...]
    out[tile : 2 * tile, :] = g_ref[...]
    ones = jnp.ones((8, width), BF16)
    for h in range(count):
        cols = slice(h * width, (h + 1) * width)
        prod = g_ref[:, cols].astype(F32) * o_ref[:, cols].astype(F32)
        high = prod.astype(BF16)
        low = (prod - high.astype(F32)).astype(BF16)
        delta = dot(ones, high, ((1,), (1,))) + dot(ones, low, ((1,), (1,)))
        rows = []
        for row in (lse_ref[first + h : first + h + 1, :] * LOG2E, delta[0:1, :]):
            for term in three_terms(row):
                rows += fold(term)
        rows.append(flag_ref[...])
        rows.append(jnp.zeros((EXTRA - len(rows), width), F32))
        out[2 * tile : 2 * tile + EXTRA, cols] = jnp.concatenate(rows, axis=0).astype(BF16)


def prep(first, count, head_width, q, g, o, lse, flags):
    tile, full = q.shape
    wide = count * head_width
    offset = first * head_width
    cols = pl.BlockSpec((pl.Element(tile), pl.Element(wide)), lambda i: (0, offset))
    return pl.pallas_call(
        functools.partial(prep_kernel, first, count),
        grid=(1,),
        in_specs=[
            cols,
            cols,
            cols,
            pl.BlockSpec(lse.shape, lambda i: (0, 0)),
            pl.BlockSpec(flags.shape, lambda i: (0, 0)),
        ],
        out_specs=pl.BlockSpec((2 * tile + EXTRA, wide), lambda i: (0, 0)),
        out_shape=jax.ShapeDtypeStruct((2 * tile + EXTRA, wide), BF16),
        cost_estimate=pl.CostEstimate(
            flops=2 * tile * wide, bytes_accessed=10 * tile * wide, transcendentals=0
        ),
        name="prep",
    )(q, g, o, lse, flags)


def row_stats(message, tile):
    extra = message[2 * tile : 2 * tile + EXTRA, :].astype(F32)
    parts = tile // 128
    rows = []
    for base in (0, 3 * parts):
        pieces = []
        for p in range(parts):
            a, b, c = (extra[base + i * parts + p : base + i * parts + p + 1] for i in range(3))
            pieces.append(a + b + c)
        rows.append(jnp.concatenate(pieces, axis=1))
    return (rows[0], rows[1], extra[6 * parts : 6 * parts + 1])


def stage_kernel(work, names, carried, factor, far_ref, *refs):
    env = dict(zip(names, refs))
    tile = env["message%d" % work[0][1][0]].shape[0] - EXTRA
    tile //= 2
    used = sorted({j for _, js in work for j in js})
    stats = {j: row_stats(env["message%d" % j], tile) for j in used}
    started = set()

    def add_q(j, term):
        name = "q%d" % j
        if name in started:
            env["sum_" + name][...] += term
        elif "acc_" + name in env:
            env["sum_" + name][...] = env["acc_" + name][...] + term
        else:
            env["sum_" + name][...] = term
        started.add(name)

    def key_frame(slot, js):
        key = env["k%d" % slot][...]
        value = env["v%d" % slot][...]
        name = "acc_kv%d" % slot
        dk, dv = (env[name][0], env[name][1]) if name in env else (None, None)
        for j in js:
            message = env["message%d" % j]
            qj = message[0:tile, :]
            gj = message[tile : 2 * tile, :]
            shift, delta, flags = stats[j]
            lane = 3 * j + slot
            shift = jnp.where(flags[:, lane : lane + 1] > 0, shift, FAR_AWAY)
            scores = dot(key, qj, ((1,), (1,)))
            weights = jnp.exp2(scores * (factor * LOG2E) - shift)
            grad_prob = dot(value, gj, ((1,), (1,)))
            grad_score = (weights * (grad_prob - delta)).astype(BF16)
            term_v = dot(weights.astype(BF16), gj, ((1,), (0,)))
            term_k = dot(grad_score, qj, ((1,), (0,))) * factor
            add_q(j, dot(grad_score, key, ((0,), (0,))))
            dv = term_v if dv is None else dv + term_v
            dk = term_k if dk is None else dk + term_k
        out = env["out_kv%d" % slot]
        out[0] = dk.astype(out.dtype)
        out[1] = dv.astype(out.dtype)

    for slot, js in work:
        if slot != FAR:
            key_frame(slot, js)
    for slot, js in work:
        if slot == FAR:
            pl.when(far_ref[0] > 0)(functools.partial(key_frame, slot, js))

            @pl.when(far_ref[0] == 0)
            def _():
                out = env["out_kv%d" % FAR]
                out[...] = jnp.zeros_like(out)
                for j in js:
                    name = "q%d" % j
                    if name not in carried:
                        continue
                    env["sum_" + name][...] = env["acc_" + name][...]

    for j in used:
        out = env["out_q%d" % j]
        out[...] = (env["sum_q%d" % j][...]).astype(out.dtype)


def run_stage(work, last, first, count, head_width, far, keys, messages, sums):
    rows, wide = next(iter(messages.values())).shape
    tile = (rows - EXTRA) // 2
    one = pl.BlockSpec((tile, head_width), lambda h, *_: (0, h))
    two = pl.BlockSpec((2, tile, head_width), lambda h, *_: (0, 0, h))
    cols = pl.BlockSpec((tile, head_width), lambda h, *_: (0, h + first))
    whole = pl.BlockSpec((rows, head_width), lambda h, *_: (0, h))
    used = sorted({j for _, js in work for j in js})
    slots = [slot for slot, _ in work]
    names, args, specs = ([], [], [])

    def give(name, arg, spec):
        names.append(name)
        args.append(arg)
        specs.append(spec)

    for j in used:
        give("message%d" % j, messages[j], whole)
    for slot in slots:
        give("k%d" % slot, keys[slot][0], cols)
        give("v%d" % slot, keys[slot][1], cols)
    touched = [("q%d" % j, one) for j in used] + [("kv%d" % s, two) for s in slots]
    carried = [name for name, _ in touched if name in sums]
    for name, spec in touched:
        if name in sums:
            give("acc_" + name, sums[name], spec)
    out_specs, out_shapes = ([], [])
    for name, spec in touched:
        names.append("out_" + name)
        out_specs.append(spec)
        shape = (tile, wide) if name.startswith("q") else (2, tile, wide)
        out_shapes.append(jax.ShapeDtypeStruct(shape, BF16 if name in last else F32))
    names += ["sum_q%d" % j for j in used]
    pairs = count * sum(len(js) for _, js in work)
    results = pl.pallas_call(
        functools.partial(stage_kernel, work, names, carried, head_width**-0.5),
        grid_spec=pltpu.PrefetchScalarGridSpec(
            num_scalar_prefetch=1,
            grid=(count,),
            in_specs=specs,
            out_specs=out_specs,
            scratch_shapes=[pltpu.VMEM((tile, head_width), F32)] * len(used),
        ),
        out_shape=out_shapes,
        compiler_params=pltpu.CompilerParams(vmem_limit_bytes=40 * 1024 * 1024),
        cost_estimate=pl.CostEstimate(
            flops=20 * pairs * tile * tile * head_width,
            bytes_accessed=40 * tile * wide,
            transcendentals=pairs * tile * tile,
        ),
        name="pairs",
    )(far, *args)
    return {**sums, **{name: value for (name, _), value in zip(touched, results)}}


def finish_kernel(factor, own_q, back_q, own_kv, near, far, *rest):
    out_q, out_k, out_v = rest[-3:]
    out_q[...] = (own_q[...] * factor + back_q[...].astype(F32)).astype(BF16)
    sums = own_kv[...] + near[...].astype(F32) + far[...].astype(F32)
    out_k[...] = sums[0].astype(BF16)
    out_v[...] = sums[1].astype(BF16)


def finish(first, count, head_width, full, parts, so_far):
    tile = parts[0].shape[0]
    one = pl.BlockSpec((tile, head_width), lambda h: (0, h))
    two = pl.BlockSpec((2, tile, head_width), lambda h: (0, 0, h))
    cols = pl.BlockSpec((tile, head_width), lambda h: (0, h + first))
    kept = [] if so_far is None else list(so_far)
    return pl.pallas_call(
        functools.partial(finish_kernel, head_width**-0.5),
        grid=(count,),
        in_specs=[one, one, two, two, two] + [pl.BlockSpec(memory_space=pl.ANY)] * len(kept),
        out_specs=[cols] * 3,
        out_shape=[jax.ShapeDtypeStruct((tile, full), BF16)] * 3,
        input_output_aliases={5 + i: i for i in range(len(kept))},
        cost_estimate=pl.CostEstimate(
            flops=8 * tile * count * head_width,
            bytes_accessed=30 * tile * count * head_width,
            transcendentals=0,
        ),
        name="finish",
    )(*parts, *kept)


def pair_flags(window_mask, lanes):
    mask = window_mask.reshape(9)
    frames, rows = (lax.axis_size("tm"), lax.axis_size("space"))
    frame, row = (lax.axis_index("tm"), lax.axis_index("space"))
    toward = 1 - 2 * lax.rem(row, 2)
    near = 1 - 2 * lax.rem(frame, 2)
    lane = jnp.arange(9, dtype=jnp.int32)
    row_off = (lane // 3 - 1) * toward
    slot = lane % 3
    frame_off = jnp.where(slot == NEAR, near, jnp.where(slot == FAR, -near, 0))
    inside = (
        (row + row_off >= 0)
        & (row + row_off < rows)
        & (frame + frame_off >= 0)
        & (frame + frame_off < frames)
    )
    index = 3 * (frame_off + 1) + row_off + 1
    picked = jnp.sum(jnp.where(index[:, None] == lane[None, :], mask[None, :], 0), axis=1)
    flags = (inside & ((picked > 0) | (index == 4))).astype(F32)
    return jnp.pad(flags, (0, lanes - 9)).reshape(1, lanes)


def after(value, *earlier):
    return lax.optimization_barrier((value, *earlier))[0]


def per_device(queries, keys, values, outputs, out_grads, log_sums, window_mask):
    tile, full = queries.shape[2:]
    heads = log_sums.shape[2]
    width = full // heads
    frames, rows = (lax.axis_size("tm"), lax.axis_size("space"))
    q, k, v, o, g = (a.reshape(tile, full) for a in (queries, keys, values, outputs, out_grads))
    partner = [(i, i ^ 1) for i in range(rows)]
    onward = [(i, i + 2) for i in range(0, rows - 2, 2)]
    onward += [(i, i - 2) for i in range(3, rows, 2)]
    homeward = [(b, a) for a, b in onward]
    near_pairs = [(i, i ^ 1) for i in range(frames)]
    far_pairs = [(i, i + 1) for i in range(1, frames - 1, 2)]
    far_pairs += [(b, a) for a, b in far_pairs]

    frame = lax.axis_index("tm")
    far_frame = frame - 1 + 2 * lax.rem(frame, 2)
    has_far = ((far_frame >= 0) & (far_frame < frames)).astype(jnp.int32).reshape(1)

    firsts = [sum(CHUNKS[:c]) for c in range(len(CHUNKS))]
    flags = pair_flags(window_mask, width)
    lse = log_sums.reshape(heads, tile)
    near_kv = [lax.ppermute(a, "tm", near_pairs) for a in (k, v)]
    far_kv = [lax.ppermute(a, "tm", far_pairs) for a in (k, v)]
    mine, theirs, outers = ([], [], [])
    for c, count in enumerate(CHUNKS):
        source = q
        if c == 1:
            source = after(q, *near_kv)
        if c >= 2:
            source = after(q, theirs[c - 2])
        mine.append(prep(firsts[c], count, width, source, g, o, lse, flags))
        theirs.append(lax.ppermute(mine[c], "space", partner))
        outers.append(lax.ppermute(theirs[c], "space", onward))
    frames_kv = {HERE: (k, v), NEAR: near_kv, FAR: far_kv}

    out = None
    for c, count in enumerate(CHUNKS):
        messages = {OUTER: outers[c], OWN: mine[c], PARTNER: theirs[c]}
        sums = {}
        for step, work in enumerate(STAGES):
            last = ("q0", "kv1", "kv2") if step + 1 == len(STAGES) else ()
            needed = {j: messages[j] for _, js in work for j in js}
            sums = run_stage(
                work, last, firsts[c], count, width, has_far, frames_kv, needed, sums
            )
        home = lax.ppermute(sums["q0"], "space", homeward)
        total = (sums["q2"] + home.astype(F32)) * (width**-0.5)
        dq_back = lax.ppermute(total.astype(BF16), "space", partner)
        near_back = lax.ppermute(sums["kv1"], "tm", near_pairs)
        far_back = lax.ppermute(sums["kv2"], "tm", far_pairs)
        out = finish(
            firsts[c], count, width, full,
            (sums["q1"], dq_back, sums["kv0"], near_back, far_back), out,
        )
    return tuple(a.reshape(queries.shape) for a in out)


def solution(mesh):
    tile = P("tm", "space", None, None)
    return jax.shard_map(
        per_device,
        mesh=mesh,
        in_specs=(tile,) * 6 + (P("tm", "space", None),),
        out_specs=(tile,) * 3,
        check_vma=False,
    )
```

time: 221 us -> 176 us (0.80)
  waiting for transfers between devices: 76.8 us -> 9.53 us
  Pallas kernels: 82.8 us -> 92.4 us
  starting transfers between devices: 45.1 us -> 52.2 us
  local copies, waits for them, and re-layouts: 10.3 us -> 16.1 us
    ppermute x20 -> x24, waiting for transfers between devices: 60.3 us -> 9.52 us  [the longest x4 8.34 us: per_device(): theirs.append(lax.ppermute(mine[c], 'space', partner))]
    ppermute x2, waiting for transfers between devices: 16.5 us -> 0.01 us  [per_device(): far_kv = [lax.ppermute(a, 'tm', far_pairs) for a in (k, v)]]
    ppermute x20 -> x24, starting transfers between devices: 36 us -> 45.7 us  [the longest x4 15.7 us: per_device(): far_back = lax.ppermute(sums['kv2'], 'tm', far_pairs)]
    pallas_call x7 -> x16, Pallas kernels: 82.8 us -> 92.4 us  [the longest x8 68.5 us: run_stage(): pl.pallas_call(functools.partial(stage_kernel, work, names, carried, head...]
    unnamed x49 -> x71, local copies, waits for them, and re-layouts: 10.3 us -> 16.1 us
    ppermute x2, starting transfers between devices: 3.5 us -> 0.82 us  [per_device(): near_kv = [lax.ppermute(a, 'tm', near_pairs) for a in (k, v)]]
  transfers between devices with their start and end apart: 24 -> 28, of which waited for: 5 -> 3; matrix products, arithmetic and copies ran while one was open for 1% -> 3% of each run, Pallas kernels for 32% -> 51%
where the time goes in v2:
time: 176 us; the launch traced here: 175 us
  Pallas kernels  92.4 us (52%)
  starting transfers between devices  52.2 us (30%)
  local copies, waits for them, and re-layouts  16.1 us (9%)
  waiting for transfers between devices  9.53 us (5%)
  other arithmetic  3.27 us (2%)
    pallas_call x8, Pallas kernels, run_stage(): pl.pallas_call(functools.partial(stage_kernel, work, names, carried, head...  68.5 us
    unnamed x71, local copies, waits for them, and re-layouts  16.1 us
    ppermute x4, starting transfers between devices, per_device(): far_back = lax.ppermute(sums['kv2'], 'tm', far_pairs)  15.7 us
    pallas_call x4, Pallas kernels, finish(): pl.pallas_call(functools.partial(finish_kernel, head_width ** (-0.5)), gr...  14.4 us
    ppermute x4, starting transfers between devices, per_device(): outers.append(lax.ppermute(theirs[c], 'space', onward))  12.1 us
    ppermute x4, starting transfers between devices, per_device(): home = lax.ppermute(sums['q0'], 'space', homeward)  11.3 us
    pallas_call x4, Pallas kernels, prep(): pl.pallas_call(functools.partial(prep_kernel, first, count), grid=(1,), i...  9.54 us
    ppermute x4, waiting for transfers between devices, per_device(): theirs.append(lax.ppermute(mine[c], 'space', partner))  8.34 us
  transfers between devices with their start and end apart: 28, of which 3 were waited for; matrix products, arithmetic and copies ran while one was open for 3% of the time, Pallas kernels for 51%

profile of v2, /device:TPU:9, one launch (start us, length us, event | category | flops | bytes accessed | tf_op | source)
XLA Modules:
  0.0 174.6 jit_solution(9092372520014294967)
XLA Ops:
  2.3 1.3 copy.21
  4.2 2.4 %prep.6.refs_0_.refs_1_ = bf16[800,384]{1,0:T(8,128)(2,1)} custom-call(bf16[384,1536]{1,0:T(8,128)(2,1)} %bitcast.25, bf16[384,1536]{1,0:T(8,128)(2,1)} %bitcast.29, bf16[384,1536]{1,0:T(8,128)(2,1)} %bitcast.33, f32[12,384]{1,0:T(8,128)} %bitcast.40, f32[1,128]{1,0:T(1,128)} %fusion.2.flag_ref), custom_call_target="tpu_custom_call" | custom-call | flops 294912 | bytes 1474560 | tf_op jit(solution)/shard_map/prep/pallas_call | solution.py:70
  6.6 1.2 collective-permute-start.11
  7.8 3.7 %collective-permute-start.5 = (bf16[384,1536]{1,0:T(8,128)(2,1)S(1)}, bf16[384,1536]{1,0:T(8,128)(2,1)}, u32[]{:S(2)}, u32[]{:S(2)}) collective-permute-start(bf16[384,1536]{1,0:T(8,128)(2,1)S(1)} %bitcast.16), channel_id=1, source_target_pairs={{8,16},{16,8},{9,17},{17,9},{10,18},{18,10},{11,19},{19,11},{12,20... | collective-permute-start | bytes 3538952 | tf_op jit(solution)/shard_map/ppermute | solution.py:300
  11.6 1.9 %collective-permute-start.6 = (bf16[384,1536]{1,0:T(8,128)(2,1)}, bf16[384,1536]{1,0:T(8,128)(2,1)}, u32[]{:S(2)}, u32[]{:S(2)}) collective-permute-start(bf16[384,1536]{1,0:T(8,128)(2,1)} %bitcast.3.refs_3_.refs_4_), channel_id=1, source_target_pairs={{8,16},{16,8},{9,17},{17,9},{10,18},{18,10},{11,19},{19,11},{12,20... | collective-permute-start | bytes 3538952 | tf_op jit(solution)/shard_map/ppermute | solution.py:300
  13.5 8.3 %collective-permute-done.11.refs_1_.refs_2_ = bf16[800,384]{1,0:T(8,128)(2,1)S(1)} collective-permute-done((bf16[800,384]{1,0:T(8,128)(2,1)}, bf16[800,384]{1,0:T(8,128)(2,1)S(1)}, u32[]{:S(2)}, u32[]{:S(2)}) %collective-permute-start.11) | collective-permute-done | bytes 614432 | tf_op jit(solution)/shard_map/ppermute | solution.py:309
  21.8 3.2 %collective-permute-start.23 = (bf16[800,384]{1,0:T(8,128)(2,1)S(1)}, bf16[800,384]{1,0:T(8,128)(2,1)}, u32[]{:S(2)}, u32[]{:S(2)}) collective-permute-start(bf16[800,384]{1,0:T(8,128)(2,1)S(1)} %collective-permute-done.11.refs_1_.refs_2_), channel_id=1, source_target_pairs={{0,2},{2,4},{4,6},{3,1},{5,3},{7,5},{8,10},{10,12},{12,14},{11,9},... | collective-permute-start | bytes 1843208 | tf_op jit(solution)/shard_map/ppermute | solution.py:310
  25.0 2.3 %prep.7.refs_0_.refs_1_ = bf16[800,384]{1,0:T(8,128)(2,1)} custom-call(bf16[384,1536]{1,0:T(8,128)(2,1)} %bitcast.26, bf16[384,1536]{1,0:T(8,128)(2,1)} %bitcast.30, bf16[384,1536]{1,0:T(8,128)(2,1)} %bitcast.34, f32[12,384]{1,0:T(8,128)} %bitcast.41, f32[1,128]{1,0:T(1,128)} %fusion.2.flag_ref), custom_call_target="tpu_custom_call" | custom-call | flops 294912 | bytes 1474560 | tf_op jit(solution)/shard_map/prep/pallas_call | solution.py:70
  27.5 2.5 %prep.4.refs_0_.refs_1_ = bf16[800,384]{1,0:T(8,128)(2,1)} custom-call(bf16[384,1536]{1,0:T(8,128)(2,1)} %bitcast.27, bf16[384,1536]{1,0:T(8,128)(2,1)} %bitcast.31, bf16[384,1536]{1,0:T(8,128)(2,1)} %bitcast.35, f32[12,384]{1,0:T(8,128)} %bitcast.42, f32[1,128]{1,0:T(1,128)} %fusion.2.flag_ref), custom_call_target="tpu_custom_call" | custom-call | flops 294912 | bytes 1474560 | tf_op jit(solution)/shard_map/prep/pallas_call | solution.py:70
  29.9 1.3 collective-permute-start.2
  31.2 7.1 %pairs.14 = (f32[384,384]{1,0:T(8,128)S(1)}, f32[384,384]{1,0:T(8,128)S(1)}, f32[2,384,384]{2,1,0:T(8,128)S(1)}, f32[2,384,384]{2,1,0:T(8,128)S(1)}) custom-call(s32[1]{0:T(128)} %bitcast.far_ref, bf16[800,384]{1,0:T(8,128)(2,1)S(1)} %copy-done.7, bf16[800,384]{1,0:T(8,128)(2,1)S(1)} %collective-permute-done.11.refs_1_.refs_2_, ...), custom_call_target="tpu_custom_call" | custom-call | flops 4529848320 | bytes 5898240 | tf_op jit(solution)/shard_map/pairs/pallas_call | solution.py:201
  38.4 1.0 copy-done.21
  39.4 1.0 copy-done.22
  40.4 1.1 copy-done.14
  41.5 10.2 %pairs.15 = (bf16[384,384]{1,0:T(8,128)(2,1)S(1)}, f32[384,384]{1,0:T(8,128)S(1)}, f32[384,384]{1,0:T(8,128)S(1)}, f32[2,384,384]{2,1,0:T(8,128)S(1)}, bf16[2,38...) custom-call(s32[1]{0:T(128)} %bitcast.far_ref, bf16[800,384]{1,0:T(8,128)(2,1)} %collective-permute-done.23.refs_0_, ...), custom_call_target="tpu_custom_call" | custom-call | flops 5662310400 | bytes 5898240 | tf_op jit(solution)/shard_map/pairs/pallas_call | solution.py:201
  51.7 2.9 %collective-permute-start.24 = (bf16[384,384]{1,0:T(8,128)(2,1)S(1)}, bf16[384,384]{1,0:T(8,128)(2,1)S(1)}, u32[]{:S(2)}, u32[]{:S(2)}) collective-permute-start(bf16[384,384]{1,0:T(8,128)(2,1)S(1)} %get-tuple-element.97), channel_id=1, source_target_pairs={{2,0},{4,2},{6,4},{1,3},{3,5},{5,7},{10,8},{12,10},{14,12},{9,11},... | collective-permute-start | bytes 884744 | tf_op jit(solution)/shard_map/ppermute | solution.py:323
  54.6 5.4 %collective-permute-start.27 = (bf16[2,384,384]{2,1,0:T(8,128)(2,1)}, bf16[2,384,384]{2,1,0:T(8,128)(2,1)}, u32[]{:S(2)}, u32[]{:S(2)}) collective-permute-start(bf16[2,384,384]{2,1,0:T(8,128)(2,1)} %get-tuple-element.100), channel_id=1, source_target_pairs={{8,16},{16,8},{9,17},{17,9},{10,18},{18,10},{11,19},{19,11},{12,20... | collective-permute-start | bytes 1769480 | tf_op jit(solution)/shard_map/ppermute | solution.py:327
  60.1 2.4 %collective-permute-start.13 = (bf16[800,384]{1,0:T(8,128)(2,1)}, bf16[800,384]{1,0:T(8,128)(2,1)}, u32[]{:S(2)}, u32[]{:S(2)}) collective-permute-start(bf16[800,384]{1,0:T(8,128)(2,1)} %collective-permute-done.12.refs_1_.refs_2_), channel_id=1, source_target_pairs={{0,2},{2,4},{4,6},{3,1},{5,3},{7,5},{8,10},{10,12},{12,14},{11,9},... | collective-permute-start | bytes 1843208 | tf_op jit(solution)/shard_map/ppermute | solution.py:310
  62.5 7.2 %pairs.10 = (f32[384,384]{1,0:T(8,128)S(1)}, f32[384,384]{1,0:T(8,128)S(1)}, f32[2,384,384]{2,1,0:T(8,128)S(1)}, f32[2,384,384]{2,1,0:T(8,128)S(1)}) custom-call(s32[1]{0:T(128)} %bitcast.far_ref, bf16[800,384]{1,0:T(8,128)(2,1)S(1)} %copy-done.6, bf16[800,384]{1,0:T(8,128)(2,1)} %collective-permute-done.12.refs_1_.refs_2_, bf16[384,1536]{1,0:T(8,128)(2,1)S(1)} %bitcast.19, ...), custom_call_target="tpu_custom_call" | custom-call | flops 4529848320 | bytes 5898240 | tf_op jit(solution)/shard_map/pairs/pallas_call | solution.py:201
  69.7 1.0 copy-done.18
  72.4 0.9 multiply_convert_fusion
  73.6 2.3 %prep.5.refs_0_.refs_1_ = bf16[800,384]{1,0:T(8,128)(2,1)} custom-call(bf16[384,1536]{1,0:T(8,128)(2,1)} %bitcast.28, bf16[384,1536]{1,0:T(8,128)(2,1)} %bitcast.32, bf16[384,1536]{1,0:T(8,128)(2,1)} %bitcast.36, f32[12,384]{1,0:T(8,128)} %bitcast.43, f32[1,128]{1,0:T(1,128)} %fusion.2.flag_ref), custom_call_target="tpu_custom_call" | custom-call | flops 294912 | bytes 1474560 | tf_op jit(solution)/shard_map/prep/pallas_call | solution.py:70
  75.9 4.0 %collective-permute-start.18 = (bf16[800,384]{1,0:T(8,128)(2,1)S(1)}, bf16[800,384]{1,0:T(8,128)(2,1)S(1)}, u32[]{:S(2)}, u32[]{:S(2)}) collective-permute-start(bf16[800,384]{1,0:T(8,128)(2,1)S(1)} %collective-permute-done.2.refs_1_.refs_2_), channel_id=1, source_target_pairs={{0,2},{2,4},{4,6},{3,1},{5,3},{7,5},{8,10},{10,12},{12,14},{11,9},... | collective-permute-start | bytes 1843208 | tf_op jit(solution)/shard_map/ppermute | solution.py:310
  79.9 1.1 copy-done.24
  81.0 1.1 copy-done.26
  82.0 10.2 %pairs.11 = (bf16[384,384]{1,0:T(8,128)(2,1)S(1)}, f32[384,384]{1,0:T(8,128)S(1)}, f32[384,384]{1,0:T(8,128)S(1)}, f32[2,384,384]{2,1,0:T(8,128)S(1)}, bf16[2,38...) custom-call(s32[1]{0:T(128)} %bitcast.far_ref, bf16[800,384]{1,0:T(8,128)(2,1)} %collective-permute-done.13.refs_0_, ...), custom_call_target="tpu_custom_call" | custom-call | flops 5662310400 | bytes 5898240 | tf_op jit(solution)/shard_map/pairs/pallas_call | solution.py:201
  93.1 2.0 %collective-permute-start.14 = (bf16[384,384]{1,0:T(8,128)(2,1)S(1)}, bf16[384,384]{1,0:T(8,128)(2,1)S(1)}, u32[]{:S(2)}, u32[]{:S(2)}) collective-permute-start(bf16[384,384]{1,0:T(8,128)(2,1)S(1)} %get-tuple-element.77), channel_id=1, source_target_pairs={{2,0},{4,2},{6,4},{1,3},{3,5},{5,7},{10,8},{12,10},{14,12},{9,11},... | collective-permute-start | bytes 884744 | tf_op jit(solution)/shard_map/ppermute | solution.py:323
  95.2 7.2 %pairs.12 = (f32[384,384]{1,0:T(8,128)S(1)}, f32[384,384]{1,0:T(8,128)S(1)}, f32[2,384,384]{2,1,0:T(8,128)S(1)}, f32[2,384,384]{2,1,0:T(8,128)S(1)}) custom-call(s32[1]{0:T(128)} %bitcast.far_ref, bf16[800,384]{1,0:T(8,128)(2,1)S(1)} %copy-done.4, bf16[800,384]{1,0:T(8,128)(2,1)S(1)} %collective-permute-done.2.refs_1_.refs_2_, ...), custom_call_target="tpu_custom_call" | custom-call | flops 4529848320 | bytes 5898240 | tf_op jit(solution)/shard_map/pairs/pallas_call | solution.py:201
  102.4 1.0 copy-done.20
  103.4 1.3 collective-permute-start.3
  104.8 9.7 %pairs.13 = (bf16[384,384]{1,0:T(8,128)(2,1)S(1)}, f32[384,384]{1,0:T(8,128)S(1)}, f32[384,384]{1,0:T(8,128)S(1)}, f32[2,384,384]{2,1,0:T(8,128)S(1)}, bf16[2,38...) custom-call(s32[1]{0:T(128)} %bitcast.far_ref, bf16[800,384]{1,0:T(8,128)(2,1)S(1)} %collective-permute-done.18.refs_0_, ...), custom_call_target="tpu_custom_call" | custom-call | flops 5662310400 | bytes 5898240 | tf_op jit(solution)/shard_map/pairs/pallas_call | solution.py:201
  114.5 3.4 %collective-permute-start.19 = (bf16[384,384]{1,0:T(8,128)(2,1)S(1)}, bf16[384,384]{1,0:T(8,128)(2,1)S(1)}, u32[]{:S(2)}, u32[]{:S(2)}) collective-permute-start(bf16[384,384]{1,0:T(8,128)(2,1)S(1)} %get-tuple-element.87), channel_id=1, source_target_pairs={{2,0},{4,2},{6,4},{1,3},{3,5},{5,7},{10,8},{12,10},{14,12},{9,11},... | collective-permute-start | bytes 884744 | tf_op jit(solution)/shard_map/ppermute | solution.py:323
  117.9 2.5 %collective-permute-start.4 = (bf16[800,384]{1,0:T(8,128)(2,1)S(1)}, bf16[800,384]{1,0:T(8,128)(2,1)S(1)}, u32[]{:S(2)}, u32[]{:S(2)}) collective-permute-start(bf16[800,384]{1,0:T(8,128)(2,1)S(1)} %collective-permute-done.3.refs_1_.refs_2_), channel_id=1, source_target_pairs={{0,2},{2,4},{4,6},{3,1},{5,3},{7,5},{8,10},{10,12},{12,14},{11,9},... | collective-permute-start | bytes 1843208 | tf_op jit(solution)/shard_map/ppermute | solution.py:310
  120.4 7.2 %pairs.8 = (f32[384,384]{1,0:T(8,128)S(1)}, f32[384,384]{1,0:T(8,128)S(1)}, f32[2,384,384]{2,1,0:T(8,128)S(1)}, f32[2,384,384]{2,1,0:T(8,128)S(1)}) custom-call(s32[1]{0:T(128)} %bitcast.far_ref, bf16[800,384]{1,0:T(8,128)(2,1)S(1)} %copy-done.5, bf16[800,384]{1,0:T(8,128)(2,1)S(1)} %collective-permute-done.3.refs_1_.refs_2_, ...), custom_call_target="tpu_custom_call" | custom-call | flops 4529848320 | bytes 5898240 | tf_op jit(solution)/shard_map/pairs/pallas_call | solution.py:201
  127.6 1.0 copy-done.16
  129.5 0.9 collective-permute-start.20
  130.4 9.6 %pairs.9 = (bf16[384,384]{1,0:T(8,128)(2,1)S(1)}, f32[384,384]{1,0:T(8,128)S(1)}, f32[384,384]{1,0:T(8,128)S(1)}, f32[2,384,384]{2,1,0:T(8,128)S(1)}, bf16[2,384...) custom-call(s32[1]{0:T(128)} %bitcast.far_ref, bf16[800,384]{1,0:T(8,128)(2,1)S(1)} %collective-permute-done.4.refs_0_, ...), custom_call_target="tpu_custom_call" | custom-call | flops 5662310400 | bytes 5898240 | tf_op jit(solution)/shard_map/pairs/pallas_call | solution.py:201
  140.0 1.0 copy-done.3
  141.9 3.0 %collective-permute-start.7 = (bf16[384,384]{1,0:T(8,128)(2,1)S(1)}, bf16[384,384]{1,0:T(8,128)(2,1)S(1)}, u32[]{:S(2)}, u32[]{:S(2)}) collective-permute-start(bf16[384,384]{1,0:T(8,128)(2,1)S(1)} %get-tuple-element.66), channel_id=1, source_target_pairs={{2,0},{4,2},{6,4},{1,3},{3,5},{5,7},{10,8},{12,10},{14,12},{9,11},... | collective-permute-start | bytes 884744 | tf_op jit(solution)/shard_map/ppermute | solution.py:323
  144.9 4.7 %collective-permute-start.22 = (bf16[2,384,384]{2,1,0:T(8,128)(2,1)S(1)}, bf16[2,384,384]{2,1,0:T(8,128)(2,1)S(1)}, u32[]{:S(2)}, u32[]{:S(2)}) collective-permute-start(bf16[2,384,384]{2,1,0:T(8,128)(2,1)S(1)} %get-tuple-element.90), channel_id=1, source_target_pairs={{8,16},{16,8},{9,17},{17,9},{10,18},{18,10},{11,19},{19,11},{12,20... | collective-permute-start | bytes 1769480 | tf_op jit(solution)/shard_map/ppermute | solution.py:327
  149.8 1.9 %collective-permute-start.17 = (bf16[2,384,384]{2,1,0:T(8,128)(2,1)}, bf16[2,384,384]{2,1,0:T(8,128)(2,1)}, u32[]{:S(2)}, u32[]{:S(2)}) collective-permute-start(bf16[2,384,384]{2,1,0:T(8,128)(2,1)} %get-tuple-element.80), channel_id=1, source_target_pairs={{8,16},{16,8},{9,17},{17,9},{10,18},{18,10},{11,19},{19,11},{12,20... | collective-permute-start | bytes 1769480 | tf_op jit(solution)/shard_map/ppermute | solution.py:327
  151.7 3.6 %collective-permute-start.10 = (bf16[2,384,384]{2,1,0:T(8,128)(2,1)S(1)}, bf16[2,384,384]{2,1,0:T(8,128)(2,1)S(1)}, u32[]{:S(2)}, u32[]{:S(2)}) collective-permute-start(bf16[2,384,384]{2,1,0:T(8,128)(2,1)S(1)} %get-tuple-element.69), channel_id=1, source_target_pairs={{8,16},{16,8},{9,17},{17,9},{10,18},{18,10},{11,19},{19,11},{12,20... | collective-permute-start | bytes 1769480 | tf_op jit(solution)/shard_map/ppermute | solution.py:327
  156.3 0.9 collective-permute-done.22.far
  157.2 0.8 copy-done.30
  158.8 3.6 %finish.4 = (bf16[384,1536]{1,0:T(8,128)(2,1)}, bf16[384,1536]{1,0:T(8,128)(2,1)}, bf16[384,1536]{1,0:T(8,128)(2,1)}) custom-call(f32[384,384]{1,0:T(8,128)} %copy-done.11, bf16[384,384]{1,0:T(8,128)(2,1)} %copy-done.31, f32[2,384,384]{2,1,0:T(8,128)} %copy-done, bf16[2,384,384]{2,1,0:T(8,128)(2,1)} %collective-permute-done.26.near, ...), custom_call_target="tpu_custom_call" | custom-call | flops 1179648 | bytes 4423680 | tf_op jit(solution)/shard_map/finish/pallas_call | solution.py:236
  162.4 3.6 %finish.5 = (bf16[384,1536]{1,0:T(8,128)(2,1)}, bf16[384,1536]{1,0:T(8,128)(2,1)}, bf16[384,1536]{1,0:T(8,128)(2,1)}) custom-call(f32[384,384]{1,0:T(8,128)} %copy-done.9, bf16[384,384]{1,0:T(8,128)(2,1)} %copy-done.33, f32[2,384,384]{2,1,0:T(8,128)} %copy-done.2, ...), custom_call_target="tpu_custom_call", output_to_operand_aliasing={{0}: (5, {}), {1}: (6, {}), {2}: (7, {})} | custom-call | flops 1179648 | bytes 4423680 | tf_op jit(solution)/shard_map/finish/pallas_call | solution.py:236
  166.0 3.6 %finish.6 = (bf16[384,1536]{1,0:T(8,128)(2,1)}, bf16[384,1536]{1,0:T(8,128)(2,1)}, bf16[384,1536]{1,0:T(8,128)(2,1)}) custom-call(f32[384,384]{1,0:T(8,128)} %copy-done.8, bf16[384,384]{1,0:T(8,128)(2,1)} %copy-done.32, f32[2,384,384]{2,1,0:T(8,128)} %copy-done.1, ...), custom_call_target="tpu_custom_call", output_to_operand_aliasing={{0}: (5, {}), {1}: (6, {}), {2}: (7, {})} | custom-call | flops 1179648 | bytes 4423680 | tf_op jit(solution)/shard_map/finish/pallas_call | solution.py:236
  171.0 3.6 %finish.7 = (bf16[384,1536]{1,0:T(8,128)(2,1)}, bf16[384,1536]{1,0:T(8,128)(2,1)}, bf16[384,1536]{1,0:T(8,128)(2,1)}) custom-call(f32[384,384]{1,0:T(8,128)} %copy-done.10, bf16[384,384]{1,0:T(8,128)(2,1)} %copy-done.34, f32[2,384,384]{2,1,0:T(8,128)} %copy-done.3, ...), custom_call_target="tpu_custom_call", output_to_operand_aliasing={{0}: (5, {}), {1}: (6, {}), {2}: (7, {})} | custom-call | flops 1179648 | bytes 4423680 | tf_op jit(solution)/shard_map/finish/pallas_call | solution.py:236
  (103 shorter events, 10.0 us)
Async XLA Ops:
  0.6 26.7 %collective-permute-start = (bf16[384,1536]{1,0:T(8,128)(2,1)}, bf16[384,1536]{1,0:T(8,128)(2,1)}, u32[]{:S(2)}, u32[]{:S(2)}) collective-permute-start(bf16[384,1536]{1,0:T(8,128)(2,1)} %bitcast.15), channel_id=1, source_target_pairs={{0,8},{8,0},{16,24},{24,16},{1,9},{9,1},{17,25},{25,17},{2,10},{10... | collective-permute-start | bytes 3538952 | tf_op jit(solution)/shard_map/ppermute | solution.py:299
  1.4 26.1 %collective-permute-start.1 = (bf16[384,1536]{1,0:T(8,128)(2,1)}, bf16[384,1536]{1,0:T(8,128)(2,1)}, u32[]{:S(2)}, u32[]{:S(2)}) collective-permute-start(bf16[384,1536]{1,0:T(8,128)(2,1)} %bitcast.3.refs_3_.refs_4_), channel_id=1, source_target_pairs={{0,8},{8,0},{16,24},{24,16},{1,9},{9,1},{17,25},{25,17},{2,10},{10... | collective-permute-start | bytes 3538952 | tf_op jit(solution)/shard_map/ppermute | solution.py:299
  4.2 3.6 %copy-start.12 = (bf16[1,1,384,1536]{3,2,1,0:T(8,128)(2,1)S(1)}, bf16[1,1,384,1536]{3,2,1,0:T(8,128)(2,1)}, u32[]{:S(2)}) copy-start(bf16[1,1,384,1536]{3,2,1,0:T(8,128)(2,1)} %param.8) | copy-start | bytes 3538948
  6.6 15.2 %collective-permute-start.11 = (bf16[800,384]{1,0:T(8,128)(2,1)}, bf16[800,384]{1,0:T(8,128)(2,1)S(1)}, u32[]{:S(2)}, u32[]{:S(2)}) collective-permute-start(bf16[800,384]{1,0:T(8,128)(2,1)} %prep.6.refs_0_.refs_1_), channel_id=1, source_target_pairs={{0,1},{1,0},{2,3},{3,2},{4,5},{5,4},{6,7},{7,6},{8,9},{9,8},{10,11... | collective-permute-start | bytes 1843208 | tf_op jit(solution)/shard_map/ppermute | solution.py:309
  7.8 32.6 %collective-permute-start.5 = (bf16[384,1536]{1,0:T(8,128)(2,1)S(1)}, bf16[384,1536]{1,0:T(8,128)(2,1)}, u32[]{:S(2)}, u32[]{:S(2)}) collective-permute-start(bf16[384,1536]{1,0:T(8,128)(2,1)S(1)} %bitcast.16), channel_id=1, source_target_pairs={{8,16},{16,8},{9,17},{17,9},{10,18},{18,10},{11,19},{19,11},{12,20... | collective-permute-start | bytes 3538952 | tf_op jit(solution)/shard_map/ppermute | solution.py:300
  11.6 28.9 %collective-permute-start.6 = (bf16[384,1536]{1,0:T(8,128)(2,1)}, bf16[384,1536]{1,0:T(8,128)(2,1)}, u32[]{:S(2)}, u32[]{:S(2)}) collective-permute-start(bf16[384,1536]{1,0:T(8,128)(2,1)} %bitcast.3.refs_3_.refs_4_), channel_id=1, source_target_pairs={{8,16},{16,8},{9,17},{17,9},{10,18},{18,10},{11,19},{19,11},{12,20... | collective-permute-start | bytes 3538952 | tf_op jit(solution)/shard_map/ppermute | solution.py:300
  21.8 9.4 %copy-start.13 = (bf16[800,384]{1,0:T(8,128)(2,1)}, bf16[800,384]{1,0:T(8,128)(2,1)S(1)}, u32[]{:S(2)}) copy-start(bf16[800,384]{1,0:T(8,128)(2,1)S(1)} %collective-permute-done.11.refs_1_.refs_2_) | copy-start | bytes 1843204
  21.8 18.6 %collective-permute-start.23 = (bf16[800,384]{1,0:T(8,128)(2,1)S(1)}, bf16[800,384]{1,0:T(8,128)(2,1)}, u32[]{:S(2)}, u32[]{:S(2)}) collective-permute-start(bf16[800,384]{1,0:T(8,128)(2,1)S(1)} %collective-permute-done.11.refs_1_.refs_2_), channel_id=1, source_target_pairs={{0,2},{2,4},{4,6},{3,1},{5,3},{7,5},{8,10},{10,12},{12,14},{11,9},... | collective-permute-start | bytes 1843208 | tf_op jit(solution)/shard_map/ppermute | solution.py:310
  27.4 3.9 %copy-start.7 = (bf16[800,384]{1,0:T(8,128)(2,1)S(1)}, bf16[800,384]{1,0:T(8,128)(2,1)}, u32[]{:S(2)}) copy-start(bf16[800,384]{1,0:T(8,128)(2,1)} %prep.6.refs_0_.refs_1_) | copy-start | bytes 1843204
  27.4 32.7 %collective-permute-start.12 = (bf16[800,384]{1,0:T(8,128)(2,1)}, bf16[800,384]{1,0:T(8,128)(2,1)}, u32[]{:S(2)}, u32[]{:S(2)}) collective-permute-start(bf16[800,384]{1,0:T(8,128)(2,1)} %prep.7.refs_0_.refs_1_), channel_id=1, source_target_pairs={{0,1},{1,0},{2,3},{3,2},{4,5},{5,4},{6,7},{7,6},{8,9},{9,8},{10,11... | collective-permute-start | bytes 1843208 | tf_op jit(solution)/shard_map/ppermute | solution.py:309
  29.9 43.7 %collective-permute-start.2 = (bf16[800,384]{1,0:T(8,128)(2,1)}, bf16[800,384]{1,0:T(8,128)(2,1)S(1)}, u32[]{:S(2)}, u32[]{:S(2)}) collective-permute-start(bf16[800,384]{1,0:T(8,128)(2,1)} %prep.4.refs_0_.refs_1_), channel_id=1, source_target_pairs={{0,1},{1,0},{2,3},{3,2},{4,5},{5,4},{6,7},{7,6},{8,9},{9,8},{10,11... | collective-permute-start | bytes 1843208 | tf_op jit(solution)/shard_map/ppermute | solution.py:309
  40.4 1.1 copy-start.14
  41.5 21.0 %copy-start.6 = (bf16[800,384]{1,0:T(8,128)(2,1)S(1)}, bf16[800,384]{1,0:T(8,128)(2,1)}, u32[]{:S(2)}) copy-start(bf16[800,384]{1,0:T(8,128)(2,1)} %prep.7.refs_0_.refs_1_) | copy-start | bytes 1843204
  51.7 18.0 %copy-start = (f32[2,384,384]{2,1,0:T(8,128)}, f32[2,384,384]{2,1,0:T(8,128)S(1)}, u32[]{:S(2)}) copy-start(f32[2,384,384]{2,1,0:T(8,128)S(1)} %get-tuple-element.98.own_kv) | copy-start | bytes 3538948
  51.7 18.0 %copy-start.11 = (f32[384,384]{1,0:T(8,128)}, f32[384,384]{1,0:T(8,128)S(1)}, u32[]{:S(2)}) copy-start(f32[384,384]{1,0:T(8,128)S(1)} %get-tuple-element.95.own_q) | copy-start | bytes 1769476
  51.7 20.7 %collective-permute-start.24 = (bf16[384,384]{1,0:T(8,128)(2,1)S(1)}, bf16[384,384]{1,0:T(8,128)(2,1)S(1)}, u32[]{:S(2)}, u32[]{:S(2)}) collective-permute-start(bf16[384,384]{1,0:T(8,128)(2,1)S(1)} %get-tuple-element.97), channel_id=1, source_target_pairs={{2,0},{4,2},{6,4},{1,3},{3,5},{5,7},{10,8},{12,10},{14,12},{9,11},... | collective-permute-start | bytes 884744 | tf_op jit(solution)/shard_map/ppermute | solution.py:323
  54.6 87.3 %collective-permute-start.26 = (bf16[2,384,384]{2,1,0:T(8,128)(2,1)}, bf16[2,384,384]{2,1,0:T(8,128)(2,1)}, u32[]{:S(2)}, u32[]{:S(2)}) collective-permute-start(bf16[2,384,384]{2,1,0:T(8,128)(2,1)} %get-tuple-element.99), channel_id=1, source_target_pairs={{0,8},{8,0},{16,24},{24,16},{1,9},{9,1},{17,25},{25,17},{2,10},{10... | collective-permute-start | bytes 1769480 | tf_op jit(solution)/shard_map/ppermute | solution.py:326
  54.6 90.3 %collective-permute-start.27 = (bf16[2,384,384]{2,1,0:T(8,128)(2,1)}, bf16[2,384,384]{2,1,0:T(8,128)(2,1)}, u32[]{:S(2)}, u32[]{:S(2)}) collective-permute-start(bf16[2,384,384]{2,1,0:T(8,128)(2,1)} %get-tuple-element.100), channel_id=1, source_target_pairs={{8,16},{16,8},{9,17},{17,9},{10,18},{18,10},{11,19},{19,11},{12,20... | collective-permute-start | bytes 1769480 | tf_op jit(solution)/shard_map/ppermute | solution.py:327
  60.1 19.8 %collective-permute-start.13 = (bf16[800,384]{1,0:T(8,128)(2,1)}, bf16[800,384]{1,0:T(8,128)(2,1)}, u32[]{:S(2)}, u32[]{:S(2)}) collective-permute-start(bf16[800,384]{1,0:T(8,128)(2,1)} %collective-permute-done.12.refs_1_.refs_2_), channel_id=1, source_target_pairs={{0,2},{2,4},{4,6},{3,1},{5,3},{7,5},{8,10},{10,12},{12,14},{11,9},... | collective-permute-start | bytes 1843208 | tf_op jit(solution)/shard_map/ppermute | solution.py:310
  72.4 1.1 copy-start.17
  73.5 55.9 %collective-permute-start.25 = (bf16[384,384]{1,0:T(8,128)(2,1)}, bf16[384,384]{1,0:T(8,128)(2,1)S(1)}, u32[]{:S(2)}, u32[]{:S(2)}) collective-permute-start(bf16[384,384]{1,0:T(8,128)(2,1)} %multiply_convert_fusion), channel_id=1, source_target_pairs={{0,1},{1,0},{2,3},{3,2},{4,5},{5,4},{6,7},{7,6},{8,9},{9,8},{10,11... | collective-permute-start | bytes 884744 | tf_op jit(solution)/shard_map/ppermute | solution.py:325
  75.9 28.9 %collective-permute-start.18 = (bf16[800,384]{1,0:T(8,128)(2,1)S(1)}, bf16[800,384]{1,0:T(8,128)(2,1)S(1)}, u32[]{:S(2)}, u32[]{:S(2)}) collective-permute-start(bf16[800,384]{1,0:T(8,128)(2,1)S(1)} %collective-permute-done.2.refs_1_.refs_2_), channel_id=1, source_target_pairs={{0,2},{2,4},{4,6},{3,1},{5,3},{7,5},{8,10},{10,12},{12,14},{11,9},... | collective-permute-start | bytes 1843208 | tf_op jit(solution)/shard_map/ppermute | solution.py:310
  82.0 13.1 %copy-start.4 = (bf16[800,384]{1,0:T(8,128)(2,1)S(1)}, bf16[800,384]{1,0:T(8,128)(2,1)}, u32[]{:S(2)}) copy-start(bf16[800,384]{1,0:T(8,128)(2,1)} %prep.4.refs_0_.refs_1_) | copy-start | bytes 1843204
  93.1 9.3 %copy-start.1 = (f32[2,384,384]{2,1,0:T(8,128)}, f32[2,384,384]{2,1,0:T(8,128)S(1)}, u32[]{:S(2)}) copy-start(f32[2,384,384]{2,1,0:T(8,128)S(1)} %get-tuple-element.78.own_kv) | copy-start | bytes 3538948
  93.1 10.3 %copy-start.5 = (bf16[800,384]{1,0:T(8,128)(2,1)S(1)}, bf16[800,384]{1,0:T(8,128)(2,1)}, u32[]{:S(2)}) copy-start(bf16[800,384]{1,0:T(8,128)(2,1)} %prep.5.refs_0_.refs_1_) | copy-start | bytes 1843204
  93.1 10.3 %collective-permute-start.14 = (bf16[384,384]{1,0:T(8,128)(2,1)S(1)}, bf16[384,384]{1,0:T(8,128)(2,1)S(1)}, u32[]{:S(2)}, u32[]{:S(2)}) collective-permute-start(bf16[384,384]{1,0:T(8,128)(2,1)S(1)} %get-tuple-element.77), channel_id=1, source_target_pairs={{2,0},{4,2},{6,4},{1,3},{3,5},{5,7},{10,8},{12,10},{14,12},{9,11},... | collective-permute-start | bytes 884744 | tf_op jit(solution)/shard_map/ppermute | solution.py:323
  103.4 1.4 copy-start.19
  103.4 14.5 %collective-permute-start.3 = (bf16[800,384]{1,0:T(8,128)(2,1)S(1)}, bf16[800,384]{1,0:T(8,128)(2,1)S(1)}, u32[]{:S(2)}, u32[]{:S(2)}) collective-permute-start(bf16[800,384]{1,0:T(8,128)(2,1)S(1)} %copy-done.5), channel_id=1, source_target_pairs={{0,1},{1,0},{2,3},{3,2},{4,5},{5,4},{6,7},{7,6},{8,9},{9,8},{10,11... | collective-permute-start | bytes 1843208 | tf_op jit(solution)/shard_map/ppermute | solution.py:309
  114.5 13.1 %copy-start.2 = (f32[2,384,384]{2,1,0:T(8,128)}, f32[2,384,384]{2,1,0:T(8,128)S(1)}, u32[]{:S(2)}) copy-start(f32[2,384,384]{2,1,0:T(8,128)S(1)} %get-tuple-element.88.own_kv) | copy-start | bytes 3538948
  114.5 13.1 %copy-start.9 = (f32[384,384]{1,0:T(8,128)}, f32[384,384]{1,0:T(8,128)S(1)}, u32[]{:S(2)}) copy-start(f32[384,384]{1,0:T(8,128)S(1)} %get-tuple-element.85.own_q) | copy-start | bytes 1769476
  114.5 14.1 %collective-permute-start.19 = (bf16[384,384]{1,0:T(8,128)(2,1)S(1)}, bf16[384,384]{1,0:T(8,128)(2,1)S(1)}, u32[]{:S(2)}, u32[]{:S(2)}) collective-permute-start(bf16[384,384]{1,0:T(8,128)(2,1)S(1)} %get-tuple-element.87), channel_id=1, source_target_pairs={{2,0},{4,2},{6,4},{1,3},{3,5},{5,7},{10,8},{12,10},{14,12},{9,11},... | collective-permute-start | bytes 884744 | tf_op jit(solution)/shard_map/ppermute | solution.py:323
  117.9 11.6 %collective-permute-start.4 = (bf16[800,384]{1,0:T(8,128)(2,1)S(1)}, bf16[800,384]{1,0:T(8,128)(2,1)S(1)}, u32[]{:S(2)}, u32[]{:S(2)}) collective-permute-start(bf16[800,384]{1,0:T(8,128)(2,1)S(1)} %collective-permute-done.3.refs_1_.refs_2_), channel_id=1, source_target_pairs={{0,2},{2,4},{4,6},{3,1},{5,3},{7,5},{8,10},{10,12},{12,14},{11,9},... | collective-permute-start | bytes 1843208 | tf_op jit(solution)/shard_map/ppermute | solution.py:310
  128.6 1.7 copy-start.15
  128.7 21.0 %collective-permute-start.15 = (bf16[384,384]{1,0:T(8,128)(2,1)S(1)}, bf16[384,384]{1,0:T(8,128)(2,1)S(1)}, u32[]{:S(2)}, u32[]{:S(2)}) collective-permute-start(bf16[384,384]{1,0:T(8,128)(2,1)S(1)} %multiply_convert_fusion.2), channel_id=1, source_target_pairs={{0,1},{1,0},{2,3},{3,2},{4,5},{5,4},{6,7},{7,6},{8,9},{9,8},{10,11... | collective-permute-start | bytes 884744 | tf_op jit(solution)/shard_map/ppermute | solution.py:325
  129.4 10.6 %copy-start.31 = (bf16[384,384]{1,0:T(8,128)(2,1)}, bf16[384,384]{1,0:T(8,128)(2,1)S(1)}, u32[]{:S(2)}) copy-start(bf16[384,384]{1,0:T(8,128)(2,1)S(1)} %collective-permute-done.25.back_q) | copy-start | bytes 884740
  129.4 22.3 %collective-permute-start.21 = (bf16[2,384,384]{2,1,0:T(8,128)(2,1)S(1)}, bf16[2,384,384]{2,1,0:T(8,128)(2,1)S(1)}, u32[]{:S(2)}, u32[]{:S(2)}) collective-permute-start(bf16[2,384,384]{2,1,0:T(8,128)(2,1)S(1)} %get-tuple-element.89), channel_id=1, source_target_pairs={{0,8},{8,0},{16,24},{24,16},{1,9},{9,1},{17,25},{25,17},{2,10},{10... | collective-permute-start | bytes 1769480 | tf_op jit(solution)/shard_map/ppermute | solution.py:326
  129.5 20.3 %collective-permute-start.20 = (bf16[384,384]{1,0:T(8,128)(2,1)S(1)}, bf16[384,384]{1,0:T(8,128)(2,1)S(1)}, u32[]{:S(2)}, u32[]{:S(2)}) collective-permute-start(bf16[384,384]{1,0:T(8,128)(2,1)S(1)} %multiply_convert_fusion.1), channel_id=1, source_target_pairs={{0,1},{1,0},{2,3},{3,2},{4,5},{5,4},{6,7},{7,6},{8,9},{9,8},{10,11... | collective-permute-start | bytes 884744 | tf_op jit(solution)/shard_map/ppermute | solution.py:325
  141.9 13.5 %collective-permute-start.7 = (bf16[384,384]{1,0:T(8,128)(2,1)S(1)}, bf16[384,384]{1,0:T(8,128)(2,1)S(1)}, u32[]{:S(2)}, u32[]{:S(2)}) collective-permute-start(bf16[384,384]{1,0:T(8,128)(2,1)S(1)} %get-tuple-element.66), channel_id=1, source_target_pairs={{2,0},{4,2},{6,4},{1,3},{3,5},{5,7},{10,8},{12,10},{14,12},{9,11},... | collective-permute-start | bytes 884744 | tf_op jit(solution)/shard_map/ppermute | solution.py:323
  144.9 12.3 %collective-permute-start.22 = (bf16[2,384,384]{2,1,0:T(8,128)(2,1)S(1)}, bf16[2,384,384]{2,1,0:T(8,128)(2,1)S(1)}, u32[]{:S(2)}, u32[]{:S(2)}) collective-permute-start(bf16[2,384,384]{2,1,0:T(8,128)(2,1)S(1)} %get-tuple-element.90), channel_id=1, source_target_pairs={{8,16},{16,8},{9,17},{17,9},{10,18},{18,10},{11,19},{19,11},{12,20... | collective-permute-start | bytes 1769480 | tf_op jit(solution)/shard_map/ppermute | solution.py:327
  149.7 9.2 %copy-start.32 = (bf16[384,384]{1,0:T(8,128)(2,1)}, bf16[384,384]{1,0:T(8,128)(2,1)S(1)}, u32[]{:S(2)}) copy-start(bf16[384,384]{1,0:T(8,128)(2,1)S(1)} %collective-permute-done.15.back_q) | copy-start | bytes 884740
  149.7 16.3 %collective-permute-start.16 = (bf16[2,384,384]{2,1,0:T(8,128)(2,1)}, bf16[2,384,384]{2,1,0:T(8,128)(2,1)}, u32[]{:S(2)}, u32[]{:S(2)}) collective-permute-start(bf16[2,384,384]{2,1,0:T(8,128)(2,1)} %get-tuple-element.79), channel_id=1, source_target_pairs={{0,8},{8,0},{16,24},{24,16},{1,9},{9,1},{17,25},{25,17},{2,10},{10... | collective-permute-start | bytes 1769480 | tf_op jit(solution)/shard_map/ppermute | solution.py:326
  149.8 9.1 %copy-start.33 = (bf16[384,384]{1,0:T(8,128)(2,1)}, bf16[384,384]{1,0:T(8,128)(2,1)S(1)}, u32[]{:S(2)}) copy-start(bf16[384,384]{1,0:T(8,128)(2,1)S(1)} %collective-permute-done.20.back_q) | copy-start | bytes 884740
  149.8 16.2 %collective-permute-start.17 = (bf16[2,384,384]{2,1,0:T(8,128)(2,1)}, bf16[2,384,384]{2,1,0:T(8,128)(2,1)}, u32[]{:S(2)}, u32[]{:S(2)}) collective-permute-start(bf16[2,384,384]{2,1,0:T(8,128)(2,1)} %get-tuple-element.80), channel_id=1, source_target_pairs={{8,16},{16,8},{9,17},{17,9},{10,18},{18,10},{11,19},{19,11},{12,20... | collective-permute-start | bytes 1769480 | tf_op jit(solution)/shard_map/ppermute | solution.py:327
  151.7 10.7 %copy-start.27 = (bf16[2,384,384]{2,1,0:T(8,128)(2,1)}, bf16[2,384,384]{2,1,0:T(8,128)(2,1)S(1)}, u32[]{:S(2)}) copy-start(bf16[2,384,384]{2,1,0:T(8,128)(2,1)S(1)} %collective-permute-done.21.near) | copy-start | bytes 1769476
  151.7 18.1 %collective-permute-start.10 = (bf16[2,384,384]{2,1,0:T(8,128)(2,1)S(1)}, bf16[2,384,384]{2,1,0:T(8,128)(2,1)S(1)}, u32[]{:S(2)}, u32[]{:S(2)}) collective-permute-start(bf16[2,384,384]{2,1,0:T(8,128)(2,1)S(1)} %get-tuple-element.69), channel_id=1, source_target_pairs={{8,16},{16,8},{9,17},{17,9},{10,18},{18,10},{11,19},{19,11},{12,20... | collective-permute-start | bytes 1769480 | tf_op jit(solution)/shard_map/ppermute | solution.py:327
  155.4 14.5 %collective-permute-start.9 = (bf16[2,384,384]{2,1,0:T(8,128)(2,1)S(1)}, bf16[2,384,384]{2,1,0:T(8,128)(2,1)S(1)}, u32[]{:S(2)}, u32[]{:S(2)}) collective-permute-start(bf16[2,384,384]{2,1,0:T(8,128)(2,1)S(1)} %get-tuple-element.68), channel_id=1, source_target_pairs={{0,8},{8,0},{16,24},{24,16},{1,9},{9,1},{17,25},{25,17},{2,10},{10... | collective-permute-start | bytes 1769480 | tf_op jit(solution)/shard_map/ppermute | solution.py:326
  158.1 11.8 %collective-permute-start.8 = (bf16[384,384]{1,0:T(8,128)(2,1)}, bf16[384,384]{1,0:T(8,128)(2,1)S(1)}, u32[]{:S(2)}, u32[]{:S(2)}) collective-permute-start(bf16[384,384]{1,0:T(8,128)(2,1)} %multiply_convert_fusion.3), channel_id=1, source_target_pairs={{0,1},{1,0},{2,3},{3,2},{4,5},{5,4},{6,7},{7,6},{8,9},{9,8},{10,11... | collective-permute-start | bytes 884744 | tf_op jit(solution)/shard_map/ppermute | solution.py:325
  169.9 1.1 copy-start.34
  (15 other events, 14.2 us)

commit v3 on v2

v3 whole, which is shorter than its diff:
```python
import functools
import math

import jax
import jax.numpy as jnp
from jax import lax
from jax.experimental import pallas as pl
from jax.experimental.pallas import tpu as pltpu
from jax.sharding import PartitionSpec as P

F32 = jnp.float32
BF16 = jnp.bfloat16
LOG2E = math.log2(math.e)
FAR_AWAY = 1e30

EVEN_ROW, ODD_ROW, OUTER = (0, 1, 2)
EVEN, ODD, FAR = (0, 1, 2)
BOTH = (EVEN_ROW, ODD_ROW)
CHUNKS = (2, 3, 4, 3)
STAGES = (
    ((EVEN, BOTH), (ODD, BOTH)),
    ((EVEN, (OUTER,)), (ODD, (OUTER,)), (FAR, (EVEN_ROW, ODD_ROW, OUTER))),
)
EXTRA = 32
VMEM_LIMIT = 16 * 1024 * 1024


def dot(a, b, dims):
    return lax.dot_general(a, b, (dims, ((), ())), preferred_element_type=F32)


def three_terms(row):
    terms = []
    for _ in range(3):
        term = row.astype(BF16).astype(F32)
        terms.append(term)
        row = row - term
    return terms


def fold(row):
    lanes = 128
    return [row[:, i : i + lanes] for i in range(0, row.shape[1], lanes)]


def prep_kernel(first, count, q_ref, g_ref, o_ref, lse_ref, flag_ref, out):
    tile = q_ref.shape[0]
    width = q_ref.shape[1] // count
    out[0:tile, :] = q_ref[...]
    out[tile : 2 * tile, :] = g_ref[...]
    ones = jnp.ones((8, width), BF16)
    for h in range(count):
        cols = slice(h * width, (h + 1) * width)
        prod = g_ref[:, cols].astype(F32) * o_ref[:, cols].astype(F32)
        high = prod.astype(BF16)
        low = (prod - high.astype(F32)).astype(BF16)
        delta = dot(ones, high, ((1,), (1,))) + dot(ones, low, ((1,), (1,)))
        rows = []
        for row in (lse_ref[first + h : first + h + 1, :] * LOG2E, delta[0:1, :]):
            for term in three_terms(row):
                rows += fold(term)
        rows.append(flag_ref[...])
        rows.append(jnp.zeros((EXTRA - len(rows), width), F32))
        out[2 * tile : 2 * tile + EXTRA, cols] = jnp.concatenate(rows, axis=0).astype(BF16)


def prep(first, count, head_width, q, g, o, lse, flags):
    tile, full = q.shape
    wide = count * head_width
    offset = first * head_width
    cols = pl.BlockSpec((pl.Element(tile), pl.Element(wide)), lambda i: (0, offset))
    return pl.pallas_call(
        functools.partial(prep_kernel, first, count),
        grid=(1,),
        in_specs=[
            cols,
            cols,
            cols,
            pl.BlockSpec(lse.shape, lambda i: (0, 0)),
            pl.BlockSpec(flags.shape, lambda i: (0, 0)),
        ],
        out_specs=pl.BlockSpec((2 * tile + EXTRA, wide), lambda i: (0, 0)),
        out_shape=jax.ShapeDtypeStruct((2 * tile + EXTRA, wide), BF16),
        cost_estimate=pl.CostEstimate(
            flops=2 * tile * wide, bytes_accessed=10 * tile * wide, transcendentals=0
        ),
        name="prep",
    )(q, g, o, lse, flags)


def row_stats(message, parity):
    tile = (message.shape[0] - EXTRA) // 2
    extra = message[2 * tile : 2 * tile + EXTRA, :].astype(F32)
    parts = tile // 128
    rows = []
    for base in (0, 3 * parts):
        pieces = []
        for p in range(parts):
            a, b, c = (extra[base + i * parts + p : base + i * parts + p + 1] for i in range(3))
            pieces.append(a + b + c)
        rows.append(jnp.concatenate(pieces, axis=1))
    flags = extra[6 * parts : 6 * parts + 1]
    lanes = [flags[:, i : i + 1] for i in range(9)]
    if parity is None:
        chosen = lanes[6:9]
    else:
        chosen = [jnp.where(parity == 0, lanes[i], lanes[3 + i]) for i in range(3)]
    return (rows[0], rows[1], chosen)


def stage_kernel(work, names, factor, place_ref, *refs):
    env = dict(zip(names, refs))
    has_far, parity = (place_ref[0], place_ref[1])
    used = sorted({j for _, js in work for j in js})
    messages = {j: env["outer"] if j == OUTER else env["pair"].at[j] for j in used}
    stats = {j: row_stats(messages[j], None if j == OUTER else parity) for j in used}
    tile = (messages[used[0]].shape[0] - EXTRA) // 2
    sums = {j: env["sum%d" % j] for j in used}
    started = set()

    def before(j):
        if j == OUTER or "acc_pair" not in env:
            return None
        return env["acc_pair"][j]

    def add_q(j, term):
        if j in started:
            sums[j][...] += term
        else:
            earlier = before(j)
            sums[j][...] = term if earlier is None else earlier + term
        started.add(j)

    def key_frame(slot, js):
        key, value = (
            (env["far_k"][...], env["far_v"][...])
            if slot == FAR
            else (env["k"][slot], env["v"][slot])
        )
        dk, dv = (None, None)
        if slot != FAR and "acc_keys" in env:
            dk, dv = (env["acc_keys"][slot, 0], env["acc_keys"][slot, 1])
        for j in js:
            qj = messages[j][0:tile, :]
            gj = messages[j][tile : 2 * tile, :]
            shift, delta, flags = stats[j]
            shift = jnp.where(flags[slot] > 0, shift, FAR_AWAY)
            scores = dot(key, qj, ((1,), (1,)))
            weights = jnp.exp2(scores * (factor * LOG2E) - shift)
            grad_prob = dot(value, gj, ((1,), (1,)))
            grad_score = (weights * (grad_prob - delta)).astype(BF16)
            term_v = dot(weights.astype(BF16), gj, ((1,), (0,)))
            term_k = dot(grad_score, qj, ((1,), (0,))) * factor
            add_q(j, dot(grad_score, key, ((0,), (0,))) * factor)
            dv = term_v if dv is None else dv + term_v
            dk = term_k if dk is None else dk + term_k
        out = env["out_far"] if slot == FAR else env["out_keys"].at[slot]
        out[0] = dk.astype(out.dtype)
        out[1] = dv.astype(out.dtype)

    for slot, js in work:
        if slot != FAR:
            key_frame(slot, js)
    for slot, js in work:
        if slot == FAR:
            fresh = [j for j in js if j not in started]
            pl.when(has_far > 0)(functools.partial(key_frame, slot, js))

            @pl.when(has_far == 0)
            def _():
                out = env["out_far"]
                out[...] = jnp.zeros_like(out)
                for j in fresh:
                    earlier = before(j)
                    sums[j][...] = jnp.zeros_like(sums[j]) if earlier is None else earlier

    for j in used:
        out = env["out_outer"] if j == OUTER else env["out_pair"].at[j]
        out[...] = sums[j][...].astype(out.dtype)


def run_stage(work, final, first, count, head_width, place, operands, sums):
    rows, wide = operands["pair"].shape[1:]
    tile = (rows - EXTRA) // 2
    used = sorted({j for _, js in work for j in js})
    slots = [slot for slot, _ in work]
    specs = {
        "pair": pl.BlockSpec((2, rows, head_width), lambda h, *_: (0, 0, h)),
        "outer": pl.BlockSpec((rows, head_width), lambda h, *_: (0, h)),
        "k": pl.BlockSpec((2, tile, head_width), lambda h, *_: (0, 0, h + first)),
        "far_k": pl.BlockSpec((tile, head_width), lambda h, *_: (0, h + first)),
    }
    specs.update(v=specs["k"], far_v=specs["far_k"])
    sum_specs = {
        "pair": pl.BlockSpec((2, tile, head_width), lambda h, *_: (0, 0, h)),
        "outer": pl.BlockSpec((tile, head_width), lambda h, *_: (0, h)),
        "keys": pl.BlockSpec((2, 2, tile, head_width), lambda h, *_: (0, 0, 0, h)),
        "far": pl.BlockSpec((2, tile, head_width), lambda h, *_: (0, 0, h)),
    }
    shapes = {
        "pair": (2, tile, wide),
        "outer": (tile, wide),
        "keys": (2, 2, tile, wide),
        "far": (2, tile, wide),
    }
    names = []
    if set(used) & set(BOTH):
        names.append("pair")
    if OUTER in used:
        names.append("outer")
    if EVEN in slots or ODD in slots:
        names += ["k", "v"]
    if FAR in slots:
        names += ["far_k", "far_v"]
    args = [operands[name] for name in names]
    in_specs = [specs[name] for name in names]
    touched = [name for name in ("pair", "outer") if name in names]
    touched += ["keys"] if "k" in names else []
    touched += ["far"] if "far_k" in names else []
    for name in touched:
        if name in sums:
            names.append("acc_" + name)
            args.append(sums[name])
            in_specs.append(sum_specs[name])
    names += ["out_" + name for name in touched]
    names += ["sum%d" % j for j in used]
    pairs = count * sum(len(js) for _, js in work)
    results = pl.pallas_call(
        functools.partial(stage_kernel, work, names, head_width**-0.5),
        grid_spec=pltpu.PrefetchScalarGridSpec(
            num_scalar_prefetch=1,
            grid=(count,),
            in_specs=in_specs,
            out_specs=[sum_specs[name] for name in touched],
            scratch_shapes=[pltpu.VMEM((tile, head_width), F32)] * len(used),
        ),
        out_shape=[
            jax.ShapeDtypeStruct(shapes[name], BF16 if name in final else F32)
            for name in touched
        ],
        compiler_params=pltpu.CompilerParams(vmem_limit_bytes=VMEM_LIMIT),
        cost_estimate=pl.CostEstimate(
            flops=20 * pairs * tile * tile * head_width,
            bytes_accessed=40 * tile * wide,
            transcendentals=pairs * tile * tile,
        ),
        name="pairs",
    )(place, *args)
    return {**sums, **dict(zip(touched, results))}


def finish_kernel(q, keys, far, *rest):
    out_q, out_k, out_v = rest[-3:]
    out_q[...] = q[...]
    sums = keys[...].astype(F32) + far[...].astype(F32)
    out_k[...] = sums[0].astype(BF16)
    out_v[...] = sums[1].astype(BF16)


def finish(first, count, head_width, full, parts, so_far):
    tile = parts[0].shape[0]
    one = pl.BlockSpec((tile, head_width), lambda h: (0, h))
    two = pl.BlockSpec((2, tile, head_width), lambda h: (0, 0, h))
    cols = pl.BlockSpec((tile, head_width), lambda h: (0, h + first))
    kept = [] if so_far is None else list(so_far)
    return pl.pallas_call(
        finish_kernel,
        grid=(count,),
        in_specs=[one, two, two] + [pl.BlockSpec(memory_space=pl.ANY)] * len(kept),
        out_specs=[cols] * 3,
        out_shape=[jax.ShapeDtypeStruct((tile, full), BF16)] * 3,
        input_output_aliases={3 + i: i for i in range(len(kept))},
        cost_estimate=pl.CostEstimate(
            flops=4 * tile * count * head_width,
            bytes_accessed=16 * tile * count * head_width,
            transcendentals=0,
        ),
        name="finish",
    )(*parts, *kept)


def pair_flags(window_mask, lanes):
    mask = window_mask.reshape(9)
    frames, rows = (lax.axis_size("tm"), lax.axis_size("space"))
    frame, row = (lax.axis_index("tm"), lax.axis_index("space"))
    row_odd, frame_odd = (lax.rem(row, 2), lax.rem(frame, 2))
    lane = jnp.arange(9, dtype=jnp.int32)
    role, slot = (lane // 3, lane % 3)
    row_off = jnp.where(role == OUTER, 2 * row_odd - 1, role - row_odd)
    frame_off = jnp.where(slot == FAR, 2 * frame_odd - 1, slot - frame_odd)
    inside = (
        (row + row_off >= 0)
        & (row + row_off < rows)
        & (frame + frame_off >= 0)
        & (frame + frame_off < frames)
    )
    index = 3 * (frame_off + 1) + row_off + 1
    picked = jnp.sum(jnp.where(index[:, None] == lane[None, :], mask[None, :], 0), axis=1)
    flags = (inside & ((picked > 0) | (index == 4))).astype(F32)
    return jnp.pad(flags, (0, lanes - 9)).reshape(1, lanes)


def after(value, *earlier):
    return lax.optimization_barrier((value, *earlier))[0]


def per_device(queries, keys, values, outputs, out_grads, log_sums, window_mask):
    tile, full = queries.shape[2:]
    heads = log_sums.shape[2]
    width = full // heads
    frames, rows = (lax.axis_size("tm"), lax.axis_size("space"))
    q, k, v, o, g = (a.reshape(tile, full) for a in (queries, keys, values, outputs, out_grads))
    row_pairs = [[i, i + 1] for i in range(0, rows, 2)]
    frame_pairs = [[i, i + 1] for i in range(0, frames, 2)]
    onward = [(i, i + 2) for i in range(0, rows - 2, 2)]
    onward += [(i, i - 2) for i in range(3, rows, 2)]
    homeward = [(b, a) for a, b in onward]
    far_pairs = [(i, i + 1) for i in range(1, frames - 1, 2)]
    far_pairs += [(b, a) for a, b in far_pairs]

    frame, row = (lax.axis_index("tm"), lax.axis_index("space"))
    far_frame = frame - 1 + 2 * lax.rem(frame, 2)
    has_far = ((far_frame >= 0) & (far_frame < frames)).astype(jnp.int32)
    parity = lax.rem(row, 2)
    place = jnp.stack([has_far, parity])

    firsts = [sum(CHUNKS[:c]) for c in range(len(CHUNKS))]
    flags = pair_flags(window_mask, width)
    lse = log_sums.reshape(heads, tile)
    pair_k, pair_v = (
        lax.all_gather(a, "tm", axis_index_groups=frame_pairs) for a in (k, v)
    )
    far_k, far_v = (lax.ppermute(a, "tm", far_pairs) for a in (k, v))
    pairs, outers = ([], [])
    for c, count in enumerate(CHUNKS):
        source = q
        if c >= 2:
            source = after(q, pairs[c - 2])
        message = prep(firsts[c], count, width, source, g, o, lse, flags)
        pairs.append(lax.all_gather(message, "space", axis_index_groups=row_pairs))
        theirs = lax.dynamic_index_in_dim(pairs[c], 1 - parity, 0, False)
        outers.append(lax.ppermute(theirs, "space", onward))

    out = None
    for c, count in enumerate(CHUNKS):
        operands = {
            "pair": pairs[c],
            "outer": outers[c],
            "k": pair_k,
            "v": pair_v,
            "far_k": far_k,
            "far_v": far_v,
        }
        sums = {}
        for step, work in enumerate(STAGES):
            final = ("outer", "keys", "far") if step + 1 == len(STAGES) else ()
            sums = run_stage(work, final, firsts[c], count, width, place, operands, sums)
        home = lax.ppermute(sums["outer"], "space", homeward)
        theirs = jnp.arange(2).reshape(2, 1, 1) == 1 - parity
        total = sums["pair"] + jnp.where(theirs, home.astype(F32)[None], 0.0)
        back_q = lax.psum_scatter(
            total.astype(BF16), "space", axis_index_groups=row_pairs
        )
        back_keys = lax.psum_scatter(sums["keys"], "tm", axis_index_groups=frame_pairs)
        back_far = lax.ppermute(sums["far"], "tm", far_pairs)
        out = finish(firsts[c], count, width, full, (back_q, back_keys, back_far), out)
    return tuple(a.reshape(queries.shape) for a in out)


def solution(mesh):
    tile = P("tm", "space", None, None)
    return jax.shard_map(
        per_device,
        mesh=mesh,
        in_specs=(tile,) * 6 + (P("tm", "space", None),),
        out_specs=(tile,) * 3,
        check_vma=False,
    )
```

time: 176 us -> 276 us (1.57)
  waiting for transfers between devices: 9.53 us -> 75.3 us
  local copies, waits for them, and re-layouts: 16.1 us -> 35.9 us
  between operations: 1.17 us -> 14.4 us
  starting transfers between devices: 52.2 us -> 42.7 us
  blocking collectives: 0 us -> 9 us
  other arithmetic: 3.27 us -> 6.21 us
    all_gather x0 -> x5, waiting for transfers between devices: none -> 24.2 us  [the longest x3 23.1 us: per_device(): pairs.append(lax.all_gather(message, 'space', axis_index_groups=row_pairs))]
    ppermute x28 -> x14, waiting for transfers between devices: 9.53 us -> 29.9 us  [the longest x4 19 us: per_device(): back_far = lax.ppermute(sums['far'], 'tm', far_pairs)]
    reduce_scatter x0 -> x8, waiting for transfers between devices: none -> 17.1 us  [the longest x4 11.8 us: per_device(): lax.psum_scatter(sums['keys'], 'tm', axis_index_groups=frame_pairs)]
    unnamed x71 -> x73, local copies, waits for them, and re-layouts: 16.1 us -> 30.5 us
    ppermute x28 -> x14, starting transfers between devices: 52.2 us -> 42.2 us  [the longest x4 14.6 us: per_device(): back_far = lax.ppermute(sums['far'], 'tm', far_pairs)]
    all_gather x0 -> x1, blocking collectives: none -> 9 us  [per_device(): pairs.append(lax.all_gather(message, 'space', axis_index_groups=row_pairs))]
    squeeze x0 -> x4, local copies, waits for them, and re-layouts: none -> 5.43 us  [per_device(): theirs = lax.dynamic_index_in_dim(pairs[c], 1 - parity, 0, False)]
    unnamed x0 -> x13, waiting for transfers between devices: none -> 4.07 us
  transfers between devices with their start and end apart: 28 -> 27, of which waited for: 3 -> 8; matrix products, arithmetic and copies ran while one was open for 3% -> 4% of each run, Pallas kernels for 51% -> 31%
where the time goes in v3:
time: 276 us; the launch traced here: 274 us
  Pallas kernels  90.1 us (33%)
  waiting for transfers between devices  75.3 us (27%)
  starting transfers between devices  42.7 us (15%)
  local copies, waits for them, and re-layouts  35.9 us (13%)
  between operations  14.4 us (5%)
  blocking collectives  9 us (3%)
  other arithmetic  6.21 us (2%)
    pallas_call x8, Pallas kernels, run_stage(): pl.pallas_call(functools.partial(stage_kernel, work, names, head_width **...  68.7 us
    unnamed x73, local copies, waits for them, and re-layouts  30.5 us
    all_gather x3, waiting for transfers between devices, per_device(): pairs.append(lax.all_gather(message, 'space', axis_index_groups=row_pairs))  23.1 us
    ppermute x4, waiting for transfers between devices, per_device(): back_far = lax.ppermute(sums['far'], 'tm', far_pairs)  19 us
    ppermute x4, starting transfers between devices, per_device(): back_far = lax.ppermute(sums['far'], 'tm', far_pairs)  14.6 us
    ppermute x4, starting transfers between devices, per_device(): outers.append(lax.ppermute(theirs, 'space', onward))  12.7 us
    pallas_call x4, Pallas kernels, finish(): pl.pallas_call(finish_kernel, grid=(count,), in_specs=[one, two, two] + [...  11.9 us
    reduce_scatter x4, waiting for transfers between devices, per_device(): lax.psum_scatter(sums['keys'], 'tm', axis_index_groups=frame_pairs)  11.8 us
  transfers between devices with their start and end apart: 27, of which 8 were waited for; matrix products, arithmetic and copies ran while one was open for 4% of the time, Pallas kernels for 31%

profile of v3, /device:TPU:9, one launch (start us, length us, event | category | flops | bytes accessed | tf_op | source)
XLA Modules:
  0.0 273.7 jit_solution(8757574426501613552)
XLA Ops:
  10.0 2.3 prep.4
  13.9 23.1 %all-gather.12.cloned.1.call-done = bf16[1600,384]{1,0:T(8,128)(2,1)} async-done(((bf16[800,384]{1,0:T(8,128)(2,1)}), bf16[1600,384]{1,0:T(8,128)(2,1)}) %all-gather.12.cloned.1.call-update) | async-done | bytes 1228816 | tf_op jit(solution)/shard_map/all_gather | solution.py:340
  37.0 2.4 prep.5
  39.4 3.7 %collective-permute-start.1 = (bf16[384,1536]{1,0:T(8,128)(2,1)}, bf16[384,1536]{1,0:T(8,128)(2,1)S(1)}, u32[]{:S(2)}, u32[]{:S(2)}) collective-permute-start(bf16[384,1536]{1,0:T(8,128)(2,1)} %bitcast.12), channel_id=1, source_target_pairs={{8,16},{16,8},{9,17},{17,9},{10,18},{18,10},{11,19},{19,11},{12,20... | collective-permute-start | bytes 3538952 | tf_op jit(solution)/shard_map/ppermute | solution.py:333
  43.1 1.9 collective-permute-start.2
  45.0 2.3 prep.6
  47.3 9.0 %all-gather.4 = bf16[1600,256]{1,0:T(8,128)(2,1)S(1)} all-gather(bf16[800,256]{1,0:T(8,128)(2,1)} %prep.6), channel_id=6, replica_groups={{0,1},{2,3},{4,5},{6,7},{8,9},{10,11},{12,13},{14,15},{16,17},{18,19},{..., dimensions={0}, use_global_device_ids=true | all-gather | bytes 1228800 | tf_op jit(solution)/shard_map/all_gather | solution.py:340
  56.3 2.6 prep.7
  59.7 3.1 %collective-permute-start.11 = (bf16[800,256]{1,0:T(8,128)(2,1)}, bf16[800,256]{1,0:T(8,128)(2,1)}, u32[]{:S(2)}, u32[]{:S(2)}) collective-permute-start(bf16[800,256]{1,0:T(8,128)(2,1)} %dynamic-slice_bitcast_fusion.3), channel_id=1, source_target_pairs={{0,2},{2,4},{4,6},{3,1},{5,3},{7,5},{8,10},{10,12},{12,14},{11,9},... | collective-permute-start | bytes 1228808 | tf_op jit(solution)/shard_map/ppermute | solution.py:342
  64.0 1.7 copy-done.4
  65.6 1.7 copy-done.11
  67.3 4.8 %pairs.14 = (f32[2,384,256]{2,1,0:T(8,128)S(1)}, f32[2,2,384,256]{3,2,1,0:T(8,128)S(1)}) custom-call(s32[2]{0:T(128)S(1)} %pad_add_fusion.place_ref, bf16[2,800,256]{2,1,0:T(8,128)(2,1)S(1)} %bitcast.39, bf16[2,384,1536]{2,1,0:T(8,128)(2,1)S(1)} %bitcast.50, bf16[2,384,1536]{2,1,0:T(8,128)(2,1)S(1)} %bitcast.58), custom_call_target="tpu_custom_call" | custom-call | flops 3019898880 | bytes 3932160 | tf_op jit(solution)/shard_map/pairs/pallas_call | solution.py:228
  74.5 7.4 %pairs.15 = (f32[2,384,256]{2,1,0:T(8,128)S(1)}, bf16[384,256]{1,0:T(8,128)(2,1)S(1)}, bf16[2,2,384,256]{3,2,1,0:T(8,128)(2,1)}, bf16[2,384,256]{2,1,0:T(8,128)(2,1)S(1)}) custom-call(s32[2]{0:T(128)S(1)} %pad_add_fusion.place_ref, bf16[2,800,256]{2,1,0:T(8,128)(2,1)S(1)} %bitcast.40, bf16[800,256]{1,0:T(8,128)(2,1)} %collective-permute-done.11.refs_1_, ...), custom_call_target="tpu_custom_call" | custom-call | flops 3774873600 | bytes 3932160 | tf_op jit(solution)/shard_map/pairs/pallas_call | solution.py:228
  82.7 1.9 collective-permute-start.12
  85.6 3.3 %collective-permute-start.8 = (bf16[800,384]{1,0:T(8,128)(2,1)}, bf16[800,384]{1,0:T(8,128)(2,1)S(1)}, u32[]{:S(2)}, u32[]{:S(2)}) collective-permute-start(bf16[800,384]{1,0:T(8,128)(2,1)} %dynamic-slice_bitcast_fusion.1), channel_id=1, source_target_pairs={{0,2},{2,4},{4,6},{3,1},{5,3},{7,5},{8,10},{10,12},{12,14},{11,9},... | collective-permute-start | bytes 1843208 | tf_op jit(solution)/shard_map/ppermute | solution.py:342
  90.5 1.7 copy-done.6
  92.1 1.7 copy-done.12
  93.8 6.9 %pairs.12 = (f32[2,384,384]{2,1,0:T(8,128)S(1)}, f32[2,2,384,384]{3,2,1,0:T(8,128)S(1)}) custom-call(s32[2]{0:T(128)S(1)} %pad_add_fusion.place_ref, bf16[2,800,384]{2,1,0:T(8,128)(2,1)S(1)} %bitcast.45, bf16[2,384,1536]{2,1,0:T(8,128)(2,1)S(1)} %bitcast.52, bf16[2,384,1536]{2,1,0:T(8,128)(2,1)S(1)} %bitcast.60), custom_call_target="tpu_custom_call" | custom-call | flops 4529848320 | bytes 5898240 | tf_op jit(solution)/shard_map/pairs/pallas_call | solution.py:228
  102.1 2.4 dynamic-slice_bitcast_fusion.2
  104.5 3.3 %collective-permute-start = (bf16[800,384]{1,0:T(8,128)(2,1)}, bf16[800,384]{1,0:T(8,128)(2,1)}, u32[]{:S(2)}, u32[]{:S(2)}) collective-permute-start(bf16[800,384]{1,0:T(8,128)(2,1)} %dynamic-slice_bitcast_fusion.2), channel_id=1, source_target_pairs={{0,2},{2,4},{4,6},{3,1},{5,3},{7,5},{8,10},{10,12},{12,14},{11,9},... | collective-permute-start | bytes 1843208 | tf_op jit(solution)/shard_map/ppermute | solution.py:342
  107.8 1.7 copy-done.7
  109.5 1.7 copy-done.13
  112.4 1.7 copy-done.31
  115.4 9.9 %pairs.13 = (f32[2,384,384]{2,1,0:T(8,128)S(1)}, bf16[384,384]{1,0:T(8,128)(2,1)S(1)}, bf16[2,2,384,384]{3,2,1,0:T(8,128)(2,1)}, bf16[2,384,384]{2,1,0:T(8,128)(2,1)S(1)}) custom-call(s32[2]{0:T(128)S(1)} %pad_add_fusion.place_ref, bf16[2,800,384]{2,1,0:T(8,128)(2,1)S(1)} %bitcast.46, bf16[800,384]{1,0:T(8,128)(2,1)S(1)} %collective-permute-done.8.refs_1_, ...), custom_call_target="tpu_custom_call" | custom-call | flops 5662310400 | bytes 5898240 | tf_op jit(solution)/shard_map/pairs/pallas_call | solution.py:228
  126.1 2.8 %collective-permute-start.9 = (bf16[384,384]{1,0:T(8,128)(2,1)S(1)}, bf16[384,384]{1,0:T(8,128)(2,1)}, u32[]{:S(2)}, u32[]{:S(2)}) collective-permute-start(bf16[384,384]{1,0:T(8,128)(2,1)S(1)} %get-tuple-element.58), channel_id=1, source_target_pairs={{2,0},{4,2},{6,4},{1,3},{3,5},{5,7},{10,8},{12,10},{14,12},{9,11},... | collective-permute-start | bytes 884744 | tf_op jit(solution)/shard_map/ppermute | solution.py:358
  130.3 1.7 copy-done.8
  132.0 1.7 copy-done.14
  133.7 6.9 %pairs.8 = (f32[2,384,384]{2,1,0:T(8,128)S(1)}, f32[2,2,384,384]{3,2,1,0:T(8,128)S(1)}) custom-call(s32[2]{0:T(128)S(1)} %pad_add_fusion.place_ref, bf16[2,800,384]{2,1,0:T(8,128)(2,1)S(1)} %bitcast.48, bf16[2,384,1536]{2,1,0:T(8,128)(2,1)S(1)} %bitcast.54, bf16[2,384,1536]{2,1,0:T(8,128)(2,1)S(1)} %bitcast.62), custom_call_target="tpu_custom_call" | custom-call | flops 4529848320 | bytes 5898240 | tf_op jit(solution)/shard_map/pairs/pallas_call | solution.py:228
  140.6 10.3 %pairs.9 = (f32[2,384,384]{2,1,0:T(8,128)S(1)}, bf16[384,384]{1,0:T(8,128)(2,1)S(1)}, bf16[2,2,384,384]{3,2,1,0:T(8,128)(2,1)}, bf16[2,384,384]{2,1,0:T(8,128)(2,1)S(1)}) custom-call(s32[2]{0:T(128)S(1)} %pad_add_fusion.place_ref, bf16[2,800,384]{2,1,0:T(8,128)(2,1)S(1)} %bitcast.49, bf16[800,384]{1,0:T(8,128)(2,1)} %collective-permute-done.refs_1_, ...), custom_call_target="tpu_custom_call" | custom-call | flops 5662310400 | bytes 5898240 | tf_op jit(solution)/shard_map/pairs/pallas_call | solution.py:228
  150.9 1.9 collective-permute-start.3
  153.8 4.5 %collective-permute-done.3 = bf16[384,384]{1,0:T(8,128)(2,1)S(1)} collective-permute-done((bf16[384,384]{1,0:T(8,128)(2,1)S(1)}, bf16[384,384]{1,0:T(8,128)(2,1)S(1)}, u32[]{:S(2)}, u32[]{:S(2)}) %collective-permute-start.3) | collective-permute-done | bytes 294944 | tf_op jit(solution)/shard_map/ppermute | solution.py:358
  161.9 3.0 %collective-permute-start.5 = (bf16[800,512]{1,0:T(8,128)(2,1)S(1)}, bf16[800,512]{1,0:T(8,128)(2,1)S(1)}, u32[]{:S(2)}, u32[]{:S(2)}) collective-permute-start(bf16[800,512]{1,0:T(8,128)(2,1)S(1)} %dynamic-slice_bitcast_fusion), channel_id=1, source_target_pairs={{0,2},{2,4},{4,6},{3,1},{5,3},{7,5},{8,10},{10,12},{12,14},{11,9},... | collective-permute-start | bytes 2457608 | tf_op jit(solution)/shard_map/ppermute | solution.py:342
  166.6 1.7 copy-done.15
  168.3 9.3 %pairs.10 = (f32[2,384,512]{2,1,0:T(8,128)S(1)}, f32[2,2,384,512]{3,2,1,0:T(8,128)S(1)}) custom-call(s32[2]{0:T(128)S(1)} %pad_add_fusion.place_ref, bf16[2,800,512]{2,1,0:T(8,128)(2,1)S(1)} %bitcast.42, bf16[2,384,1536]{2,1,0:T(8,128)(2,1)S(1)} %bitcast.56, bf16[2,384,1536]{2,1,0:T(8,128)(2,1)S(1)} %bitcast.64), custom_call_target="tpu_custom_call" | custom-call | flops 6039797760 | bytes 7864320 | tf_op jit(solution)/shard_map/pairs/pallas_call | solution.py:228
  177.6 13.2 %pairs.11 = (f32[2,384,512]{2,1,0:T(8,128)S(1)}, bf16[384,512]{1,0:T(8,128)(2,1)S(1)}, bf16[2,2,384,512]{3,2,1,0:T(8,128)(2,1)}, bf16[2,384,512]{2,1,0:T(8,128)(2,1)S(1)}) custom-call(s32[2]{0:T(128)S(1)} %pad_add_fusion.place_ref, bf16[2,800,512]{2,1,0:T(8,128)(2,1)S(1)} %bitcast.43, bf16[800,512]{1,0:T(8,128)(2,1)S(1)} %collective-permute-done.5.refs_1_, ...), custom_call_target="tpu_custom_call" | custom-call | flops 7549747200 | bytes 7864320 | tf_op jit(solution)/shard_map/pairs/pallas_call | solution.py:228
  190.8 2.6 collective-permute-start.6
  193.5 5.9 %collective-permute-done.6 = bf16[384,512]{1,0:T(8,128)(2,1)S(1)} collective-permute-done((bf16[384,512]{1,0:T(8,128)(2,1)S(1)}, bf16[384,512]{1,0:T(8,128)(2,1)S(1)}, u32[]{:S(2)}, u32[]{:S(2)}) %collective-permute-start.6) | collective-permute-done | bytes 393248 | tf_op jit(solution)/shard_map/ppermute | solution.py:358
  202.8 7.2 %collective-permute-start.7 = (bf16[2,384,512]{2,1,0:T(8,128)(2,1)S(1)}, bf16[2,384,512]{2,1,0:T(8,128)(2,1)S(1)}, u32[]{:S(2)}, u32[]{:S(2)}) collective-permute-start(bf16[2,384,512]{2,1,0:T(8,128)(2,1)S(1)} %get-tuple-element.54), channel_id=1, source_target_pairs={{8,16},{16,8},{9,17},{17,9},{10,18},{18,10},{11,19},{19,11},{12,20... | collective-permute-start | bytes 2359304 | tf_op jit(solution)/shard_map/ppermute | solution.py:365
  210.0 1.9 collective-permute-start.10
  211.9 3.6 %collective-permute-start.4 = (bf16[2,384,384]{2,1,0:T(8,128)(2,1)S(1)}, bf16[2,384,384]{2,1,0:T(8,128)(2,1)}, u32[]{:S(2)}, u32[]{:S(2)}) collective-permute-start(bf16[2,384,384]{2,1,0:T(8,128)(2,1)S(1)} %copy-done.25), channel_id=1, source_target_pairs={{8,16},{16,8},{9,17},{17,9},{10,18},{18,10},{11,19},{19,11},{12,20... | collective-permute-start | bytes 1769480 | tf_op jit(solution)/shard_map/ppermute | solution.py:365
  215.6 1.9 collective-permute-start.13
  217.5 19.0 %collective-permute-done.13.far = bf16[2,384,256]{2,1,0:T(8,128)(2,1)S(1)} collective-permute-done((bf16[2,384,256]{2,1,0:T(8,128)(2,1)S(1)}, bf16[2,384,256]{2,1,0:T(8,128)(2,1)S(1)}, u32[]{:S(2)}, u32[]{:S(2)}) %collective-permute-start.13) | collective-permute-done | bytes 393248 | tf_op jit(solution)/shard_map/ppermute | solution.py:365
  237.3 2.0 finish.4
  239.3 3.1 %finish.5 = (bf16[384,1536]{1,0:T(8,128)(2,1)}, bf16[384,1536]{1,0:T(8,128)(2,1)}, bf16[384,1536]{1,0:T(8,128)(2,1)}) custom-call(bf16[384,384]{1,0:T(8,128)(2,1)} %bitcast.91, bf16[2,384,384]{2,1,0:T(8,128)(2,1)} %bitcast.87, bf16[2,384,384]{2,1,0:T(8,128)(2,1)} %collective-permute-done.10.far, ...), custom_call_target="tpu_custom_call", output_to_operand_aliasing={{0}: (3, {}), {1}: (4, {}), {2}: (5, {})} | custom-call | flops 589824 | bytes 2359296 | tf_op jit(solution)/shard_map/finish/pallas_call | solution.py:266
  243.3 3.6 %finish.6 = (bf16[384,1536]{1,0:T(8,128)(2,1)}, bf16[384,1536]{1,0:T(8,128)(2,1)}, bf16[384,1536]{1,0:T(8,128)(2,1)}) custom-call(bf16[384,512]{1,0:T(8,128)(2,1)} %bitcast.90, bf16[2,384,512]{2,1,0:T(8,128)(2,1)} %bitcast.82, bf16[2,384,512]{2,1,0:T(8,128)(2,1)} %copy-done.34, ...), custom_call_target="tpu_custom_call", output_to_operand_aliasing={{0}: (3, {}), {1}: (4, {}), {2}: (5, {})} | custom-call | flops 786432 | bytes 3145728 | tf_op jit(solution)/shard_map/finish/pallas_call | solution.py:266
  247.0 5.3 %reduce-scatter.9.cloned.1.call-done = bf16[1,384,384]{2,1,0:T(8,128)(2,1)} async-done(((bf16[2,384,384]{2,1,0:T(8,128)(2,1)}), bf16[1,384,384]{2,1,0:T(8,128)(2,1)}) %reduce-scatter.9.cloned.1.call-update) | async-done | bytes 294928 | tf_op jit(solution)/shard_map/reduce_scatter | solution.py:361
  252.3 11.7 %reduce-scatter.11.cloned.1.call-done = bf16[1,2,384,384]{3,2,1,0:T(8,128)(2,1)} async-done(((bf16[2,2,384,384]{3,2,1,0:T(8,128)(2,1)}), bf16[1,2,384,384]{3,2,1,0:T(8,128)(2,1)}) %reduce-scatter.11.cloned.1.call-update) | async-done | bytes 589840 | tf_op jit(solution)/shard_map/reduce_scatter | solution.py:364
  264.0 3.1 %finish.7 = (bf16[384,1536]{1,0:T(8,128)(2,1)}, bf16[384,1536]{1,0:T(8,128)(2,1)}, bf16[384,1536]{1,0:T(8,128)(2,1)}) custom-call(bf16[384,384]{1,0:T(8,128)(2,1)} %bitcast.92, bf16[2,384,384]{2,1,0:T(8,128)(2,1)} %bitcast.88, bf16[2,384,384]{2,1,0:T(8,128)(2,1)} %collective-permute-done.4.far, ...), custom_call_target="tpu_custom_call", output_to_operand_aliasing={{0}: (3, {}), {1}: (4, {}), {2}: (5, {})} | custom-call | flops 589824 | bytes 2359296 | tf_op jit(solution)/shard_map/finish/pallas_call | solution.py:266
  (126 shorter events, 29.3 us)
Async XLA Ops:
  7.2 29.8 %all-gather.12.cloned.1.call-start = ((), (), s32[]{:S(2)}) async-start(), calls=%async_computation.16 | async-start | bytes 1843200 | tf_op jit(solution)/shard_map/all_gather | solution.py:340
  12.3 50.6 %all-gather.16.cloned.1.call-start = ((), (), s32[]{:S(2)}) async-start(), calls=%async_computation.18 | async-start | bytes 3538944 | tf_op jit(solution)/shard_map/all_gather | solution.py:331
  13.1 50.9 %all-gather.18.cloned.1.call-start = ((), (), s32[]{:S(2)}) async-start(), calls=%async_computation.19 | async-start | bytes 3538944 | tf_op jit(solution)/shard_map/all_gather | solution.py:331
  13.8 88.3 %all-gather.14.cloned.1.call-start = ((), (), s32[]{:S(2)}) async-start(), calls=%async_computation.17 | async-start | bytes 1843200 | tf_op jit(solution)/shard_map/all_gather | solution.py:340
  39.4 121.2 %all-gather.20.cloned.1.call-start = ((), (), s32[]{:S(2)}) async-start(), calls=%async_computation.20 | async-start | bytes 2457600 | tf_op jit(solution)/shard_map/all_gather | solution.py:340
  39.4 32.7 %collective-permute-start.1 = (bf16[384,1536]{1,0:T(8,128)(2,1)}, bf16[384,1536]{1,0:T(8,128)(2,1)S(1)}, u32[]{:S(2)}, u32[]{:S(2)}) collective-permute-start(bf16[384,1536]{1,0:T(8,128)(2,1)} %bitcast.12), channel_id=1, source_target_pairs={{8,16},{16,8},{9,17},{17,9},{10,18},{18,10},{11,19},{19,11},{12,20... | collective-permute-start | bytes 3538952 | tf_op jit(solution)/shard_map/ppermute | solution.py:333
  43.1 29.0 %collective-permute-start.2 = (bf16[384,1536]{1,0:T(8,128)(2,1)}, bf16[384,1536]{1,0:T(8,128)(2,1)S(1)}, u32[]{:S(2)}, u32[]{:S(2)}) collective-permute-start(bf16[384,1536]{1,0:T(8,128)(2,1)} %bitcast.81), channel_id=1, source_target_pairs={{8,16},{16,8},{9,17},{17,9},{10,18},{18,10},{11,19},{19,11},{12,20... | collective-permute-start | bytes 3538952 | tf_op jit(solution)/shard_map/ppermute | solution.py:333
  58.9 177.7 %reduce-scatter.21.cloned.1.call-start = ((), (), s32[]{:S(2)}) async-start(), calls=%async_computation.14 | async-start | bytes 589824 | tf_op jit(solution)/shard_map/reduce_scatter | solution.py:361
  59.7 12.4 %collective-permute-start.11 = (bf16[800,256]{1,0:T(8,128)(2,1)}, bf16[800,256]{1,0:T(8,128)(2,1)}, u32[]{:S(2)}, u32[]{:S(2)}) collective-permute-start(bf16[800,256]{1,0:T(8,128)(2,1)} %dynamic-slice_bitcast_fusion.3), channel_id=1, source_target_pairs={{0,2},{2,4},{4,6},{3,1},{5,3},{7,5},{8,10},{10,12},{12,14},{11,9},... | collective-permute-start | bytes 1228808 | tf_op jit(solution)/shard_map/ppermute | solution.py:342
  67.3 5.9 %copy-start.5 = (bf16[2,1,384,1536]{3,2,1,0:T(8,128)(2,1)S(1)}, bf16[2,1,384,1536]{3,2,1,0:T(8,128)(2,1)}, u32[]{:S(2)}) copy-start(bf16[2,1,384,1536]{3,2,1,0:T(8,128)(2,1)} %all-gather.16.cloned.1.call-done) | copy-start | bytes 7077892
  72.1 9.8 %copy-start.16 = (bf16[384,1536]{1,0:T(8,128)(2,1)}, bf16[384,1536]{1,0:T(8,128)(2,1)S(1)}, u32[]{:S(2)}) copy-start(bf16[384,1536]{1,0:T(8,128)(2,1)S(1)} %collective-permute-done.1.refs_4_) | copy-start | bytes 3538948
  74.5 10.1 %copy-start.1 = (bf16[1600,384]{1,0:T(8,128)(2,1)S(1)}, bf16[1600,384]{1,0:T(8,128)(2,1)}, u32[]{:S(2)}) copy-start(bf16[1600,384]{1,0:T(8,128)(2,1)} %all-gather.12.cloned.1.call-done) | copy-start | bytes 3686404
  82.7 6.7 %collective-permute-start.12 = (bf16[384,256]{1,0:T(8,128)(2,1)S(1)}, bf16[384,256]{1,0:T(8,128)(2,1)S(1)}, u32[]{:S(2)}, u32[]{:S(2)}) collective-permute-start(bf16[384,256]{1,0:T(8,128)(2,1)S(1)} %get-tuple-element.64), channel_id=1, source_target_pairs={{2,0},{4,2},{6,4},{1,3},{3,5},{5,7},{10,8},{12,10},{14,12},{9,11},... | collective-permute-start | bytes 589832 | tf_op jit(solution)/shard_map/ppermute | solution.py:358
  85.6 22.2 %collective-permute-start.8 = (bf16[800,384]{1,0:T(8,128)(2,1)}, bf16[800,384]{1,0:T(8,128)(2,1)S(1)}, u32[]{:S(2)}, u32[]{:S(2)}) collective-permute-start(bf16[800,384]{1,0:T(8,128)(2,1)} %dynamic-slice_bitcast_fusion.1), channel_id=1, source_target_pairs={{0,2},{2,4},{4,6},{3,1},{5,3},{7,5},{8,10},{10,12},{12,14},{11,9},... | collective-permute-start | bytes 1843208 | tf_op jit(solution)/shard_map/ppermute | solution.py:342
  90.4 146.1 %reduce-scatter.23.cloned.1.call-start = ((), (), s32[]{:S(2)}) async-start(), calls=%async_computation.15 | async-start | bytes 1179648 | tf_op jit(solution)/shard_map/reduce_scatter | solution.py:364
  90.4 1.7 copy-start.6
  92.1 1.7 copy-start.12
  102.1 5.7 %copy-start.32 = (f32[2,384,384]{2,1,0:T(8,128)}, f32[2,384,384]{2,1,0:T(8,128)S(1)}, u32[]{:S(2)}) copy-start(f32[2,384,384]{2,1,0:T(8,128)S(1)} %get-tuple-element.55.refs_6_) | copy-start | bytes 3538948
  102.1 5.7 %copy-start.17 = (bf16[384,1536]{1,0:T(8,128)(2,1)S(1)}, bf16[384,1536]{1,0:T(8,128)(2,1)}, u32[]{:S(2)}) copy-start(bf16[384,1536]{1,0:T(8,128)(2,1)} %copy-done.16) | copy-start | bytes 3538948
  104.5 36.1 %collective-permute-start = (bf16[800,384]{1,0:T(8,128)(2,1)}, bf16[800,384]{1,0:T(8,128)(2,1)}, u32[]{:S(2)}, u32[]{:S(2)}) collective-permute-start(bf16[800,384]{1,0:T(8,128)(2,1)} %dynamic-slice_bitcast_fusion.2), channel_id=1, source_target_pairs={{0,2},{2,4},{4,6},{3,1},{5,3},{7,5},{8,10},{10,12},{12,14},{11,9},... | collective-permute-start | bytes 1843208 | tf_op jit(solution)/shard_map/ppermute | solution.py:342
  107.8 1.7 copy-start.7
  126.1 26.7 %collective-permute-start.9 = (bf16[384,384]{1,0:T(8,128)(2,1)S(1)}, bf16[384,384]{1,0:T(8,128)(2,1)}, u32[]{:S(2)}, u32[]{:S(2)}) collective-permute-start(bf16[384,384]{1,0:T(8,128)(2,1)S(1)} %get-tuple-element.58), channel_id=1, source_target_pairs={{2,0},{4,2},{6,4},{1,3},{3,5},{5,7},{10,8},{12,10},{14,12},{9,11},... | collective-permute-start | bytes 884744 | tf_op jit(solution)/shard_map/ppermute | solution.py:358
  129.0 110.3 %reduce-scatter.17.cloned.1.call-start = ((), (), s32[]{:S(2)}) async-start(), calls=%async_computation.12 | async-start | bytes 884736 | tf_op jit(solution)/shard_map/reduce_scatter | solution.py:361
  130.3 1.7 copy-start.8
  132.0 1.7 copy-start.14
  133.7 6.9 %copy-start.3 = (bf16[1600,384]{1,0:T(8,128)(2,1)S(1)}, bf16[1600,384]{1,0:T(8,128)(2,1)}, u32[]{:S(2)}) copy-start(bf16[1600,384]{1,0:T(8,128)(2,1)} %all-gather.14.cloned.1.call-done) | copy-start | bytes 3686404
  133.7 6.9 %copy-start.18 = (bf16[384,1536]{1,0:T(8,128)(2,1)S(1)}, bf16[384,1536]{1,0:T(8,128)(2,1)}, u32[]{:S(2)}) copy-start(bf16[384,1536]{1,0:T(8,128)(2,1)} %copy-done.16) | copy-start | bytes 3538948
  133.7 6.9 %copy-start.22 = (bf16[384,1536]{1,0:T(8,128)(2,1)S(1)}, bf16[384,1536]{1,0:T(8,128)(2,1)}, u32[]{:S(2)}) copy-start(bf16[384,1536]{1,0:T(8,128)(2,1)} %copy-done.19) | copy-start | bytes 3538948
  150.9 8.9 %copy-start.24 = (bf16[2,384,384]{2,1,0:T(8,128)(2,1)}, bf16[2,384,384]{2,1,0:T(8,128)(2,1)S(1)}, u32[]{:S(2)}) copy-start(bf16[2,384,384]{2,1,0:T(8,128)(2,1)S(1)} %get-tuple-element.47) | copy-start | bytes 1769476
  150.9 7.5 %collective-permute-start.3 = (bf16[384,384]{1,0:T(8,128)(2,1)S(1)}, bf16[384,384]{1,0:T(8,128)(2,1)S(1)}, u32[]{:S(2)}, u32[]{:S(2)}) collective-permute-start(bf16[384,384]{1,0:T(8,128)(2,1)S(1)} %get-tuple-element.45), channel_id=1, source_target_pairs={{2,0},{4,2},{6,4},{1,3},{3,5},{5,7},{10,8},{12,10},{14,12},{9,11},... | collective-permute-start | bytes 884744 | tf_op jit(solution)/shard_map/ppermute | solution.py:358
  159.8 79.5 %reduce-scatter.19.cloned.1.call-start = ((), (), s32[]{:S(2)}) async-start(), calls=%async_computation.13 | async-start | bytes 1769472 | tf_op jit(solution)/shard_map/reduce_scatter | solution.py:364
  160.5 82.0 %reduce-scatter.13.cloned.1.call-start = ((), (), s32[]{:S(2)}) async-start(), calls=%async_computation.10 | async-start | bytes 1179648 | tf_op jit(solution)/shard_map/reduce_scatter | solution.py:361
  160.6 4.3 %copy-start = (bf16[1600,512]{1,0:T(8,128)(2,1)S(1)}, bf16[1600,512]{1,0:T(8,128)(2,1)}, u32[]{:S(2)}) copy-start(bf16[1600,512]{1,0:T(8,128)(2,1)} %all-gather.20.cloned.1.call-done) | copy-start | bytes 4915204
  161.9 15.6 %collective-permute-start.5 = (bf16[800,512]{1,0:T(8,128)(2,1)S(1)}, bf16[800,512]{1,0:T(8,128)(2,1)S(1)}, u32[]{:S(2)}, u32[]{:S(2)}) collective-permute-start(bf16[800,512]{1,0:T(8,128)(2,1)S(1)} %dynamic-slice_bitcast_fusion), channel_id=1, source_target_pairs={{0,2},{2,4},{4,6},{3,1},{5,3},{7,5},{8,10},{10,12},{12,14},{11,9},... | collective-permute-start | bytes 2457608 | tf_op jit(solution)/shard_map/ppermute | solution.py:342
  164.9 1.7 copy-start.9
  168.3 9.3 %copy-start.10 = (bf16[2,1,384,1536]{3,2,1,0:T(8,128)(2,1)S(1)}, bf16[2,1,384,1536]{3,2,1,0:T(8,128)(2,1)}, u32[]{:S(2)}) copy-start(bf16[2,1,384,1536]{3,2,1,0:T(8,128)(2,1)} %all-gather.16.cloned.1.call-done) | copy-start | bytes 7077892
  168.3 9.3 %copy-start.23 = (bf16[384,1536]{1,0:T(8,128)(2,1)S(1)}, bf16[384,1536]{1,0:T(8,128)(2,1)}, u32[]{:S(2)}) copy-start(bf16[384,1536]{1,0:T(8,128)(2,1)} %copy-done.19) | copy-start | bytes 3538948
  190.8 8.5 %collective-permute-start.6 = (bf16[384,512]{1,0:T(8,128)(2,1)S(1)}, bf16[384,512]{1,0:T(8,128)(2,1)S(1)}, u32[]{:S(2)}, u32[]{:S(2)}) collective-permute-start(bf16[384,512]{1,0:T(8,128)(2,1)S(1)} %get-tuple-element.52), channel_id=1, source_target_pairs={{2,0},{4,2},{6,4},{1,3},{3,5},{5,7},{10,8},{12,10},{14,12},{9,11},... | collective-permute-start | bytes 1179656 | tf_op jit(solution)/shard_map/ppermute | solution.py:358
  200.7 41.8 %reduce-scatter.15.cloned.1.call-start = ((), (), s32[]{:S(2)}) async-start(), calls=%async_computation.11 | async-start | bytes 2359296 | tf_op jit(solution)/shard_map/reduce_scatter | solution.py:364
  201.5 8.5 %copy-start.27 = (bf16[2,384,384]{2,1,0:T(8,128)(2,1)S(1)}, bf16[2,384,384]{2,1,0:T(8,128)(2,1)}, u32[]{:S(2)}) copy-start(bf16[2,384,384]{2,1,0:T(8,128)(2,1)} %copy-done.26) | copy-start | bytes 1769476
  201.5 10.5 %copy-start.25 = (bf16[2,384,384]{2,1,0:T(8,128)(2,1)S(1)}, bf16[2,384,384]{2,1,0:T(8,128)(2,1)}, u32[]{:S(2)}) copy-start(bf16[2,384,384]{2,1,0:T(8,128)(2,1)} %copy-done.24) | copy-start | bytes 1769476
  201.5 14.1 %copy-start.29 = (bf16[2,384,256]{2,1,0:T(8,128)(2,1)S(1)}, bf16[2,384,256]{2,1,0:T(8,128)(2,1)}, u32[]{:S(2)}) copy-start(bf16[2,384,256]{2,1,0:T(8,128)(2,1)} %copy-done.28) | copy-start | bytes 1179652
  201.5 50.8 %reduce-scatter.9.cloned.1.call-start = ((), (), s32[]{:S(2)}) async-start(), calls=%async_computation.8 | async-start | bytes 884736 | tf_op jit(solution)/shard_map/reduce_scatter | solution.py:361
  202.1 62.0 %reduce-scatter.11.cloned.1.call-start = ((), (), s32[]{:S(2)}) async-start(), calls=%async_computation.9 | async-start | bytes 1769472 | tf_op jit(solution)/shard_map/reduce_scatter | solution.py:364
  202.8 39.6 %collective-permute-start.7 = (bf16[2,384,512]{2,1,0:T(8,128)(2,1)S(1)}, bf16[2,384,512]{2,1,0:T(8,128)(2,1)S(1)}, u32[]{:S(2)}, u32[]{:S(2)}) collective-permute-start(bf16[2,384,512]{2,1,0:T(8,128)(2,1)S(1)} %get-tuple-element.54), channel_id=1, source_target_pairs={{8,16},{16,8},{9,17},{17,9},{10,18},{18,10},{11,19},{19,11},{12,20... | collective-permute-start | bytes 2359304 | tf_op jit(solution)/shard_map/ppermute | solution.py:365
  210.0 29.3 %collective-permute-start.10 = (bf16[2,384,384]{2,1,0:T(8,128)(2,1)S(1)}, bf16[2,384,384]{2,1,0:T(8,128)(2,1)}, u32[]{:S(2)}, u32[]{:S(2)}) collective-permute-start(bf16[2,384,384]{2,1,0:T(8,128)(2,1)S(1)} %copy-done.27), channel_id=1, source_target_pairs={{8,16},{16,8},{9,17},{17,9},{10,18},{18,10},{11,19},{19,11},{12,20... | collective-permute-start | bytes 1769480 | tf_op jit(solution)/shard_map/ppermute | solution.py:365
  211.9 35.0 %collective-permute-start.4 = (bf16[2,384,384]{2,1,0:T(8,128)(2,1)S(1)}, bf16[2,384,384]{2,1,0:T(8,128)(2,1)}, u32[]{:S(2)}, u32[]{:S(2)}) collective-permute-start(bf16[2,384,384]{2,1,0:T(8,128)(2,1)S(1)} %copy-done.25), channel_id=1, source_target_pairs={{8,16},{16,8},{9,17},{17,9},{10,18},{18,10},{11,19},{19,11},{12,20... | collective-permute-start | bytes 1769480 | tf_op jit(solution)/shard_map/ppermute | solution.py:365
  215.6 20.9 %collective-permute-start.13 = (bf16[2,384,256]{2,1,0:T(8,128)(2,1)S(1)}, bf16[2,384,256]{2,1,0:T(8,128)(2,1)S(1)}, u32[]{:S(2)}, u32[]{:S(2)}) collective-permute-start(bf16[2,384,256]{2,1,0:T(8,128)(2,1)S(1)} %copy-done.29), channel_id=1, source_target_pairs={{8,16},{16,8},{9,17},{17,9},{10,18},{18,10},{11,19},{19,11},{12,20... | collective-permute-start | bytes 1179656 | tf_op jit(solution)/shard_map/ppermute | solution.py:365
  (15 other events, 19.2 us)
Sparse Core Ops, SparseCore 0:
  12.4 24.4 all-gather.11
  38.5 11.6 all-gather.15
  51.8 12.1 all-gather.17
  65.4 23.7 all-gather.13
  90.6 27.9 all-gather.19
  120.6 13.1 reduce-scatter.20
  136.1 8.9 reduce-scatter.22
  159.9 17.3 reduce-scatter.16
  179.7 9.3 reduce-scatter.18
  200.9 21.3 reduce-scatter.12
  224.6 9.7 reduce-scatter.14
  236.5 15.7 reduce-scatter.8
  254.6 9.3 reduce-scatter.10

commit v4 on v2

--- a/solution.py
+++ b/solution.py
@@ -15,12 +15,14 @@
 
 OUTER, OWN, PARTNER = (0, 1, 2)
 HERE, NEAR, FAR = (0, 1, 2)
-CHUNKS = (3, 3, 3, 3)
+CHUNKS = (4, 5, 3)
 STAGES = (
-    ((HERE, (OWN, PARTNER)), (NEAR, (OWN, PARTNER))),
+    ((HERE, (OWN,)), (NEAR, (OWN,))),
+    ((HERE, (PARTNER,)), (NEAR, (PARTNER,))),
     ((HERE, (OUTER,)), (NEAR, (OUTER,)), (FAR, (OWN, PARTNER, OUTER))),
 )
 EXTRA = 32
+VMEM_LIMIT = 16 * 1024 * 1024
 
 
 def dot(a, b, dims):
@@ -41,49 +43,90 @@
     return [row[:, i : i + lanes] for i in range(0, row.shape[1], lanes)]
 
 
-def prep_kernel(first, count, q_ref, g_ref, o_ref, lse_ref, flag_ref, out):
+def flag_row(frames, rows, frame, row, mask_ref, lanes):
+    toward = 1 - 2 * lax.rem(row, 2)
+    near = 1 - 2 * lax.rem(frame, 2)
+    lane = lax.broadcasted_iota(jnp.int32, (1, lanes), 1)
+    flags = jnp.zeros((1, lanes), F32)
+    for role in (OUTER, OWN, PARTNER):
+        for slot in (HERE, NEAR, FAR):
+            row_off = (role - 1) * toward
+            frame_off = (0, near, -near)[slot]
+            inside = (
+                (row + row_off >= 0)
+                & (row + row_off < rows)
+                & (frame + frame_off >= 0)
+                & (frame + frame_off < frames)
+            )
+            index = 3 * (frame_off + 1) + row_off + 1
+            on = inside & ((mask_ref[index] > 0) | (index == 4))
+            flags = jnp.where(lane == 3 * role + slot, on.astype(F32), flags)
+    return flags
+
+
+def prep_kernel(
+    counts, frames, rows, frame_ref, row_ref, mask_ref, q_ref, g_ref, o_ref, lse_ref, *outs
+):
     tile = q_ref.shape[0]
-    width = q_ref.shape[1] // count
-    out[0:tile, :] = q_ref[...]
-    out[tile : 2 * tile, :] = g_ref[...]
+    width = q_ref.shape[1] // sum(counts)
+    flags = flag_row(frames, rows, frame_ref[0], row_ref[0], mask_ref, width)
     ones = jnp.ones((8, width), BF16)
-    for h in range(count):
-        cols = slice(h * width, (h + 1) * width)
-        prod = g_ref[:, cols].astype(F32) * o_ref[:, cols].astype(F32)
-        high = prod.astype(BF16)
-        low = (prod - high.astype(F32)).astype(BF16)
-        delta = dot(ones, high, ((1,), (1,))) + dot(ones, low, ((1,), (1,)))
-        rows = []
-        for row in (lse_ref[first + h : first + h + 1, :] * LOG2E, delta[0:1, :]):
-            for term in three_terms(row):
-                rows += fold(term)
-        rows.append(flag_ref[...])
-        rows.append(jnp.zeros((EXTRA - len(rows), width), F32))
-        out[2 * tile : 2 * tile + EXTRA, cols] = jnp.concatenate(rows, axis=0).astype(BF16)
-
-
-def prep(first, count, head_width, q, g, o, lse, flags):
+    head = 0
+    for out, count in zip(outs, counts):
+        for h in range(count):
+            source = slice(head * width, (head + 1) * width)
+            cols = slice(h * width, (h + 1) * width)
+            grad = g_ref[:, source]
+            out[0:tile, cols] = q_ref[:, source]
+            out[tile : 2 * tile, cols] = grad
+            prod = grad.astype(F32) * o_ref[:, source].astype(F32)
+            high = prod.astype(BF16)
+            low = (prod - high.astype(F32)).astype(BF16)
+            delta = dot(ones, high, ((1,), (1,))) + dot(ones, low, ((1,), (1,)))
+            lines = []
+            for line in (lse_ref[head] * LOG2E, delta[0:1, :]):
+                for term in three_terms(line):
+                    lines += fold(term)
+            lines.append(flags)
+            lines.append(jnp.zeros((EXTRA - len(lines), width), F32))
+            extra = jnp.concatenate(lines, axis=0).astype(BF16)
+            out[2 * tile : 2 * tile + EXTRA, cols] = extra
+            head += 1
+
+
+def prep(first, counts, head_width, sizes, place, mask, q, g, o, lse):
     tile, full = q.shape
-    wide = count * head_width
+    count = sum(counts)
     offset = first * head_width
-    cols = pl.BlockSpec((pl.Element(tile), pl.Element(wide)), lambda i: (0, offset))
+    cols = pl.BlockSpec(
+        (pl.Element(tile), pl.Element(count * head_width)), lambda i, *_: (0, offset)
+    )
+    shapes = [(2 * tile + EXTRA, n * head_width) for n in counts]
     return pl.pallas_call(
-        functools.partial(prep_kernel, first, count),
-        grid=(1,),
-        in_specs=[
-            cols,
-            cols,
-            cols,
-            pl.BlockSpec(lse.shape, lambda i: (0, 0)),
-            pl.BlockSpec(flags.shape, lambda i: (0, 0)),
-        ],
-        out_specs=pl.BlockSpec((2 * tile + EXTRA, wide), lambda i: (0, 0)),
-        out_shape=jax.ShapeDtypeStruct((2 * tile + EXTRA, wide), BF16),
+        functools.partial(prep_kernel, counts, *sizes),
+        grid_spec=pltpu.PrefetchScalarGridSpec(
+            num_scalar_prefetch=3,
+            grid=(1,),
+            in_specs=[
+                cols,
+                cols,
+                cols,
+                pl.BlockSpec(
+                    (pl.Element(count), pl.Element(1), pl.Element(tile)),
+                    lambda i, *_: (first, 0, 0),
+                ),
+            ],
+            out_specs=[pl.BlockSpec(shape, lambda i, *_: (0, 0)) for shape in shapes],
+        ),
+        out_shape=[jax.ShapeDtypeStruct(shape, BF16) for shape in shapes],
+        compiler_params=pltpu.CompilerParams(vmem_limit_bytes=VMEM_LIMIT),
         cost_estimate=pl.CostEstimate(
-            flops=2 * tile * wide, bytes_accessed=10 * tile * wide, transcendentals=0
+            flops=2 * tile * count * head_width,
+            bytes_accessed=10 * tile * count * head_width,
+            transcendentals=0,
         ),
         name="prep",
-    )(q, g, o, lse, flags)
+    )(*place, mask, q, g, o, lse)
 
 
 def row_stats(message, tile):
@@ -208,7 +251,7 @@
             scratch_shapes=[pltpu.VMEM((tile, head_width), F32)] * len(used),
         ),
         out_shape=out_shapes,
-        compiler_params=pltpu.CompilerParams(vmem_limit_bytes=40 * 1024 * 1024),
+        compiler_params=pltpu.CompilerParams(vmem_limit_bytes=VMEM_LIMIT),
         cost_estimate=pl.CostEstimate(
             flops=20 * pairs * tile * tile * head_width,
             bytes_accessed=40 * tile * wide,
@@ -229,17 +272,21 @@
 
 def finish(first, count, head_width, full, parts, so_far):
     tile = parts[0].shape[0]
-    one = pl.BlockSpec((tile, head_width), lambda h: (0, h))
-    two = pl.BlockSpec((2, tile, head_width), lambda h: (0, 0, h))
-    cols = pl.BlockSpec((tile, head_width), lambda h: (0, h + first))
+    wide = count * head_width
+    one = pl.BlockSpec((tile, wide), lambda i: (0, 0))
+    two = pl.BlockSpec((2, tile, wide), lambda i: (0, 0, 0))
+    cols = pl.BlockSpec(
+        (pl.Element(tile), pl.Element(wide)), lambda i: (0, first * head_width)
+    )
     kept = [] if so_far is None else list(so_far)
     return pl.pallas_call(
         functools.partial(finish_kernel, head_width**-0.5),
-        grid=(count,),
+        grid=(1,),
         in_specs=[one, one, two, two, two] + [pl.BlockSpec(memory_space=pl.ANY)] * len(kept),
         out_specs=[cols] * 3,
         out_shape=[jax.ShapeDtypeStruct((tile, full), BF16)] * 3,
         input_output_aliases={5 + i: i for i in range(len(kept))},
+        compiler_params=pltpu.CompilerParams(vmem_limit_bytes=VMEM_LIMIT),
         cost_estimate=pl.CostEstimate(
             flops=8 * tile * count * head_width,
             bytes_accessed=30 * tile * count * head_width,
@@ -249,28 +296,6 @@
     )(*parts, *kept)
 
 
-def pair_flags(window_mask, lanes):
-    mask = window_mask.reshape(9)
-    frames, rows = (lax.axis_size("tm"), lax.axis_size("space"))
-    frame, row = (lax.axis_index("tm"), lax.axis_index("space"))
-    toward = 1 - 2 * lax.rem(row, 2)
-    near = 1 - 2 * lax.rem(frame, 2)
-    lane = jnp.arange(9, dtype=jnp.int32)
-    row_off = (lane // 3 - 1) * toward
-    slot = lane % 3
-    frame_off = jnp.where(slot == NEAR, near, jnp.where(slot == FAR, -near, 0))
-    inside = (
-        (row + row_off >= 0)
-        & (row + row_off < rows)
-        & (frame + frame_off >= 0)
-        & (frame + frame_off < frames)
-    )
-    index = 3 * (frame_off + 1) + row_off + 1
-    picked = jnp.sum(jnp.where(index[:, None] == lane[None, :], mask[None, :], 0), axis=1)
-    flags = (inside & ((picked > 0) | (index == 4))).astype(F32)
-    return jnp.pad(flags, (0, lanes - 9)).reshape(1, lanes)
-
-
 def after(value, *earlier):
     return lax.optimization_barrier((value, *earlier))[0]
 
@@ -282,53 +307,96 @@
     frames, rows = (lax.axis_size("tm"), lax.axis_size("space"))
     q, k, v, o, g = (a.reshape(tile, full) for a in (queries, keys, values, outputs, out_grads))
     partner = [(i, i ^ 1) for i in range(rows)]
-    onward = [(i, i + 2) for i in range(0, rows - 2, 2)]
-    onward += [(i, i - 2) for i in range(3, rows, 2)]
+    onward = [(i, (i + 2) % rows) for i in range(0, rows, 2)]
+    onward += [(i, (i - 2) % rows) for i in range(1, rows, 2)]
     homeward = [(b, a) for a, b in onward]
     near_pairs = [(i, i ^ 1) for i in range(frames)]
-    far_pairs = [(i, i + 1) for i in range(1, frames - 1, 2)]
-    far_pairs += [(b, a) for a, b in far_pairs]
-
-    frame = lax.axis_index("tm")
+    far_pairs = [(0, 0), (frames - 1, frames - 1)]
+    for i in range(1, frames - 1, 2):
+        far_pairs += [(i, i + 1), (i + 1, i)]
+
+    frame, row = (lax.axis_index("tm"), lax.axis_index("space"))
     far_frame = frame - 1 + 2 * lax.rem(frame, 2)
     has_far = ((far_frame >= 0) & (far_frame < frames)).astype(jnp.int32).reshape(1)
+    place = (frame.reshape(1), row.reshape(1))
 
     firsts = [sum(CHUNKS[:c]) for c in range(len(CHUNKS))]
-    flags = pair_flags(window_mask, width)
-    lse = log_sums.reshape(heads, tile)
+    lse = log_sums.reshape(heads, 1, tile)
+    mask = window_mask.reshape(9)
     near_kv = [lax.ppermute(a, "tm", near_pairs) for a in (k, v)]
-    far_kv = [lax.ppermute(a, "tm", far_pairs) for a in (k, v)]
-    mine, theirs, outers = ([], [], [])
-    for c, count in enumerate(CHUNKS):
-        source = q
-        if c == 1:
-            source = after(q, *near_kv)
+    make = lambda first, counts, source: prep(
+        first, counts, width, (frames, rows), place, mask, source, g, o, lse
+    )
+    mine = make(0, CHUNKS[:1], q)
+    theirs = {0: lax.ppermute(mine[0], "space", partner)}
+    mine += make(firsts[1], CHUNKS[1:], after(q, mine[0]))
+    far_kv = [lax.ppermute(after(a, mine[1]), "tm", far_pairs) for a in (k, v)]
+    frames_kv = {HERE: (k, v), NEAR: near_kv, FAR: far_kv}
+    outers = {}
+    sums = [{} for _ in CHUNKS]
+    backs = {}
+    done = []
+    out = None
+
+    def stage(c, step):
+        messages = {OUTER: outers.get(c), OWN: mine[c], PARTNER: theirs.get(c)}
+        work = STAGES[step]
+        needed = {j: messages[j] for _, js in work for j in js}
+        first_used = min(needed)
+        needed[first_used] = after(needed[first_used], *done[-1:])
+        last = ("q0", "kv1", "kv2") if step + 1 == len(STAGES) else ()
+        sums[c] = run_stage(
+            work, last, firsts[c], CHUNKS[c], width, has_far, frames_kv, needed, sums[c]
+        )
+        done.append(sums[c]["kv0"])
+
+    def hand_on(c):
+        outers[c] = lax.ppermute(after(theirs[c], *done[-1:]), "space", onward)
+
+    def send_home(c):
+        backs[c] = [
+            lax.ppermute(sums[c]["q0"], "space", homeward),
+            lax.ppermute(sums[c]["kv1"], "tm", near_pairs),
+            lax.ppermute(sums[c]["kv2"], "tm", far_pairs),
+        ]
+
+    def send_back(c):
+        home = after(backs[c][0], *done[-1:])
+        total = (sums[c]["q2"] + home.astype(F32)) * (width**-0.5)
+        backs[c][0] = lax.ppermute(total.astype(BF16), "space", partner)
+
+    def complete(c, so_far):
+        back_q, back_near, back_far = backs[c]
+        back_q = after(back_q, *done[-1:])
+        return finish(
+            firsts[c], CHUNKS[c], width, full,
+            (sums[c]["q1"], back_q, sums[c]["kv0"], back_near, back_far), so_far,
+        )
+
+    last = len(CHUNKS) - 1
+    theirs[1] = lax.ppermute(mine[1], "space", partner)
+    stage(0, 0)
+    stage(1, 0)
+    for c in range(2, len(CHUNKS)):
+        theirs[c] = lax.ppermute(after(mine[c], theirs[c - 2]), "space", partner)
+    hand_on(0)
+    for c in range(2, len(CHUNKS)):
+        stage(c, 0)
+    stage(0, 1)
+    for c in range(len(CHUNKS)):
+        if c < last:
+            hand_on(c + 1)
+        stage(c, 2)
+        send_home(c)
+        if c < last:
+            stage(c + 1, 1)
+            send_back(c)
         if c >= 2:
-            source = after(q, theirs[c - 2])
-        mine.append(prep(firsts[c], count, width, source, g, o, lse, flags))
-        theirs.append(lax.ppermute(mine[c], "space", partner))
-        outers.append(lax.ppermute(theirs[c], "space", onward))
-    frames_kv = {HERE: (k, v), NEAR: near_kv, FAR: far_kv}
-
-    out = None
-    for c, count in enumerate(CHUNKS):
-        messages = {OUTER: outers[c], OWN: mine[c], PARTNER: theirs[c]}
-        sums = {}
-        for step, work in enumerate(STAGES):
-            last = ("q0", "kv1", "kv2") if step + 1 == len(STAGES) else ()
-            needed = {j: messages[j] for _, js in work for j in js}
-            sums = run_stage(
-                work, last, firsts[c], count, width, has_far, frames_kv, needed, sums
-            )
-        home = lax.ppermute(sums["q0"], "space", homeward)
-        total = (sums["q2"] + home.astype(F32)) * (width**-0.5)
-        dq_back = lax.ppermute(total.astype(BF16), "space", partner)
-        near_back = lax.ppermute(sums["kv1"], "tm", near_pairs)
-        far_back = lax.ppermute(sums["kv2"], "tm", far_pairs)
-        out = finish(
-            firsts[c], count, width, full,
-            (sums["q1"], dq_back, sums["kv0"], near_back, far_back), out,
-        )
+            out = complete(c - 2, out)
+    send_back(last)
+    if last >= 1:
+        out = complete(last - 1, out)
+    out = complete(last, out)
     return tuple(a.reshape(queries.shape) for a in out)
 
 

time: 176 us -> 142 us (0.81)
  Pallas kernels: 92.4 us -> 77.9 us
  starting transfers between devices: 52.2 us -> 38.7 us
  local copies, waits for them, and re-layouts: 16.1 us -> 6.03 us
  waiting for transfers between devices: 9.53 us -> 15.7 us
  other arithmetic: 3.27 us -> 0.33 us
    ppermute x26 -> x20, starting transfers between devices: 51.3 us -> 37.8 us  [the longest x3 20.7 us: send_home(): lax.ppermute(sums[c]['kv2'], 'tm', far_pairs)]
    pallas_call x4 -> x3, Pallas kernels: 14.4 us -> 3.72 us  [finish(): pl.pallas_call(functools.partial(finish_kernel, head_width ** (-0.5)), gr...]
    unnamed x71 -> x18, local copies, waits for them, and re-layouts: 16.1 us -> 6.03 us
    ppermute x26 -> x20, waiting for transfers between devices: 9.53 us -> 15.7 us  [the longest x1 6.7 us: per_device(): theirs[1] = lax.ppermute(mine[1], 'space', partner)]
    pallas_call x4 -> x2, Pallas kernels: 9.54 us -> 3.56 us  [prep(): pl.pallas_call(functools.partial(prep_kernel, counts, *sizes), grid_spec=...]
    pallas_call x8 -> x9, Pallas kernels: 68.5 us -> 70.7 us  [run_stage(): pl.pallas_call(functools.partial(stage_kernel, work, names, carried, head...]
  transfers between devices with their start and end apart: 28 -> 22, of which waited for: 3 -> 4; matrix products, arithmetic and copies ran while one was open for 3% -> 0% of each run, Pallas kernels for 51% -> 55%
where the time goes in v4:
time: 142 us; the launch traced here: 140 us
  Pallas kernels  77.9 us (55%)
  starting transfers between devices  38.7 us (27%)
  waiting for transfers between devices  15.7 us (11%)
  local copies, waits for them, and re-layouts  6.03 us (4%)
    pallas_call x9, Pallas kernels, run_stage(): pl.pallas_call(functools.partial(stage_kernel, work, names, carried, head...  70.7 us
    ppermute x3, starting transfers between devices, send_home(): lax.ppermute(sums[c]['kv2'], 'tm', far_pairs)  20.7 us
    ppermute x1, waiting for transfers between devices, per_device(): theirs[1] = lax.ppermute(mine[1], 'space', partner)  6.7 us
    unnamed x18, local copies, waits for them, and re-layouts  6.03 us
    ppermute x2, starting transfers between devices, per_device(): far_kv = [lax.ppermute(after(a, mine[1]), 'tm', far_pairs) for a in (k, v)]  5.93 us
    ppermute x3, waiting for transfers between devices, send_back(): backs[c][0] = lax.ppermute(total.astype(BF16), 'space', partner)  5.64 us
    ppermute x3, starting transfers between devices, send_home(): lax.ppermute(sums[c]['q0'], 'space', homeward)  5.22 us
    pallas_call x3, Pallas kernels, finish(): pl.pallas_call(functools.partial(finish_kernel, head_width ** (-0.5)), gr...  3.72 us
  transfers between devices with their start and end apart: 22, of which 4 were waited for; matrix products, arithmetic and copies ran while one was open for 0% of the time, Pallas kernels for 55%

profile of v4, /device:TPU:9, one launch (start us, length us, event | category | flops | bytes accessed | tf_op | source)
XLA Modules:
  0.0 139.7 jit_solution(8772457970471634468)
XLA Ops:
  0.6 0.7 collective-permute-start.3
  1.4 0.1 collective-permute-start.4
  1.5 1.3 copy-done
  2.7 1.3 copy-done.1
  4.0 1.3 copy-done.2
  5.3 0.7 copy-done.3
  6.0 0.7 copy-done.4
  6.6 1.1 prep.2.refs_0_.refs_1_
  7.8 1.3 collective-permute-start
  9.0 2.5 %prep.3 = (bf16[800,640]{1,0:T(8,128)(2,1)}, bf16[800,384]{1,0:T(8,128)(2,1)S(1)}) custom-call(s32[1]{0:T(128)} %bitcast.1.frame_ref, s32[1]{0:T(128)} %bitcast.2.row_ref, s32[9]{0:T(128)S(1)} %bitcast.22, bf16[384,1536]{1,0:T(8,128)(2,1)S(1)} %bitcast.14, bf16[384,1536]{1,0:T(8,128)(2,1)S(1)} %bitcast.16, bf16[384,1536]{1,0:T(8,128)(2,1)S(1)} %bitcast.18, ...), custom_call_target="tpu_custom_call" | custom-call | flops 786432 | bytes 3932160 | tf_op jit(solution)/shard_map/prep/pallas_call | solution.py:105
  11.5 0.8 copy-done.7
  12.3 0.3 collective-permute-start.2
  12.6 4.0 %collective-permute-start.6 = (bf16[384,1536]{1,0:T(8,128)(2,1)S(1)}, bf16[384,1536]{1,0:T(8,128)(2,1)}, u32[]{:S(2)}, u32[]{:S(2)}) collective-permute-start(bf16[384,1536]{1,0:T(8,128)(2,1)S(1)} %bitcast.24), channel_id=1, source_target_pairs={{0,0},{24,24},{8,16},{16,8},{1,1},{25,25},{9,17},{17,9},{2,2},{26,... | collective-permute-start | bytes 3538952 | tf_op jit(solution)/shard_map/ppermute | solution.py:333
  16.7 1.9 %collective-permute-start.7 = (bf16[384,1536]{1,0:T(8,128)(2,1)S(1)}, bf16[384,1536]{1,0:T(8,128)(2,1)S(1)}, u32[]{:S(2)}, u32[]{:S(2)}) collective-permute-start(bf16[384,1536]{1,0:T(8,128)(2,1)S(1)} %bitcast.35), channel_id=1, source_target_pairs={{0,0},{24,24},{8,16},{16,8},{1,1},{25,25},{9,17},{17,9},{2,2},{26,... | collective-permute-start | bytes 3538952 | tf_op jit(solution)/shard_map/ppermute | solution.py:333
  18.6 5.7 %pairs.9 = (f32[384,512]{1,0:T(8,128)S(1)}, f32[2,384,512]{2,1,0:T(8,128)S(1)}, f32[2,384,512]{2,1,0:T(8,128)S(1)}) custom-call(s32[1]{0:T(128)} %bitcast.far_ref, bf16[800,512]{1,0:T(8,128)(2,1)S(1)} %prep.2.refs_0_.refs_1_, bf16[384,1536]{1,0:T(8,128)(2,1)S(1)} %bitcast.25, bf16[384,1536]{1,0:T(8,128)(2,1)S(1)} %bitcast.36, ...), custom_call_target="tpu_custom_call" | custom-call | flops 3019898880 | bytes 7864320 | tf_op jit(solution)/shard_map/pairs/pallas_call | solution.py:244
  24.3 0.0 copy-start.8
  24.3 6.6 %pairs.10 = (f32[384,640]{1,0:T(8,128)S(1)}, f32[2,384,640]{2,1,0:T(8,128)S(1)}, f32[2,384,640]{2,1,0:T(8,128)S(1)}) custom-call(s32[1]{0:T(128)} %bitcast.far_ref, bf16[800,640]{1,0:T(8,128)(2,1)} %get-tuple-element.76.refs_0_.refs_1_, bf16[384,1536]{1,0:T(8,128)(2,1)S(1)} %bitcast.26, bf16[384,1536]{1,0:T(8,128)(2,1)S(1)} %bitcast.37, ...), custom_call_target="tpu_custom_call" | custom-call | flops 3774873600 | bytes 9830400 | tf_op jit(solution)/shard_map/pairs/pallas_call | solution.py:244
  31.0 1.3 collective-permute-start.5
  32.3 0.1 collective-permute-start.1
  32.4 4.3 %pairs.11 = (f32[384,384]{1,0:T(8,128)S(1)}, f32[2,384,384]{2,1,0:T(8,128)S(1)}, f32[2,384,384]{2,1,0:T(8,128)S(1)}) custom-call(s32[1]{0:T(128)} %bitcast.far_ref, bf16[800,384]{1,0:T(8,128)(2,1)S(1)} %copy-done.8, bf16[384,1536]{1,0:T(8,128)(2,1)S(1)} %bitcast.27, bf16[384,1536]{1,0:T(8,128)(2,1)S(1)} %bitcast.38, ...), custom_call_target="tpu_custom_call" | custom-call | flops 2264924160 | bytes 5898240 | tf_op jit(solution)/shard_map/pairs/pallas_call | solution.py:244
  36.7 5.9 %pairs.12 = (f32[384,512]{1,0:T(8,128)S(1)}, f32[2,384,512]{2,1,0:T(8,128)S(1)}, f32[2,384,512]{2,1,0:T(8,128)S(1)}) custom-call(s32[1]{0:T(128)} %bitcast.far_ref, bf16[800,512]{1,0:T(8,128)(2,1)} %collective-permute-done.refs_0_.refs_2_, bf16[384,1536]{1,0:T(8,128)(2,1)S(1)} %bitcast.28, bf16[384,1536]{1,0:T(8,128)(2,1)S(1)} %bitcast.39, ...), custom_call_target="tpu_custom_call" | custom-call | flops 3019898880 | bytes 7864320 | tf_op jit(solution)/shard_map/pairs/pallas_call | solution.py:244
  42.6 6.7 %collective-permute-done.2.refs_0_.refs_2_ = bf16[800,640]{1,0:T(8,128)(2,1)} collective-permute-done((bf16[800,640]{1,0:T(8,128)(2,1)}, bf16[800,640]{1,0:T(8,128)(2,1)}, u32[]{:S(2)}, u32[]{:S(2)}) %collective-permute-start.2) | collective-permute-done | bytes 1024032 | tf_op jit(solution)/shard_map/ppermute | solution.py:377
  49.3 1.3 collective-permute-start.9
  50.6 12.5 %pairs.13 = (bf16[384,512]{1,0:T(8,128)(2,1)S(1)}, f32[384,512]{1,0:T(8,128)S(1)}, f32[384,512]{1,0:T(8,128)S(1)}, f32[2,384,512]{2,1,0:T(8,128)S(1)}, bf16[2,38...) custom-call(s32[1]{0:T(128)} %bitcast.far_ref, bf16[800,512]{1,0:T(8,128)(2,1)S(1)} %collective-permute-done.5.refs_0_, ...), custom_call_target="tpu_custom_call" | custom-call | flops 7549747200 | bytes 7864320 | tf_op jit(solution)/shard_map/pairs/pallas_call | solution.py:244
  63.1 1.3 collective-permute-start.18
  64.4 6.7 %pairs.14 = (f32[384,640]{1,0:T(8,128)S(1)}, f32[2,384,640]{2,1,0:T(8,128)S(1)}, f32[2,384,640]{2,1,0:T(8,128)S(1)}) custom-call(s32[1]{0:T(128)} %bitcast.far_ref, bf16[800,640]{1,0:T(8,128)(2,1)} %collective-permute-done.2.refs_0_.refs_2_, bf16[384,1536]{1,0:T(8,128)(2,1)S(1)} %bitcast.30, bf16[384,1536]{1,0:T(8,128)(2,1)S(1)} %bitcast.41, ...), custom_call_target="tpu_custom_call" | custom-call | flops 3774873600 | bytes 9830400 | tf_op jit(solution)/shard_map/pairs/pallas_call | solution.py:244
  71.2 0.3 collective-permute-start.8
  71.5 6.2 %collective-permute-start.21 = (bf16[2,384,512]{2,1,0:T(8,128)(2,1)S(1)}, bf16[2,384,512]{2,1,0:T(8,128)(2,1)S(1)}, u32[]{:S(2)}, u32[]{:S(2)}) collective-permute-start(bf16[2,384,512]{2,1,0:T(8,128)(2,1)S(1)} %get-tuple-element.129), channel_id=1, source_target_pairs={{0,0},{24,24},{8,16},{16,8},{1,1},{25,25},{9,17},{17,9},{2,2},{26,... | collective-permute-start | bytes 2359304 | tf_op jit(solution)/shard_map/ppermute | solution.py:360
  77.7 15.1 %pairs.15 = (bf16[384,640]{1,0:T(8,128)(2,1)S(1)}, f32[384,640]{1,0:T(8,128)S(1)}, f32[384,640]{1,0:T(8,128)S(1)}, f32[2,384,640]{2,1,0:T(8,128)S(1)}, bf16[2,38...) custom-call(s32[1]{0:T(128)} %bitcast.far_ref, bf16[800,640]{1,0:T(8,128)(2,1)S(1)} %collective-permute-done.9.refs_0_, ...), custom_call_target="tpu_custom_call" | custom-call | flops 9437184000 | bytes 9830400 | tf_op jit(solution)/shard_map/pairs/pallas_call | solution.py:244
  92.8 0.5 collective-permute-start.14
  93.3 4.4 %pairs.16 = (f32[384,384]{1,0:T(8,128)S(1)}, f32[2,384,384]{2,1,0:T(8,128)S(1)}, f32[2,384,384]{2,1,0:T(8,128)S(1)}) custom-call(s32[1]{0:T(128)} %bitcast.far_ref, bf16[800,384]{1,0:T(8,128)(2,1)S(1)} %collective-permute-done.1.refs_0_.refs_2_, bf16[384,1536]{1,0:T(8,128)(2,1)S(1)} %bitcast.32, bf16[384,1536]{1,0:T(8,128)(2,1)S(1)} %bitcast.43, ...), custom_call_target="tpu_custom_call" | custom-call | flops 2264924160 | bytes 5898240 | tf_op jit(solution)/shard_map/pairs/pallas_call | solution.py:244
  97.7 0.1 collective-permute-start.16
  97.8 0.1 multiply_convert_fusion.1
  98.0 1.3 collective-permute-start.19
  99.3 9.4 %pairs.17 = (bf16[384,384]{1,0:T(8,128)(2,1)S(1)}, f32[384,384]{1,0:T(8,128)S(1)}, f32[384,384]{1,0:T(8,128)S(1)}, f32[2,384,384]{2,1,0:T(8,128)S(1)}, bf16[2,38...) custom-call(s32[1]{0:T(128)} %bitcast.far_ref, bf16[800,384]{1,0:T(8,128)(2,1)S(1)} %collective-permute-done.8.refs_0_, ...), custom_call_target="tpu_custom_call" | custom-call | flops 5662310400 | bytes 5898240 | tf_op jit(solution)/shard_map/pairs/pallas_call | solution.py:244
  108.6 9.7 %collective-permute-start.17 = (bf16[2,384,640]{2,1,0:T(8,128)(2,1)S(1)}, bf16[2,384,640]{2,1,0:T(8,128)(2,1)S(1)}, u32[]{:S(2)}, u32[]{:S(2)}) collective-permute-start(bf16[2,384,640]{2,1,0:T(8,128)(2,1)S(1)} %get-tuple-element.122), channel_id=1, source_target_pairs={{0,0},{24,24},{8,16},{16,8},{1,1},{25,25},{9,17},{17,9},{2,2},{26,... | collective-permute-start | bytes 2949128 | tf_op jit(solution)/shard_map/ppermute | solution.py:360
  118.4 3.4 %collective-permute-start.10 = (bf16[384,384]{1,0:T(8,128)(2,1)S(1)}, bf16[384,384]{1,0:T(8,128)(2,1)S(1)}, u32[]{:S(2)}, u32[]{:S(2)}) collective-permute-start(bf16[384,384]{1,0:T(8,128)(2,1)S(1)} %get-tuple-element.110), channel_id=1, source_target_pairs={{2,0},{4,2},{6,4},{0,6},{7,1},{1,3},{3,5},{5,7},{10,8},{12,10},{14... | collective-permute-start | bytes 884744 | tf_op jit(solution)/shard_map/ppermute | solution.py:358
  121.7 0.1 multiply_convert_fusion
  121.9 0.1 collective-permute-start.15
  122.0 0.1 collective-permute-start.12
  122.0 3.4 %collective-permute-done.10 = bf16[384,384]{1,0:T(8,128)(2,1)S(1)} collective-permute-done((bf16[384,384]{1,0:T(8,128)(2,1)S(1)}, bf16[384,384]{1,0:T(8,128)(2,1)S(1)}, u32[]{:S(2)}, u32[]{:S(2)}) %collective-permute-start.10) | collective-permute-done | bytes 294944 | tf_op jit(solution)/shard_map/ppermute | solution.py:358
  125.4 4.8 %collective-permute-start.13 = (bf16[2,384,384]{2,1,0:T(8,128)(2,1)S(1)}, bf16[2,384,384]{2,1,0:T(8,128)(2,1)S(1)}, u32[]{:S(2)}, u32[]{:S(2)}) collective-permute-start(bf16[2,384,384]{2,1,0:T(8,128)(2,1)S(1)} %get-tuple-element.115), channel_id=1, source_target_pairs={{0,0},{24,24},{8,16},{16,8},{1,1},{25,25},{9,17},{17,9},{2,2},{26,... | collective-permute-start | bytes 1769480 | tf_op jit(solution)/shard_map/ppermute | solution.py:360
  130.2 0.1 multiply_convert_fusion.2
  130.3 2.7 %collective-permute-done.15.back_q = bf16[384,640]{1,0:T(8,128)(2,1)S(1)} collective-permute-done((bf16[384,640]{1,0:T(8,128)(2,1)S(1)}, bf16[384,640]{1,0:T(8,128)(2,1)S(1)}, u32[]{:S(2)}, u32[]{:S(2)}) %collective-permute-start.15) | collective-permute-done | bytes 491552 | tf_op jit(solution)/shard_map/ppermute | solution.py:366
  133.0 1.3 finish.3
  134.2 1.4 finish.4
  135.6 2.9 %collective-permute-done.11.back_q = bf16[384,384]{1,0:T(8,128)(2,1)S(1)} collective-permute-done((bf16[384,384]{1,0:T(8,128)(2,1)S(1)}, bf16[384,384]{1,0:T(8,128)(2,1)S(1)}, u32[]{:S(2)}, u32[]{:S(2)}) %collective-permute-start.11) | collective-permute-done | bytes 294944 | tf_op jit(solution)/shard_map/ppermute | solution.py:366
  138.5 1.1 finish.5
  (31 shorter events, 0.1 us)
Async XLA Ops:
  0.6 16.0 %collective-permute-start.3 = (bf16[384,1536]{1,0:T(8,128)(2,1)}, bf16[384,1536]{1,0:T(8,128)(2,1)}, u32[]{:S(2)}, u32[]{:S(2)}) collective-permute-start(bf16[384,1536]{1,0:T(8,128)(2,1)} %bitcast.23), channel_id=1, source_target_pairs={{0,8},{8,0},{16,24},{24,16},{1,9},{9,1},{17,25},{25,17},{2,10},{10... | collective-permute-start | bytes 3538952 | tf_op jit(solution)/shard_map/ppermute | solution.py:326
  1.4 17.2 %collective-permute-start.4 = (bf16[384,1536]{1,0:T(8,128)(2,1)}, bf16[384,1536]{1,0:T(8,128)(2,1)}, u32[]{:S(2)}, u32[]{:S(2)}) collective-permute-start(bf16[384,1536]{1,0:T(8,128)(2,1)} %bitcast.34), channel_id=1, source_target_pairs={{0,8},{8,0},{16,24},{24,16},{1,9},{9,1},{17,25},{25,17},{2,10},{10... | collective-permute-start | bytes 3538952 | tf_op jit(solution)/shard_map/ppermute | solution.py:326
  1.5 1.3 copy-start
  2.7 1.3 copy-start.1
  4.0 1.3 copy-start.2
  5.3 0.7 copy-start.3
  6.0 0.7 copy-start.4
  7.7 4.9 %copy-start.5 = (bf16[1,1,384,1536]{3,2,1,0:T(8,128)(2,1)S(1)}, bf16[1,1,384,1536]{3,2,1,0:T(8,128)(2,1)}, u32[]{:S(2)}) copy-start(bf16[1,1,384,1536]{3,2,1,0:T(8,128)(2,1)} %param.8) | copy-start | bytes 3538948
  7.7 8.9 %copy-start.6 = (bf16[1,1,384,1536]{3,2,1,0:T(8,128)(2,1)S(1)}, bf16[1,1,384,1536]{3,2,1,0:T(8,128)(2,1)}, u32[]{:S(2)}) copy-start(bf16[1,1,384,1536]{3,2,1,0:T(8,128)(2,1)} %param.9) | copy-start | bytes 3538948
  7.8 23.2 %collective-permute-start = (bf16[800,512]{1,0:T(8,128)(2,1)S(1)}, bf16[800,512]{1,0:T(8,128)(2,1)}, u32[]{:S(2)}, u32[]{:S(2)}) collective-permute-start(bf16[800,512]{1,0:T(8,128)(2,1)S(1)} %prep.2.refs_0_.refs_1_), channel_id=1, source_target_pairs={{0,1},{1,0},{2,3},{3,2},{4,5},{5,4},{6,7},{7,6},{8,9},{9,8},{10,11... | collective-permute-start | bytes 2457608 | tf_op jit(solution)/shard_map/ppermute | solution.py:331
  11.5 0.8 copy-start.7
  12.3 36.9 %collective-permute-start.2 = (bf16[800,640]{1,0:T(8,128)(2,1)}, bf16[800,640]{1,0:T(8,128)(2,1)}, u32[]{:S(2)}, u32[]{:S(2)}) collective-permute-start(bf16[800,640]{1,0:T(8,128)(2,1)} %get-tuple-element.76.refs_0_.refs_1_), channel_id=1, source_target_pairs={{0,1},{1,0},{2,3},{3,2},{4,5},{5,4},{6,7},{7,6},{8,9},{9,8},{10,11... | collective-permute-start | bytes 3072008 | tf_op jit(solution)/shard_map/ppermute | solution.py:377
  12.6 38.0 %collective-permute-start.6 = (bf16[384,1536]{1,0:T(8,128)(2,1)S(1)}, bf16[384,1536]{1,0:T(8,128)(2,1)}, u32[]{:S(2)}, u32[]{:S(2)}) collective-permute-start(bf16[384,1536]{1,0:T(8,128)(2,1)S(1)} %bitcast.24), channel_id=1, source_target_pairs={{0,0},{24,24},{8,16},{16,8},{1,1},{25,25},{9,17},{17,9},{2,2},{26,... | collective-permute-start | bytes 3538952 | tf_op jit(solution)/shard_map/ppermute | solution.py:333
  16.7 33.9 %collective-permute-start.7 = (bf16[384,1536]{1,0:T(8,128)(2,1)S(1)}, bf16[384,1536]{1,0:T(8,128)(2,1)S(1)}, u32[]{:S(2)}, u32[]{:S(2)}) collective-permute-start(bf16[384,1536]{1,0:T(8,128)(2,1)S(1)} %bitcast.35), channel_id=1, source_target_pairs={{0,0},{24,24},{8,16},{16,8},{1,1},{25,25},{9,17},{17,9},{2,2},{26,... | collective-permute-start | bytes 3538952 | tf_op jit(solution)/shard_map/ppermute | solution.py:333
  24.3 8.0 %copy-start.8 = (bf16[800,384]{1,0:T(8,128)(2,1)S(1)}, bf16[800,384]{1,0:T(8,128)(2,1)}, u32[]{:S(2)}) copy-start(bf16[800,384]{1,0:T(8,128)(2,1)} %copy-done.7) | copy-start | bytes 1843204
  31.0 19.6 %collective-permute-start.5 = (bf16[800,512]{1,0:T(8,128)(2,1)}, bf16[800,512]{1,0:T(8,128)(2,1)S(1)}, u32[]{:S(2)}, u32[]{:S(2)}) collective-permute-start(bf16[800,512]{1,0:T(8,128)(2,1)} %collective-permute-done.refs_0_.refs_2_), channel_id=1, source_target_pairs={{0,2},{2,4},{4,6},{6,0},{1,7},{3,1},{5,3},{7,5},{8,10},{10,12},{12... | collective-permute-start | bytes 2457608 | tf_op jit(solution)/shard_map/ppermute | solution.py:354
  32.3 38.9 %collective-permute-start.1 = (bf16[800,384]{1,0:T(8,128)(2,1)S(1)}, bf16[800,384]{1,0:T(8,128)(2,1)S(1)}, u32[]{:S(2)}, u32[]{:S(2)}) collective-permute-start(bf16[800,384]{1,0:T(8,128)(2,1)S(1)} %copy-done.8), channel_id=1, source_target_pairs={{0,1},{1,0},{2,3},{3,2},{4,5},{5,4},{6,7},{7,6},{8,9},{9,8},{10,11... | collective-permute-start | bytes 1843208 | tf_op jit(solution)/shard_map/ppermute | solution.py:381
  49.3 28.4 %collective-permute-start.9 = (bf16[800,640]{1,0:T(8,128)(2,1)}, bf16[800,640]{1,0:T(8,128)(2,1)S(1)}, u32[]{:S(2)}, u32[]{:S(2)}) collective-permute-start(bf16[800,640]{1,0:T(8,128)(2,1)} %collective-permute-done.2.refs_0_.refs_2_), channel_id=1, source_target_pairs={{0,2},{2,4},{4,6},{6,0},{1,7},{3,1},{5,3},{7,5},{8,10},{10,12},{12... | collective-permute-start | bytes 3072008 | tf_op jit(solution)/shard_map/ppermute | solution.py:354
  63.1 34.6 %collective-permute-start.18 = (bf16[384,512]{1,0:T(8,128)(2,1)S(1)}, bf16[384,512]{1,0:T(8,128)(2,1)S(1)}, u32[]{:S(2)}, u32[]{:S(2)}) collective-permute-start(bf16[384,512]{1,0:T(8,128)(2,1)S(1)} %get-tuple-element.125), channel_id=1, source_target_pairs={{2,0},{4,2},{6,4},{0,6},{7,1},{1,3},{3,5},{5,7},{10,8},{12,10},{14... | collective-permute-start | bytes 1179656 | tf_op jit(solution)/shard_map/ppermute | solution.py:358
  71.2 26.8 %collective-permute-start.8 = (bf16[800,384]{1,0:T(8,128)(2,1)S(1)}, bf16[800,384]{1,0:T(8,128)(2,1)S(1)}, u32[]{:S(2)}, u32[]{:S(2)}) collective-permute-start(bf16[800,384]{1,0:T(8,128)(2,1)S(1)} %collective-permute-done.1.refs_0_.refs_2_), channel_id=1, source_target_pairs={{0,2},{2,4},{4,6},{6,0},{1,7},{3,1},{5,3},{7,5},{8,10},{10,12},{12... | collective-permute-start | bytes 1843208 | tf_op jit(solution)/shard_map/ppermute | solution.py:354
  71.5 50.4 %collective-permute-start.20 = (bf16[2,384,512]{2,1,0:T(8,128)(2,1)S(1)}, bf16[2,384,512]{2,1,0:T(8,128)(2,1)S(1)}, u32[]{:S(2)}, u32[]{:S(2)}) collective-permute-start(bf16[2,384,512]{2,1,0:T(8,128)(2,1)S(1)} %get-tuple-element.128), channel_id=1, source_target_pairs={{0,8},{8,0},{16,24},{24,16},{1,9},{9,1},{17,25},{25,17},{2,10},{10... | collective-permute-start | bytes 2359304 | tf_op jit(solution)/shard_map/ppermute | solution.py:359
  71.5 50.5 %collective-permute-start.21 = (bf16[2,384,512]{2,1,0:T(8,128)(2,1)S(1)}, bf16[2,384,512]{2,1,0:T(8,128)(2,1)S(1)}, u32[]{:S(2)}, u32[]{:S(2)}) collective-permute-start(bf16[2,384,512]{2,1,0:T(8,128)(2,1)S(1)} %get-tuple-element.129), channel_id=1, source_target_pairs={{0,0},{24,24},{8,16},{16,8},{1,1},{25,25},{9,17},{17,9},{2,2},{26,... | collective-permute-start | bytes 2359304 | tf_op jit(solution)/shard_map/ppermute | solution.py:360
  92.8 15.8 %collective-permute-start.14 = (bf16[384,640]{1,0:T(8,128)(2,1)S(1)}, bf16[384,640]{1,0:T(8,128)(2,1)S(1)}, u32[]{:S(2)}, u32[]{:S(2)}) collective-permute-start(bf16[384,640]{1,0:T(8,128)(2,1)S(1)} %get-tuple-element.118), channel_id=1, source_target_pairs={{2,0},{4,2},{6,4},{0,6},{7,1},{1,3},{3,5},{5,7},{10,8},{12,10},{14... | collective-permute-start | bytes 1474568 | tf_op jit(solution)/shard_map/ppermute | solution.py:358
  97.7 36.5 %collective-permute-start.16 = (bf16[2,384,640]{2,1,0:T(8,128)(2,1)S(1)}, bf16[2,384,640]{2,1,0:T(8,128)(2,1)S(1)}, u32[]{:S(2)}, u32[]{:S(2)}) collective-permute-start(bf16[2,384,640]{2,1,0:T(8,128)(2,1)S(1)} %get-tuple-element.121), channel_id=1, source_target_pairs={{0,8},{8,0},{16,24},{24,16},{1,9},{9,1},{17,25},{25,17},{2,10},{10... | collective-permute-start | bytes 2949128 | tf_op jit(solution)/shard_map/ppermute | solution.py:359
  98.0 20.4 %collective-permute-start.19 = (bf16[384,512]{1,0:T(8,128)(2,1)S(1)}, bf16[384,512]{1,0:T(8,128)(2,1)S(1)}, u32[]{:S(2)}, u32[]{:S(2)}) collective-permute-start(bf16[384,512]{1,0:T(8,128)(2,1)S(1)} %multiply_convert_fusion.1), channel_id=1, source_target_pairs={{0,1},{1,0},{2,3},{3,2},{4,5},{5,4},{6,7},{7,6},{8,9},{9,8},{10,11... | collective-permute-start | bytes 1179656 | tf_op jit(solution)/shard_map/ppermute | solution.py:366
  108.6 25.6 %collective-permute-start.17 = (bf16[2,384,640]{2,1,0:T(8,128)(2,1)S(1)}, bf16[2,384,640]{2,1,0:T(8,128)(2,1)S(1)}, u32[]{:S(2)}, u32[]{:S(2)}) collective-permute-start(bf16[2,384,640]{2,1,0:T(8,128)(2,1)S(1)} %get-tuple-element.122), channel_id=1, source_target_pairs={{0,0},{24,24},{8,16},{16,8},{1,1},{25,25},{9,17},{17,9},{2,2},{26,... | collective-permute-start | bytes 2949128 | tf_op jit(solution)/shard_map/ppermute | solution.py:360
  118.4 7.1 %collective-permute-start.10 = (bf16[384,384]{1,0:T(8,128)(2,1)S(1)}, bf16[384,384]{1,0:T(8,128)(2,1)S(1)}, u32[]{:S(2)}, u32[]{:S(2)}) collective-permute-start(bf16[384,384]{1,0:T(8,128)(2,1)S(1)} %get-tuple-element.110), channel_id=1, source_target_pairs={{2,0},{4,2},{6,4},{0,6},{7,1},{1,3},{3,5},{5,7},{10,8},{12,10},{14... | collective-permute-start | bytes 884744 | tf_op jit(solution)/shard_map/ppermute | solution.py:358
  121.9 11.1 %collective-permute-start.15 = (bf16[384,640]{1,0:T(8,128)(2,1)S(1)}, bf16[384,640]{1,0:T(8,128)(2,1)S(1)}, u32[]{:S(2)}, u32[]{:S(2)}) collective-permute-start(bf16[384,640]{1,0:T(8,128)(2,1)S(1)} %multiply_convert_fusion), channel_id=1, source_target_pairs={{0,1},{1,0},{2,3},{3,2},{4,5},{5,4},{6,7},{7,6},{8,9},{9,8},{10,11... | collective-permute-start | bytes 1474568 | tf_op jit(solution)/shard_map/ppermute | solution.py:366
  122.0 16.6 %collective-permute-start.12 = (bf16[2,384,384]{2,1,0:T(8,128)(2,1)S(1)}, bf16[2,384,384]{2,1,0:T(8,128)(2,1)S(1)}, u32[]{:S(2)}, u32[]{:S(2)}) collective-permute-start(bf16[2,384,384]{2,1,0:T(8,128)(2,1)S(1)} %get-tuple-element.114), channel_id=1, source_target_pairs={{0,8},{8,0},{16,24},{24,16},{1,9},{9,1},{17,25},{25,17},{2,10},{10... | collective-permute-start | bytes 1769480 | tf_op jit(solution)/shard_map/ppermute | solution.py:359
  125.4 13.1 %collective-permute-start.13 = (bf16[2,384,384]{2,1,0:T(8,128)(2,1)S(1)}, bf16[2,384,384]{2,1,0:T(8,128)(2,1)S(1)}, u32[]{:S(2)}, u32[]{:S(2)}) collective-permute-start(bf16[2,384,384]{2,1,0:T(8,128)(2,1)S(1)} %get-tuple-element.115), channel_id=1, source_target_pairs={{0,0},{24,24},{8,16},{16,8},{1,1},{25,25},{9,17},{17,9},{2,2},{26,... | collective-permute-start | bytes 1769480 | tf_op jit(solution)/shard_map/ppermute | solution.py:360
  133.0 5.6 %collective-permute-start.11 = (bf16[384,384]{1,0:T(8,128)(2,1)S(1)}, bf16[384,384]{1,0:T(8,128)(2,1)S(1)}, u32[]{:S(2)}, u32[]{:S(2)}) collective-permute-start(bf16[384,384]{1,0:T(8,128)(2,1)S(1)} %multiply_convert_fusion.2), channel_id=1, source_target_pairs={{0,1},{1,0},{2,3},{3,2},{4,5},{5,4},{6,7},{7,6},{8,9},{9,8},{10,11... | collective-permute-start | bytes 884744 | tf_op jit(solution)/shard_map/ppermute | solution.py:366

commit v5 on v4

--- a/solution.py
+++ b/solution.py
@@ -21,6 +21,14 @@
     ((HERE, (PARTNER,)), (NEAR, (PARTNER,))),
     ((HERE, (OUTER,)), (NEAR, (OUTER,)), (FAR, (OWN, PARTNER, OUTER))),
 )
+LATER_STAGES = (
+    STAGES[0],
+    STAGES[1] + ((FAR, (PARTNER,)),),
+    ((HERE, (OUTER,)), (NEAR, (OUTER,)), (FAR, (OWN, OUTER))),
+)
+ORDER = (('stage', 0, 0), ('stage', 1, 0), ('hand', 0), ('stage', 2, 0), ('stage', 0, 1), ('hand', 1), ('stage', 1, 1), ('stage', 0, 2), ('hand', 2), ('stage', 2, 1), ('stage', 1, 2, (0, 'q0')), ('stage', 2, 2, (0, 'q2'), (0, 'kv1')), ('finish', 0), ('finish', 1), ('finish', 2))
+JOINED = ()
+WEIGHTS = ((40, 40, 20), (20, 10, 20), (20, 40, 40))
 EXTRA = 32
 VMEM_LIMIT = 16 * 1024 * 1024
 
@@ -126,7 +134,31 @@
             transcendentals=0,
         ),
         name="prep",
-    )(*place, mask, q, g, o, lse)
+    )(*place, mask, *(pltpu.with_memory_space_constraint(a, pltpu.HBM) for a in (q, g, o)), lse)
+
+
+def pack_kernel(k_ref, v_ref, out, sems):
+    copies = [
+        pltpu.make_async_copy(source, out.at[i], sems.at[i])
+        for i, source in enumerate((k_ref, v_ref))
+    ]
+    for copy in copies:
+        copy.start()
+    for copy in copies:
+        copy.wait()
+
+
+def pack(k, v):
+    anywhere = pl.BlockSpec(memory_space=pl.ANY)
+    return pl.pallas_call(
+        pack_kernel,
+        in_specs=[anywhere, anywhere],
+        out_specs=anywhere,
+        out_shape=jax.ShapeDtypeStruct((2,) + k.shape, k.dtype),
+        scratch_shapes=[pltpu.SemaphoreType.DMA((2,))],
+        cost_estimate=pl.CostEstimate(flops=0, bytes_accessed=8 * k.size, transcendentals=0),
+        name="pack",
+    )(k, v)
 
 
 def row_stats(message, tile):
@@ -142,12 +174,22 @@
     return (rows[0], rows[1], extra[6 * parts : 6 * parts + 1])
 
 
-def stage_kernel(work, names, carried, factor, far_ref, *refs):
+def stage_kernel(work, names, carried, last, factor, far_ref, *refs):
     env = dict(zip(names, refs))
     tile = env["message%d" % work[0][1][0]].shape[0] - EXTRA
     tile //= 2
+    width = env["both"].shape[2] // 2
     used = sorted({j for _, js in work for j in js})
     stats = {j: row_stats(env["message%d" % j], tile) for j in used}
+    both = {j: env["both"].at[i] for i, j in enumerate(used)}
+
+    @pl.when(pl.program_id(0) == 0)
+    def _():
+        env["both"][...] = jnp.zeros_like(env["both"])
+
+    for j in used:
+        both[j][0:tile, 0:width] = env["message%d" % j][0:tile, :]
+        both[j][tile:, width:] = env["message%d" % j][tile : 2 * tile, :]
     started = set()
 
     def add_q(j, term):
@@ -160,37 +202,45 @@
             env["sum_" + name][...] = term
         started.add(name)
 
-    def key_frame(slot, js):
-        key = env["k%d" % slot][...]
-        value = env["v%d" % slot][...]
-        name = "acc_kv%d" % slot
-        dk, dv = (env[name][0], env[name][1]) if name in env else (None, None)
+    def pair(slot, j):
+        shift, delta, flags = stats[j]
+        lane = 3 * j + slot
+        shift = jnp.where(flags[:, lane : lane + 1] > 0, shift, FAR_AWAY)
+        keys = jnp.concatenate((env["keys%d" % slot][0], env["keys%d" % slot][1]), axis=1)
+        products = dot(keys, both[j][...], ((1,), (1,)))
+        weights = jnp.exp2(products[:, :tile] * (factor * LOG2E) - shift)
+        grad_score = (weights * (products[:, tile:] - delta)).astype(BF16)
+        joint = jnp.concatenate((grad_score, weights.astype(BF16)), axis=1)
+        return (grad_score, dot(joint, both[j][...], ((1,), (0,))))
+
+    def put_keys(slot, terms):
+        name = "kv%d" % slot
+        dk, dv = (terms[:, :width], terms[:, width:])
+        if "acc_" + name in env:
+            dk, dv = (dk + env["acc_" + name][0], dv + env["acc_" + name][1])
+        out = env["out_" + name]
+        out[0] = (dk * factor if name in last else dk).astype(out.dtype)
+        out[1] = dv.astype(out.dtype)
+
+    def frames(slots, js):
+        terms = {}
         for j in js:
-            message = env["message%d" % j]
-            qj = message[0:tile, :]
-            gj = message[tile : 2 * tile, :]
-            shift, delta, flags = stats[j]
-            lane = 3 * j + slot
-            shift = jnp.where(flags[:, lane : lane + 1] > 0, shift, FAR_AWAY)
-            scores = dot(key, qj, ((1,), (1,)))
-            weights = jnp.exp2(scores * (factor * LOG2E) - shift)
-            grad_prob = dot(value, gj, ((1,), (1,)))
-            grad_score = (weights * (grad_prob - delta)).astype(BF16)
-            term_v = dot(weights.astype(BF16), gj, ((1,), (0,)))
-            term_k = dot(grad_score, qj, ((1,), (0,))) * factor
-            add_q(j, dot(grad_score, key, ((0,), (0,))))
-            dv = term_v if dv is None else dv + term_v
-            dk = term_k if dk is None else dk + term_k
-        out = env["out_kv%d" % slot]
-        out[0] = dk.astype(out.dtype)
-        out[1] = dv.astype(out.dtype)
-
-    for slot, js in work:
-        if slot != FAR:
-            key_frame(slot, js)
+            scores = []
+            for slot in slots:
+                grad_score, term = pair(slot, j)
+                terms[slot] = term if slot not in terms else terms[slot] + term
+                scores.append(grad_score)
+            keys = [env["keys%d" % slot][0] for slot in slots]
+            joint = [jnp.concatenate(a, axis=0) if len(slots) > 1 else a[0] for a in (scores, keys)]
+            add_q(j, dot(*joint, ((0,), (0,))))
+        for slot in slots:
+            put_keys(slot, terms[slot])
+
+    near = [slot for slot, _ in work if slot != FAR]
+    frames(near, work[0][1])
     for slot, js in work:
         if slot == FAR:
-            pl.when(far_ref[0] > 0)(functools.partial(key_frame, slot, js))
+            pl.when(far_ref[0] > 0)(functools.partial(frames, [slot], js))
 
             @pl.when(far_ref[0] == 0)
             def _():
@@ -207,12 +257,12 @@
         out[...] = (env["sum_q%d" % j][...]).astype(out.dtype)
 
 
-def run_stage(work, last, first, count, head_width, far, keys, messages, sums):
+def run_stage(work, weight, last, joined, first, count, head_width, far, keys, messages, sums):
     rows, wide = next(iter(messages.values())).shape
     tile = (rows - EXTRA) // 2
     one = pl.BlockSpec((tile, head_width), lambda h, *_: (0, h))
     two = pl.BlockSpec((2, tile, head_width), lambda h, *_: (0, 0, h))
-    cols = pl.BlockSpec((tile, head_width), lambda h, *_: (0, h + first))
+    cols = pl.BlockSpec((2, tile, head_width), lambda h, *_: (0, 0, h + first))
     whole = pl.BlockSpec((rows, head_width), lambda h, *_: (0, h))
     used = sorted({j for _, js in work for j in js})
     slots = [slot for slot, _ in work]
@@ -226,48 +276,57 @@
     for j in used:
         give("message%d" % j, messages[j], whole)
     for slot in slots:
-        give("k%d" % slot, keys[slot][0], cols)
-        give("v%d" % slot, keys[slot][1], cols)
+        give("keys%d" % slot, keys[slot], cols)
     touched = [("q%d" % j, one) for j in used] + [("kv%d" % s, two) for s in slots]
     carried = [name for name, _ in touched if name in sums]
     for name, spec in touched:
         if name in sums:
             give("acc_" + name, sums[name], spec)
-    out_specs, out_shapes = ([], [])
+    out_specs, out_shapes, aliases = ([], [], {})
     for name, spec in touched:
-        names.append("out_" + name)
+        shape = (tile, wide) if name.startswith("q") else (2, tile, wide)
+        if name in last and name in joined:
+            total, begun = joined[name]
+            spec = cols
+            shape = (2, tile, total)
+            if begun is not None:
+                aliases[1 + len(args)] = len(out_specs)
+                give("begun_" + name, begun, pl.BlockSpec(memory_space=pl.ANY))
         out_specs.append(spec)
-        shape = (tile, wide) if name.startswith("q") else (2, tile, wide)
         out_shapes.append(jax.ShapeDtypeStruct(shape, BF16 if name in last else F32))
-    names += ["sum_q%d" % j for j in used]
+    names += ["out_" + name for name, _ in touched]
+    names += ["both"] + ["sum_q%d" % j for j in used]
     pairs = count * sum(len(js) for _, js in work)
     results = pl.pallas_call(
-        functools.partial(stage_kernel, work, names, carried, head_width**-0.5),
+        functools.partial(stage_kernel, work, names, carried, last, head_width**-0.5),
         grid_spec=pltpu.PrefetchScalarGridSpec(
             num_scalar_prefetch=1,
             grid=(count,),
             in_specs=specs,
             out_specs=out_specs,
-            scratch_shapes=[pltpu.VMEM((tile, head_width), F32)] * len(used),
+            scratch_shapes=[pltpu.VMEM((len(used), 2 * tile, 2 * head_width), BF16)]
+            + [pltpu.VMEM((tile, head_width), F32)] * len(used),
         ),
         out_shape=out_shapes,
+        input_output_aliases=aliases,
         compiler_params=pltpu.CompilerParams(vmem_limit_bytes=VMEM_LIMIT),
         cost_estimate=pl.CostEstimate(
-            flops=20 * pairs * tile * tile * head_width,
-            bytes_accessed=40 * tile * wide,
-            transcendentals=pairs * tile * tile,
+            flops=weight * pairs * tile * tile * head_width,
+            bytes_accessed=20 * tile * wide,
+            transcendentals=0,
         ),
         name="pairs",
     )(far, *args)
     return {**sums, **{name: value for (name, _), value in zip(touched, results)}}
 
 
-def finish_kernel(factor, own_q, back_q, own_kv, near, far, *rest):
+def finish_kernel(factor, own_q, from_partner, from_outer, own_kv, near, far, *rest):
     out_q, out_k, out_v = rest[-3:]
-    out_q[...] = (own_q[...] * factor + back_q[...].astype(F32)).astype(BF16)
-    sums = own_kv[...] + near[...].astype(F32) + far[...].astype(F32)
-    out_k[...] = sums[0].astype(BF16)
-    out_v[...] = sums[1].astype(BF16)
+    query = own_q[...] + from_partner[...].astype(F32) + from_outer[...].astype(F32)
+    out_q[...] = (query * factor).astype(BF16)
+    for i, (out, scale) in enumerate(((out_k, factor), (out_v, 1.0))):
+        others = near[i].astype(F32) + far[i].astype(F32)
+        out[...] = (own_kv[i] * scale + others).astype(BF16)
 
 
 def finish(first, count, head_width, full, parts, so_far):
@@ -275,6 +334,13 @@
     wide = count * head_width
     one = pl.BlockSpec((tile, wide), lambda i: (0, 0))
     two = pl.BlockSpec((2, tile, wide), lambda i: (0, 0, 0))
+
+    def part(array):
+        offset = first * head_width if array.shape[2] > wide else 0
+        return pl.BlockSpec(
+            (pl.Element(2), pl.Element(tile), pl.Element(wide)), lambda i: (0, 0, offset)
+        )
+
     cols = pl.BlockSpec(
         (pl.Element(tile), pl.Element(wide)), lambda i: (0, first * head_width)
     )
@@ -282,10 +348,10 @@
     return pl.pallas_call(
         functools.partial(finish_kernel, head_width**-0.5),
         grid=(1,),
-        in_specs=[one, one, two, two, two] + [pl.BlockSpec(memory_space=pl.ANY)] * len(kept),
+        in_specs=[one, one, one, two, part(parts[4]), part(parts[5])] + [pl.BlockSpec(memory_space=pl.ANY)] * len(kept),
         out_specs=[cols] * 3,
         out_shape=[jax.ShapeDtypeStruct((tile, full), BF16)] * 3,
-        input_output_aliases={5 + i: i for i in range(len(kept))},
+        input_output_aliases={6 + i: i for i in range(len(kept))},
         compiler_params=pltpu.CompilerParams(vmem_limit_bytes=VMEM_LIMIT),
         cost_estimate=pl.CostEstimate(
             flops=8 * tile * count * head_width,
@@ -309,7 +375,9 @@
     partner = [(i, i ^ 1) for i in range(rows)]
     onward = [(i, (i + 2) % rows) for i in range(0, rows, 2)]
     onward += [(i, (i - 2) % rows) for i in range(1, rows, 2)]
-    homeward = [(b, a) for a, b in onward]
+    owners = [(0, 0), (rows - 1, rows - 1)]
+    for i in range(1, rows - 1, 2):
+        owners += [(i, i + 1), (i + 1, i)]
     near_pairs = [(i, i ^ 1) for i in range(frames)]
     far_pairs = [(0, 0), (frames - 1, frames - 1)]
     for i in range(1, frames - 1, 2):
@@ -323,80 +391,80 @@
     firsts = [sum(CHUNKS[:c]) for c in range(len(CHUNKS))]
     lse = log_sums.reshape(heads, 1, tile)
     mask = window_mask.reshape(9)
-    near_kv = [lax.ppermute(a, "tm", near_pairs) for a in (k, v)]
+    own_kv = pack(k, v)
+    near_kv = lax.ppermute(own_kv, "tm", near_pairs)
+    far_kv = lax.ppermute(own_kv, "tm", far_pairs)
     make = lambda first, counts, source: prep(
         first, counts, width, (frames, rows), place, mask, source, g, o, lse
     )
     mine = make(0, CHUNKS[:1], q)
     theirs = {0: lax.ppermute(mine[0], "space", partner)}
     mine += make(firsts[1], CHUNKS[1:], after(q, mine[0]))
-    far_kv = [lax.ppermute(after(a, mine[1]), "tm", far_pairs) for a in (k, v)]
-    frames_kv = {HERE: (k, v), NEAR: near_kv, FAR: far_kv}
+    frames_kv = {HERE: own_kv, NEAR: near_kv, FAR: far_kv}
+    last = len(CHUNKS) - 1
     outers = {}
     sums = [{} for _ in CHUNKS]
-    backs = {}
+    backs = [{} for _ in CHUNKS]
     done = []
     out = None
 
-    def stage(c, step):
+    def stage(c, step, *awaited):
         messages = {OUTER: outers.get(c), OWN: mine[c], PARTNER: theirs.get(c)}
-        work = STAGES[step]
+        stages = LATER_STAGES if c else STAGES
+        work = stages[step]
         needed = {j: messages[j] for _, js in work for j in js}
         first_used = min(needed)
-        needed[first_used] = after(needed[first_used], *done[-1:])
-        last = ("q0", "kv1", "kv2") if step + 1 == len(STAGES) else ()
+        arrived = [backs[i][name] for i, name in awaited]
+        needed[first_used] = after(needed[first_used], *done[-1:], *arrived)
+        later = {j for other in stages[step + 1 :] for _, js in other for j in js}
+        slots = {slot for other in stages[step + 1 :] for slot, _ in other}
+        final = {"q%d" % j for j in (OUTER, PARTNER) if j not in later}
+        final |= {"kv%d" % slot for slot in (NEAR, FAR) if slot not in slots}
+        joined = {}
+        if c < last and step + 1 == len(stages):
+            for name in JOINED:
+                joined[name] = (firsts[last] * width, sums[c - 1][name] if c else None)
         sums[c] = run_stage(
-            work, last, firsts[c], CHUNKS[c], width, has_far, frames_kv, needed, sums[c]
+            work, WEIGHTS[c][step], final, joined, firsts[c], CHUNKS[c], width, has_far, frames_kv, needed, sums[c]
         )
         done.append(sums[c]["kv0"])
+        for name, axis, pairs in (
+            ("q0", "space", owners),
+            ("q2", "space", partner),
+            ("kv1", "tm", near_pairs),
+            ("kv2", "tm", far_pairs),
+        ):
+            if name not in final or name not in sums[c] or name in backs[c]:
+                continue
+            if name in joined and c + 1 < last:
+                continue
+            backs[c][name] = lax.ppermute(sums[c][name], axis, pairs)
+            if name in joined:
+                for earlier in range(c):
+                    backs[earlier][name] = backs[c][name]
 
     def hand_on(c):
         outers[c] = lax.ppermute(after(theirs[c], *done[-1:]), "space", onward)
 
-    def send_home(c):
-        backs[c] = [
-            lax.ppermute(sums[c]["q0"], "space", homeward),
-            lax.ppermute(sums[c]["kv1"], "tm", near_pairs),
-            lax.ppermute(sums[c]["kv2"], "tm", far_pairs),
-        ]
-
-    def send_back(c):
-        home = after(backs[c][0], *done[-1:])
-        total = (sums[c]["q2"] + home.astype(F32)) * (width**-0.5)
-        backs[c][0] = lax.ppermute(total.astype(BF16), "space", partner)
-
     def complete(c, so_far):
-        back_q, back_near, back_far = backs[c]
-        back_q = after(back_q, *done[-1:])
-        return finish(
+        back = backs[c]
+        own = after(sums[c]["q1"], *done[-1:])
+        so_far = finish(
             firsts[c], CHUNKS[c], width, full,
-            (sums[c]["q1"], back_q, sums[c]["kv0"], back_near, back_far), so_far,
+            (own, back["q2"], back["q0"], sums[c]["kv0"], back["kv1"], back["kv2"]), so_far,
         )
-
-    last = len(CHUNKS) - 1
-    theirs[1] = lax.ppermute(mine[1], "space", partner)
-    stage(0, 0)
-    stage(1, 0)
-    for c in range(2, len(CHUNKS)):
-        theirs[c] = lax.ppermute(after(mine[c], theirs[c - 2]), "space", partner)
-    hand_on(0)
-    for c in range(2, len(CHUNKS)):
-        stage(c, 0)
-    stage(0, 1)
-    for c in range(len(CHUNKS)):
-        if c < last:
-            hand_on(c + 1)
-        stage(c, 2)
-        send_home(c)
-        if c < last:
-            stage(c + 1, 1)
-            send_back(c)
-        if c >= 2:
-            out = complete(c - 2, out)
-    send_back(last)
-    if last >= 1:
-        out = complete(last - 1, out)
-    out = complete(last, out)
+        done.append(so_far[0])
+        return so_far
+
+    for c in range(1, len(CHUNKS)):
+        theirs[c] = lax.ppermute(mine[c], "space", partner)
+    for kind, c, *rest in ORDER:
+        if kind == "stage":
+            stage(c, *rest)
+        elif kind == "hand":
+            hand_on(c)
+        else:
+            out = complete(c, out)
     return tuple(a.reshape(queries.shape) for a in out)
 
 

time: 142 us -> 221 us (1.56)
  Pallas kernels: 77.9 us -> 168 us
  waiting for transfers between devices: 15.7 us -> 8.22 us
  local copies, waits for them, and re-layouts: 6.03 us -> 0.01 us
  starting transfers between devices: 38.7 us -> 41.4 us
    pallas_call x9 -> x10, Pallas kernels: 70.7 us -> 157 us  [the longest x9 84.9 us: run_stage(): pl.pallas_call(functools.partial(stage_kernel, work, names, carried, last...]
    ppermute x18 -> x16, waiting for transfers between devices: 15.7 us -> 8.2 us  [the longest x12 8.19 us: stage(): backs[c][name] = lax.ppermute(sums[c][name], axis, pairs)]
    unnamed x18 -> x6, local copies, waits for them, and re-layouts: 6.03 us -> 0.01 us
    pallas_call x2, Pallas kernels: 3.56 us -> 7.1 us  [prep(): pl.pallas_call(functools.partial(prep_kernel, counts, *sizes), grid_spec=...]
    ppermute x18 -> x16, starting transfers between devices: 34.5 us -> 37.5 us  [the longest x12 32.3 us: stage(): backs[c][name] = lax.ppermute(sums[c][name], axis, pairs)]
  transfers between devices with their start and end apart: 22 -> 20, of which waited for: 4 -> 1; matrix products, arithmetic and copies ran while one was open for 0% -> 0% of each run, Pallas kernels for 55% -> 43%
where the time goes in v5:
time: 221 us; the launch traced here: 219 us
  Pallas kernels  168 us (76%)
  starting transfers between devices  41.4 us (19%)
  waiting for transfers between devices  8.22 us (4%)
    pallas_call x9, Pallas kernels, run_stage(): pl.pallas_call(functools.partial(stage_kernel, work, names, carried, last...  84.9 us
    pallas_call x1, Pallas kernels, pack(): pl.pallas_call(pack_kernel, in_specs=[anywhere, anywhere], out_specs=anyw...  72.6 us
    ppermute x12, starting transfers between devices, stage(): backs[c][name] = lax.ppermute(sums[c][name], axis, pairs)  32.3 us
    ppermute x12, waiting for transfers between devices, stage(): backs[c][name] = lax.ppermute(sums[c][name], axis, pairs)  8.19 us
    pallas_call x2, Pallas kernels, prep(): pl.pallas_call(functools.partial(prep_kernel, counts, *sizes), grid_spec=...  7.1 us
  transfers between devices with their start and end apart: 20, of which 1 were waited for; matrix products, arithmetic and copies ran while one was open for 0% of the time, Pallas kernels for 43%

profile of v5, /device:TPU:9, one launch (start us, length us, event | category | flops | bytes accessed | tf_op | source)
XLA Modules:
  0.0 218.9 jit_solution(8155566231350308384)
XLA Ops:
  0.7 72.6 %pack.1.refs_1_.refs_3_.refs_2_ = bf16[2,384,1536]{2,1,0:T(8,128)(2,1)} custom-call(bf16[384,1536]{1,0:T(8,128)(2,1)} %bitcast.26, bf16[384,1536]{1,0:T(8,128)(2,1)} %bitcast.27), custom_call_target="tpu_custom_call" | custom-call | bytes 4718592 | tf_op jit(solution)/shard_map/pack/pallas_call | solution.py:153
  73.2 0.7 collective-permute-start.2
  74.0 3.0 %collective-permute-start.5 = (bf16[2,384,1536]{2,1,0:T(8,128)(2,1)}, bf16[2,384,1536]{2,1,0:T(8,128)(2,1)}, u32[]{:S(2)}, u32[]{:S(2)}) collective-permute-start(bf16[2,384,1536]{2,1,0:T(8,128)(2,1)} %pack.1.refs_1_.refs_3_.refs_2_), channel_id=1, source_target_pairs={{0,0},{24,24},{8,16},{16,8},{1,1},{25,25},{9,17},{17,9},{2,2},{26,... | collective-permute-start | bytes 7077896 | tf_op jit(solution)/shard_map/ppermute | solution.py:396
  77.1 3.1 %prep.2.refs_0_.refs_1_ = bf16[800,512]{1,0:T(8,128)(2,1)} custom-call(s32[1]{0:T(128)} %bitcast.1.frame_ref, s32[1]{0:T(128)} %bitcast.2.row_ref, s32[9]{0:T(128)S(1)} %bitcast.15, bf16[384,1536]{1,0:T(8,128)(2,1)} %bitcast.20, bf16[384,1536]{1,0:T(8,128)(2,1)} %bitcast.22, bf16[384,1536]{1,0:T(8,128)(2,1)} %bitcast.24, f32[12,1,384]{2,1,0:T(1,128)S(1)} %bitcast.13), custom_call_target="tpu_custom_call" | custom-call | flops 393216 | bytes 1966080 | tf_op jit(solution)/shard_map/prep/pallas_call | solution.py:113
  80.2 1.2 collective-permute-start.1
  81.4 4.0 %prep.3 = (bf16[800,640]{1,0:T(8,128)(2,1)}, bf16[800,384]{1,0:T(8,128)(2,1)}) custom-call(s32[1]{0:T(128)} %bitcast.1.frame_ref, s32[1]{0:T(128)} %bitcast.2.row_ref, s32[9]{0:T(128)S(1)} %bitcast.16, bf16[384,1536]{1,0:T(8,128)(2,1)} %bitcast.21, bf16[384,1536]{1,0:T(8,128)(2,1)} %bitcast.23, bf16[384,1536]{1,0:T(8,128)(2,1)} %bitcast.25, ...), custom_call_target="tpu_custom_call" | custom-call | flops 786432 | bytes 3932160 | tf_op jit(solution)/shard_map/prep/pallas_call | solution.py:113
  85.4 0.3 collective-permute-start.4
  85.6 1.2 collective-permute-start
  86.9 6.1 %pairs.9 = (f32[384,512]{1,0:T(8,128)S(1)}, f32[2,384,512]{2,1,0:T(8,128)S(1)}, f32[2,384,512]{2,1,0:T(8,128)S(1)}) custom-call(s32[1]{0:T(128)} %bitcast.far_ref, bf16[800,512]{1,0:T(8,128)(2,1)} %prep.2.refs_0_.refs_1_, bf16[2,384,1536]{2,1,0:T(8,128)(2,1)S(1)} %copy-done, bf16[2,384,1536]{2,1,0:T(8,128)(2,1)} %collective-permute-done.2.refs_2_.refs_4_.refs_3_), custom_call_target="tpu_custom_call" | custom-call | flops 6039797760 | bytes 3932160 | tf_op jit(solution)/shard_map/pairs/pallas_call | solution.py:300
  93.0 7.2 %pairs.10 = (f32[384,640]{1,0:T(8,128)S(1)}, f32[2,384,640]{2,1,0:T(8,128)S(1)}, f32[2,384,640]{2,1,0:T(8,128)S(1)}) custom-call(s32[1]{0:T(128)} %bitcast.far_ref, bf16[800,640]{1,0:T(8,128)(2,1)} %get-tuple-element.67.refs_0_.refs_1_, bf16[2,384,1536]{2,1,0:T(8,128)(2,1)S(1)} %copy-done, bf16[2,384,1536]{2,1,0:T(8,128)(2,1)} %collective-permute-done.2.refs_2_.refs_4_.refs_3_), custom_call_target="tpu_custom_call" | custom-call | flops 3774873600 | bytes 4915200 | tf_op jit(solution)/shard_map/pairs/pallas_call | solution.py:300
  100.1 4.7 %pairs.11 = (f32[384,384]{1,0:T(8,128)S(1)}, f32[2,384,384]{2,1,0:T(8,128)S(1)}, f32[2,384,384]{2,1,0:T(8,128)S(1)}) custom-call(s32[1]{0:T(128)} %bitcast.far_ref, bf16[800,384]{1,0:T(8,128)(2,1)} %get-tuple-element.70.refs_0_.refs_1_, bf16[2,384,1536]{2,1,0:T(8,128)(2,1)S(1)} %copy-done, bf16[2,384,1536]{2,1,0:T(8,128)(2,1)} %collective-permute-done.2.refs_2_.refs_4_.refs_3_), custom_call_target="tpu_custom_call" | custom-call | flops 2264924160 | bytes 2949120 | tf_op jit(solution)/shard_map/pairs/pallas_call | solution.py:300
  104.9 1.4 collective-permute-start.3
  106.2 6.3 %pairs.12 = (f32[384,512]{1,0:T(8,128)S(1)}, f32[2,384,512]{2,1,0:T(8,128)S(1)}, f32[2,384,512]{2,1,0:T(8,128)S(1)}) custom-call(s32[1]{0:T(128)} %bitcast.far_ref, bf16[800,512]{1,0:T(8,128)(2,1)} %collective-permute-done.1.refs_0_.refs_2_, bf16[2,384,1536]{2,1,0:T(8,128)(2,1)S(1)} %copy-done, ...), custom_call_target="tpu_custom_call" | custom-call | flops 6039797760 | bytes 3932160 | tf_op jit(solution)/shard_map/pairs/pallas_call | solution.py:300
  112.6 0.0 collective-permute-done.4.refs_0_
  112.6 1.4 collective-permute-start.7
  113.9 0.0 collective-permute-done.5.refs_3_.refs_5_.refs_4_
  113.9 11.6 %pairs.13 = (bf16[384,640]{1,0:T(8,128)(2,1)S(1)}, f32[2,384,640]{2,1,0:T(8,128)S(1)}, f32[2,384,640]{2,1,0:T(8,128)S(1)}, f32[2,384,640]{2,1,0:T(8,128)S(1)}) custom-call(s32[1]{0:T(128)} %bitcast.far_ref, bf16[800,640]{1,0:T(8,128)(2,1)S(1)} %collective-permute-done.4.refs_0_, bf16[2,384,1536]{2,1,0:T(8,128)(2,1)S(1)} %copy-done, ...), custom_call_target="tpu_custom_call" | custom-call | flops 2831155200 | bytes 4915200 | tf_op jit(solution)/shard_map/pairs/pallas_call | solution.py:300
  125.5 1.2 collective-permute-start.12
  126.7 0.0 collective-permute-done.3.refs_0_
  126.7 15.1 %pairs.14 = (bf16[384,512]{1,0:T(8,128)(2,1)S(1)}, f32[384,512]{1,0:T(8,128)S(1)}, bf16[384,512]{1,0:T(8,128)(2,1)S(1)}, f32[2,384,512]{2,1,0:T(8,128)S(1)}, bf1...) custom-call(s32[1]{0:T(128)} %bitcast.far_ref, bf16[800,512]{1,0:T(8,128)(2,1)S(1)} %collective-permute-done.3.refs_0_, ...), custom_call_target="tpu_custom_call" | custom-call | flops 7549747200 | bytes 3932160 | tf_op jit(solution)/shard_map/pairs/pallas_call | solution.py:300
  141.8 0.0 collective-permute-done.refs_0_
  141.8 2.1 collective-permute-start.8
  143.9 11.9 %collective-permute-start.10 = (bf16[2,384,512]{2,1,0:T(8,128)(2,1)S(1)}, bf16[2,384,512]{2,1,0:T(8,128)(2,1)S(1)}, u32[]{:S(2)}, u32[]{:S(2)}) collective-permute-start(bf16[2,384,512]{2,1,0:T(8,128)(2,1)S(1)} %get-tuple-element.93), channel_id=1, source_target_pairs={{0,8},{8,0},{16,24},{24,16},{1,9},{9,1},{17,25},{25,17},{2,10},{10... | collective-permute-start | bytes 2359304 | tf_op jit(solution)/shard_map/ppermute | solution.py:441
  155.8 0.0 collective-permute-start.6
  155.8 7.3 %pairs.15 = (bf16[384,384]{1,0:T(8,128)(2,1)S(1)}, f32[2,384,384]{2,1,0:T(8,128)S(1)}, f32[2,384,384]{2,1,0:T(8,128)S(1)}, f32[2,384,384]{2,1,0:T(8,128)S(1)}) custom-call(s32[1]{0:T(128)} %bitcast.far_ref, bf16[800,384]{1,0:T(8,128)(2,1)} %collective-permute-done.refs_0_, bf16[2,384,1536]{2,1,0:T(8,128)(2,1)S(1)} %copy-done, ...), custom_call_target="tpu_custom_call" | custom-call | flops 6794772480 | bytes 2949120 | tf_op jit(solution)/shard_map/pairs/pallas_call | solution.py:300
  163.1 0.0 collective-permute-done.7.refs_0_
  163.1 0.1 collective-permute-start.9
  163.2 0.0 collective-permute-done.8.from_outer
  163.2 2.2 %collective-permute-start.11 = (bf16[2,384,512]{2,1,0:T(8,128)(2,1)S(1)}, bf16[2,384,512]{2,1,0:T(8,128)(2,1)S(1)}, u32[]{:S(2)}, u32[]{:S(2)}) collective-permute-start(bf16[2,384,512]{2,1,0:T(8,128)(2,1)S(1)} %get-tuple-element.103), channel_id=1, source_target_pairs={{0,0},{24,24},{8,16},{16,8},{1,1},{25,25},{9,17},{17,9},{2,2},{26,... | collective-permute-start | bytes 2359304 | tf_op jit(solution)/shard_map/ppermute | solution.py:441
  165.5 16.4 %pairs.16 = (bf16[384,640]{1,0:T(8,128)(2,1)S(1)}, f32[384,640]{1,0:T(8,128)S(1)}, f32[2,384,640]{2,1,0:T(8,128)S(1)}, bf16[2,384,640]{2,1,0:T(8,128)(2,1)S(1)}, bf16[2,384,640]{2,1,0:T(8,128)(2,1)S(1)}) custom-call(s32[1]{0:T(128)} %bitcast.far_ref, bf16[800,640]{1,0:T(8,128)(2,1)S(1)} %collective-permute-done.7.refs_0_, ...), custom_call_target="tpu_custom_call" | custom-call | flops 7549747200 | bytes 4915200 | tf_op jit(solution)/shard_map/pairs/pallas_call | solution.py:300
  181.9 1.9 collective-permute-start.14
  183.8 0.0 collective-permute-done.6.refs_0_
  183.8 1.9 collective-permute-start.15
  185.7 5.0 %collective-permute-start.13 = (bf16[384,640]{1,0:T(8,128)(2,1)S(1)}, bf16[384,640]{1,0:T(8,128)(2,1)S(1)}, u32[]{:S(2)}, u32[]{:S(2)}) collective-permute-start(bf16[384,640]{1,0:T(8,128)(2,1)S(1)} %get-tuple-element.107), channel_id=1, source_target_pairs={{0,0},{7,7},{1,2},{2,1},{3,4},{4,3},{5,6},{6,5},{8,8},{15,15},{9,1... | collective-permute-start | bytes 1474568 | tf_op jit(solution)/shard_map/ppermute | solution.py:441
  190.7 10.2 %pairs.17 = (bf16[384,384]{1,0:T(8,128)(2,1)S(1)}, f32[384,384]{1,0:T(8,128)S(1)}, f32[2,384,384]{2,1,0:T(8,128)S(1)}, bf16[2,384,384]{2,1,0:T(8,128)(2,1)S(1)}, bf16[2,384,384]{2,1,0:T(8,128)(2,1)S(1)}) custom-call(s32[1]{0:T(128)} %bitcast.far_ref, bf16[800,384]{1,0:T(8,128)(2,1)S(1)} %collective-permute-done.6.refs_0_, ...), custom_call_target="tpu_custom_call" | custom-call | flops 9059696640 | bytes 2949120 | tf_op jit(solution)/shard_map/pairs/pallas_call | solution.py:300
  200.9 0.0 collective-permute-done.12.from_partner
  200.9 0.1 collective-permute-start.18
  201.0 0.0 collective-permute-done.11.far
  201.0 3.9 %collective-permute-start.19 = (bf16[2,384,384]{2,1,0:T(8,128)(2,1)S(1)}, bf16[2,384,384]{2,1,0:T(8,128)(2,1)S(1)}, u32[]{:S(2)}, u32[]{:S(2)}) collective-permute-start(bf16[2,384,384]{2,1,0:T(8,128)(2,1)S(1)} %get-tuple-element.117), channel_id=1, source_target_pairs={{0,0},{24,24},{8,16},{16,8},{1,1},{25,25},{9,17},{17,9},{2,2},{26,... | collective-permute-start | bytes 1769480 | tf_op jit(solution)/shard_map/ppermute | solution.py:441
  205.0 0.1 collective-permute-start.16
  205.0 1.9 collective-permute-start.17
  207.0 1.3 finish.3
  208.3 0.0 collective-permute-done.15.far
  208.3 1.3 finish.4
  209.6 8.2 %collective-permute-done.16.from_partner = bf16[384,384]{1,0:T(8,128)(2,1)S(1)} collective-permute-done((bf16[384,384]{1,0:T(8,128)(2,1)S(1)}, bf16[384,384]{1,0:T(8,128)(2,1)S(1)}, u32[]{:S(2)}, u32[]{:S(2)}) %collective-permute-start.16) | collective-permute-done | bytes 294944 | tf_op jit(solution)/shard_map/ppermute | solution.py:441
  217.8 0.0 collective-permute-done.17.from_outer
  217.8 0.0 collective-permute-done.18.near
  217.8 1.1 finish.5
  (13 shorter events, 0.0 us)
Async XLA Ops:
  0.6 76.4 %copy-start.1 = (f32[1,1,12,384]{3,1,2,0:T(1,128)S(1)}, f32[1,1,12,384]{3,1,2,0:T(1,128)}, u32[]{:S(2)}) copy-start(f32[1,1,12,384]{3,1,2,0:T(1,128)} %param.12) | copy-start | bytes 55300
  0.6 76.4 %copy-start.2 = (s32[1,1,9]{2,1,0:T(1,128)S(1)}, s32[1,1,9]{2,1,0:T(1,128)}, u32[]{:S(2)}) copy-start(s32[1,1,9]{2,1,0:T(1,128)} %param.13) | copy-start | bytes 112
  73.2 13.6 %collective-permute-start.2 = (bf16[2,384,1536]{2,1,0:T(8,128)(2,1)}, bf16[2,384,1536]{2,1,0:T(8,128)(2,1)}, u32[]{:S(2)}, u32[]{:S(2)}) collective-permute-start(bf16[2,384,1536]{2,1,0:T(8,128)(2,1)} %pack.1.refs_1_.refs_3_.refs_2_), channel_id=1, source_target_pairs={{0,8},{8,0},{16,24},{24,16},{1,9},{9,1},{17,25},{25,17},{2,10},{10... | collective-permute-start | bytes 7077896 | tf_op jit(solution)/shard_map/ppermute | solution.py:395
  74.0 39.9 %collective-permute-start.5 = (bf16[2,384,1536]{2,1,0:T(8,128)(2,1)}, bf16[2,384,1536]{2,1,0:T(8,128)(2,1)}, u32[]{:S(2)}, u32[]{:S(2)}) collective-permute-start(bf16[2,384,1536]{2,1,0:T(8,128)(2,1)} %pack.1.refs_1_.refs_3_.refs_2_), channel_id=1, source_target_pairs={{0,0},{24,24},{8,16},{16,8},{1,1},{25,25},{9,17},{17,9},{2,2},{26,... | collective-permute-start | bytes 7077896 | tf_op jit(solution)/shard_map/ppermute | solution.py:396
  80.2 6.7 %copy-start = (bf16[2,384,1536]{2,1,0:T(8,128)(2,1)S(1)}, bf16[2,384,1536]{2,1,0:T(8,128)(2,1)}, u32[]{:S(2)}) copy-start(bf16[2,384,1536]{2,1,0:T(8,128)(2,1)} %pack.1.refs_1_.refs_3_.refs_2_) | copy-start | bytes 7077892
  80.2 24.7 %collective-permute-start.1 = (bf16[800,512]{1,0:T(8,128)(2,1)}, bf16[800,512]{1,0:T(8,128)(2,1)}, u32[]{:S(2)}, u32[]{:S(2)}) collective-permute-start(bf16[800,512]{1,0:T(8,128)(2,1)} %prep.2.refs_0_.refs_1_), channel_id=1, source_target_pairs={{0,1},{1,0},{2,3},{3,2},{4,5},{5,4},{6,7},{7,6},{8,9},{9,8},{10,11... | collective-permute-start | bytes 2457608 | tf_op jit(solution)/shard_map/ppermute | solution.py:401
  85.4 27.2 %collective-permute-start.4 = (bf16[800,640]{1,0:T(8,128)(2,1)}, bf16[800,640]{1,0:T(8,128)(2,1)S(1)}, u32[]{:S(2)}, u32[]{:S(2)}) collective-permute-start(bf16[800,640]{1,0:T(8,128)(2,1)} %get-tuple-element.67.refs_0_.refs_1_), channel_id=1, source_target_pairs={{0,1},{1,0},{2,3},{3,2},{4,5},{5,4},{6,7},{7,6},{8,9},{9,8},{10,11... | collective-permute-start | bytes 3072008 | tf_op jit(solution)/shard_map/ppermute | solution.py:460
  85.6 56.2 %collective-permute-start = (bf16[800,384]{1,0:T(8,128)(2,1)}, bf16[800,384]{1,0:T(8,128)(2,1)}, u32[]{:S(2)}, u32[]{:S(2)}) collective-permute-start(bf16[800,384]{1,0:T(8,128)(2,1)} %get-tuple-element.70.refs_0_.refs_1_), channel_id=1, source_target_pairs={{0,1},{1,0},{2,3},{3,2},{4,5},{5,4},{6,7},{7,6},{8,9},{9,8},{10,11... | collective-permute-start | bytes 1843208 | tf_op jit(solution)/shard_map/ppermute | solution.py:460
  104.9 21.9 %collective-permute-start.3 = (bf16[800,512]{1,0:T(8,128)(2,1)}, bf16[800,512]{1,0:T(8,128)(2,1)S(1)}, u32[]{:S(2)}, u32[]{:S(2)}) collective-permute-start(bf16[800,512]{1,0:T(8,128)(2,1)} %collective-permute-done.1.refs_0_.refs_2_), channel_id=1, source_target_pairs={{0,2},{2,4},{4,6},{6,0},{1,7},{3,1},{5,3},{7,5},{8,10},{10,12},{12... | collective-permute-start | bytes 2457608 | tf_op jit(solution)/shard_map/ppermute | solution.py:447
  112.6 50.6 %collective-permute-start.7 = (bf16[800,640]{1,0:T(8,128)(2,1)S(1)}, bf16[800,640]{1,0:T(8,128)(2,1)S(1)}, u32[]{:S(2)}, u32[]{:S(2)}) collective-permute-start(bf16[800,640]{1,0:T(8,128)(2,1)S(1)} %collective-permute-done.4.refs_0_), channel_id=1, source_target_pairs={{0,2},{2,4},{4,6},{6,0},{1,7},{3,1},{5,3},{7,5},{8,10},{10,12},{12... | collective-permute-start | bytes 3072008 | tf_op jit(solution)/shard_map/ppermute | solution.py:447
  125.5 75.4 %collective-permute-start.12 = (bf16[384,640]{1,0:T(8,128)(2,1)S(1)}, bf16[384,640]{1,0:T(8,128)(2,1)S(1)}, u32[]{:S(2)}, u32[]{:S(2)}) collective-permute-start(bf16[384,640]{1,0:T(8,128)(2,1)S(1)} %get-tuple-element.106), channel_id=1, source_target_pairs={{0,1},{1,0},{2,3},{3,2},{4,5},{5,4},{6,7},{7,6},{8,9},{9,8},{10,11... | collective-permute-start | bytes 1474568 | tf_op jit(solution)/shard_map/ppermute | solution.py:441
  141.8 21.4 %collective-permute-start.8 = (bf16[384,512]{1,0:T(8,128)(2,1)S(1)}, bf16[384,512]{1,0:T(8,128)(2,1)S(1)}, u32[]{:S(2)}, u32[]{:S(2)}) collective-permute-start(bf16[384,512]{1,0:T(8,128)(2,1)S(1)} %get-tuple-element.86), channel_id=1, source_target_pairs={{0,0},{7,7},{1,2},{2,1},{3,4},{4,3},{5,6},{6,5},{8,8},{15,15},{9,1... | collective-permute-start | bytes 1179656 | tf_op jit(solution)/shard_map/ppermute | solution.py:441
  143.9 41.8 %collective-permute-start.10 = (bf16[2,384,512]{2,1,0:T(8,128)(2,1)S(1)}, bf16[2,384,512]{2,1,0:T(8,128)(2,1)S(1)}, u32[]{:S(2)}, u32[]{:S(2)}) collective-permute-start(bf16[2,384,512]{2,1,0:T(8,128)(2,1)S(1)} %get-tuple-element.93), channel_id=1, source_target_pairs={{0,8},{8,0},{16,24},{24,16},{1,9},{9,1},{17,25},{25,17},{2,10},{10... | collective-permute-start | bytes 2359304 | tf_op jit(solution)/shard_map/ppermute | solution.py:441
  155.8 27.9 %collective-permute-start.6 = (bf16[800,384]{1,0:T(8,128)(2,1)}, bf16[800,384]{1,0:T(8,128)(2,1)S(1)}, u32[]{:S(2)}, u32[]{:S(2)}) collective-permute-start(bf16[800,384]{1,0:T(8,128)(2,1)} %collective-permute-done.refs_0_), channel_id=1, source_target_pairs={{0,2},{2,4},{4,6},{6,0},{1,7},{3,1},{5,3},{7,5},{8,10},{10,12},{12... | collective-permute-start | bytes 1843208 | tf_op jit(solution)/shard_map/ppermute | solution.py:447
  163.1 18.8 %collective-permute-start.9 = (bf16[384,512]{1,0:T(8,128)(2,1)S(1)}, bf16[384,512]{1,0:T(8,128)(2,1)S(1)}, u32[]{:S(2)}, u32[]{:S(2)}) collective-permute-start(bf16[384,512]{1,0:T(8,128)(2,1)S(1)} %get-tuple-element.92), channel_id=1, source_target_pairs={{0,1},{1,0},{2,3},{3,2},{4,5},{5,4},{6,7},{7,6},{8,9},{9,8},{10,11... | collective-permute-start | bytes 1179656 | tf_op jit(solution)/shard_map/ppermute | solution.py:441
  163.2 37.8 %collective-permute-start.11 = (bf16[2,384,512]{2,1,0:T(8,128)(2,1)S(1)}, bf16[2,384,512]{2,1,0:T(8,128)(2,1)S(1)}, u32[]{:S(2)}, u32[]{:S(2)}) collective-permute-start(bf16[2,384,512]{2,1,0:T(8,128)(2,1)S(1)} %get-tuple-element.103), channel_id=1, source_target_pairs={{0,0},{24,24},{8,16},{16,8},{1,1},{25,25},{9,17},{17,9},{2,2},{26,... | collective-permute-start | bytes 2359304 | tf_op jit(solution)/shard_map/ppermute | solution.py:441
  181.9 23.1 %collective-permute-start.14 = (bf16[2,384,640]{2,1,0:T(8,128)(2,1)S(1)}, bf16[2,384,640]{2,1,0:T(8,128)(2,1)S(1)}, u32[]{:S(2)}, u32[]{:S(2)}) collective-permute-start(bf16[2,384,640]{2,1,0:T(8,128)(2,1)S(1)} %get-tuple-element.108), channel_id=1, source_target_pairs={{0,8},{8,0},{16,24},{24,16},{1,9},{9,1},{17,25},{25,17},{2,10},{10... | collective-permute-start | bytes 2949128 | tf_op jit(solution)/shard_map/ppermute | solution.py:441
  183.8 24.5 %collective-permute-start.15 = (bf16[2,384,640]{2,1,0:T(8,128)(2,1)S(1)}, bf16[2,384,640]{2,1,0:T(8,128)(2,1)S(1)}, u32[]{:S(2)}, u32[]{:S(2)}) collective-permute-start(bf16[2,384,640]{2,1,0:T(8,128)(2,1)S(1)} %get-tuple-element.109), channel_id=1, source_target_pairs={{0,0},{24,24},{8,16},{16,8},{1,1},{25,25},{9,17},{17,9},{2,2},{26,... | collective-permute-start | bytes 2949128 | tf_op jit(solution)/shard_map/ppermute | solution.py:441
  185.7 19.2 %collective-permute-start.13 = (bf16[384,640]{1,0:T(8,128)(2,1)S(1)}, bf16[384,640]{1,0:T(8,128)(2,1)S(1)}, u32[]{:S(2)}, u32[]{:S(2)}) collective-permute-start(bf16[384,640]{1,0:T(8,128)(2,1)S(1)} %get-tuple-element.107), channel_id=1, source_target_pairs={{0,0},{7,7},{1,2},{2,1},{3,4},{4,3},{5,6},{6,5},{8,8},{15,15},{9,1... | collective-permute-start | bytes 1474568 | tf_op jit(solution)/shard_map/ppermute | solution.py:441
  200.9 16.9 %collective-permute-start.18 = (bf16[2,384,384]{2,1,0:T(8,128)(2,1)S(1)}, bf16[2,384,384]{2,1,0:T(8,128)(2,1)S(1)}, u32[]{:S(2)}, u32[]{:S(2)}) collective-permute-start(bf16[2,384,384]{2,1,0:T(8,128)(2,1)S(1)} %get-tuple-element.116), channel_id=1, source_target_pairs={{0,8},{8,0},{16,24},{24,16},{1,9},{9,1},{17,25},{25,17},{2,10},{10... | collective-permute-start | bytes 1769480 | tf_op jit(solution)/shard_map/ppermute | solution.py:441
  201.0 16.8 %collective-permute-start.19 = (bf16[2,384,384]{2,1,0:T(8,128)(2,1)S(1)}, bf16[2,384,384]{2,1,0:T(8,128)(2,1)S(1)}, u32[]{:S(2)}, u32[]{:S(2)}) collective-permute-start(bf16[2,384,384]{2,1,0:T(8,128)(2,1)S(1)} %get-tuple-element.117), channel_id=1, source_target_pairs={{0,0},{24,24},{8,16},{16,8},{1,1},{25,25},{9,17},{17,9},{2,2},{26,... | collective-permute-start | bytes 1769480 | tf_op jit(solution)/shard_map/ppermute | solution.py:441
  205.0 12.8 %collective-permute-start.16 = (bf16[384,384]{1,0:T(8,128)(2,1)S(1)}, bf16[384,384]{1,0:T(8,128)(2,1)S(1)}, u32[]{:S(2)}, u32[]{:S(2)}) collective-permute-start(bf16[384,384]{1,0:T(8,128)(2,1)S(1)} %get-tuple-element.114), channel_id=1, source_target_pairs={{0,1},{1,0},{2,3},{3,2},{4,5},{5,4},{6,7},{7,6},{8,9},{9,8},{10,11... | collective-permute-start | bytes 884744 | tf_op jit(solution)/shard_map/ppermute | solution.py:441
  205.0 12.8 %collective-permute-start.17 = (bf16[384,384]{1,0:T(8,128)(2,1)S(1)}, bf16[384,384]{1,0:T(8,128)(2,1)S(1)}, u32[]{:S(2)}, u32[]{:S(2)}) collective-permute-start(bf16[384,384]{1,0:T(8,128)(2,1)S(1)} %get-tuple-element.115), channel_id=1, source_target_pairs={{0,0},{7,7},{1,2},{2,1},{3,4},{4,3},{5,6},{6,5},{8,8},{15,15},{9,1... | collective-permute-start | bytes 884744 | tf_op jit(solution)/shard_map/ppermute | solution.py:441

commit v6 on v5

--- a/solution.py
+++ b/solution.py
@@ -137,28 +137,24 @@
     )(*place, mask, *(pltpu.with_memory_space_constraint(a, pltpu.HBM) for a in (q, g, o)), lse)
 
 
-def pack_kernel(k_ref, v_ref, out, sems):
-    copies = [
-        pltpu.make_async_copy(source, out.at[i], sems.at[i])
-        for i, source in enumerate((k_ref, v_ref))
-    ]
-    for copy in copies:
-        copy.start()
-    for copy in copies:
-        copy.wait()
-
-
-def pack(k, v):
-    anywhere = pl.BlockSpec(memory_space=pl.ANY)
+def pack_kernel(k_ref, v_ref, out):
+    out[0] = k_ref[...]
+    out[1] = v_ref[...]
+
+
+def pack(k, v, steps=2):
+    tile, full = k.shape
+    cols = pl.BlockSpec((tile, full // steps), lambda i: (0, i))
     return pl.pallas_call(
         pack_kernel,
-        in_specs=[anywhere, anywhere],
-        out_specs=anywhere,
-        out_shape=jax.ShapeDtypeStruct((2,) + k.shape, k.dtype),
-        scratch_shapes=[pltpu.SemaphoreType.DMA((2,))],
+        grid=(steps,),
+        in_specs=[cols, cols],
+        out_specs=pl.BlockSpec((2, tile, full // steps), lambda i: (0, 0, i)),
+        out_shape=jax.ShapeDtypeStruct((2, tile, full), k.dtype),
+        compiler_params=pltpu.CompilerParams(vmem_limit_bytes=VMEM_LIMIT),
         cost_estimate=pl.CostEstimate(flops=0, bytes_accessed=8 * k.size, transcendentals=0),
         name="pack",
-    )(k, v)
+    )(*(pltpu.with_memory_space_constraint(a, pltpu.HBM) for a in (k, v)))
 
 
 def row_stats(message, tile):
@@ -178,18 +174,9 @@
     env = dict(zip(names, refs))
     tile = env["message%d" % work[0][1][0]].shape[0] - EXTRA
     tile //= 2
-    width = env["both"].shape[2] // 2
+    width = env["message%d" % work[0][1][0]].shape[1]
     used = sorted({j for _, js in work for j in js})
     stats = {j: row_stats(env["message%d" % j], tile) for j in used}
-    both = {j: env["both"].at[i] for i, j in enumerate(used)}
-
-    @pl.when(pl.program_id(0) == 0)
-    def _():
-        env["both"][...] = jnp.zeros_like(env["both"])
-
-    for j in used:
-        both[j][0:tile, 0:width] = env["message%d" % j][0:tile, :]
-        both[j][tile:, width:] = env["message%d" % j][tile : 2 * tile, :]
     started = set()
 
     def add_q(j, term):
@@ -202,20 +189,30 @@
             env["sum_" + name][...] = term
         started.add(name)
 
-    def pair(slot, j):
+    def operands(slot, j):
+        message = env["message%d" % j]
+        return (message[0:tile, :], message[tile : 2 * tile, :], env["keys%d" % slot])
+
+    def products(slot, j):
+        qj, gj, keys = operands(slot, j)
+        return (dot(keys[0], qj, ((1,), (1,))), dot(keys[1], gj, ((1,), (1,))))
+
+    def terms_of(slot, j, scores, grad_prob):
+        qj, gj, keys = operands(slot, j)
         shift, delta, flags = stats[j]
         lane = 3 * j + slot
         shift = jnp.where(flags[:, lane : lane + 1] > 0, shift, FAR_AWAY)
-        keys = jnp.concatenate((env["keys%d" % slot][0], env["keys%d" % slot][1]), axis=1)
-        products = dot(keys, both[j][...], ((1,), (1,)))
-        weights = jnp.exp2(products[:, :tile] * (factor * LOG2E) - shift)
-        grad_score = (weights * (products[:, tile:] - delta)).astype(BF16)
-        joint = jnp.concatenate((grad_score, weights.astype(BF16)), axis=1)
-        return (grad_score, dot(joint, both[j][...], ((1,), (0,))))
+        weights = jnp.exp2(scores * (factor * LOG2E) - shift)
+        grad_score = (weights * (grad_prob - delta)).astype(BF16)
+        return (
+            dot(grad_score, keys[0], ((0,), (0,))),
+            dot(grad_score, qj, ((1,), (0,))),
+            dot(weights.astype(BF16), gj, ((1,), (0,))),
+        )
 
     def put_keys(slot, terms):
         name = "kv%d" % slot
-        dk, dv = (terms[:, :width], terms[:, width:])
+        dk, dv = terms
         if "acc_" + name in env:
             dk, dv = (dk + env["acc_" + name][0], dv + env["acc_" + name][1])
         out = env["out_" + name]
@@ -223,18 +220,18 @@
         out[1] = dv.astype(out.dtype)
 
     def frames(slots, js):
-        terms = {}
-        for j in js:
-            scores = []
-            for slot in slots:
-                grad_score, term = pair(slot, j)
-                terms[slot] = term if slot not in terms else terms[slot] + term
-                scores.append(grad_score)
-            keys = [env["keys%d" % slot][0] for slot in slots]
-            joint = [jnp.concatenate(a, axis=0) if len(slots) > 1 else a[0] for a in (scores, keys)]
-            add_q(j, dot(*joint, ((0,), (0,))))
+        todo = [(slot, j) for slot in slots for j in js]
+        sums = {}
+        ahead = products(*todo[0])
+        for i, (slot, j) in enumerate(todo):
+            now, ahead = (ahead, products(*todo[i + 1]) if i + 1 < len(todo) else None)
+            term_q, term_k, term_v = terms_of(slot, j, *now)
+            add_q(j, term_q)
+            if slot in sums:
+                term_k, term_v = (term_k + sums[slot][0], term_v + sums[slot][1])
+            sums[slot] = (term_k, term_v)
         for slot in slots:
-            put_keys(slot, terms[slot])
+            put_keys(slot, sums[slot])
 
     near = [slot for slot, _ in work if slot != FAR]
     frames(near, work[0][1])
@@ -295,7 +292,7 @@
         out_specs.append(spec)
         out_shapes.append(jax.ShapeDtypeStruct(shape, BF16 if name in last else F32))
     names += ["out_" + name for name, _ in touched]
-    names += ["both"] + ["sum_q%d" % j for j in used]
+    names += ["sum_q%d" % j for j in used]
     pairs = count * sum(len(js) for _, js in work)
     results = pl.pallas_call(
         functools.partial(stage_kernel, work, names, carried, last, head_width**-0.5),
@@ -304,8 +301,7 @@
             grid=(count,),
             in_specs=specs,
             out_specs=out_specs,
-            scratch_shapes=[pltpu.VMEM((len(used), 2 * tile, 2 * head_width), BF16)]
-            + [pltpu.VMEM((tile, head_width), F32)] * len(used),
+            scratch_shapes=[pltpu.VMEM((tile, head_width), F32)] * len(used),
         ),
         out_shape=out_shapes,
         input_output_aliases=aliases,

time: 221 us -> 152 us (0.69)
  the two profiles are of different devices: /device:TPU:9 before, /device:TPU:24 now
where the time goes in v6:
time: 152 us; the launch traced here: 151 us
  Pallas kernels  68.1 us (45%)
  starting transfers between devices  52.4 us (34%)
  waiting for transfers between devices  29.8 us (20%)
    pallas_call x9, Pallas kernels, run_stage(): pl.pallas_call(functools.partial(stage_kernel, work, names, carried, last...  55.6 us
    ppermute x12, starting transfers between devices, stage(): backs[c][name] = lax.ppermute(sums[c][name], axis, pairs)  45.5 us
    ppermute x12, waiting for transfers between devices, stage(): backs[c][name] = lax.ppermute(sums[c][name], axis, pairs)  17.8 us
    ppermute x2, waiting for transfers between devices, per_device(): theirs[c] = lax.ppermute(mine[c], 'space', partner)  12 us
    pallas_call x2, Pallas kernels, prep(): pl.pallas_call(functools.partial(prep_kernel, counts, *sizes), grid_spec=...  7.1 us
    pallas_call x3, Pallas kernels, finish(): pl.pallas_call(functools.partial(finish_kernel, head_width ** (-0.5)), gr...  3.71 us
  transfers between devices with their start and end apart: 20, of which 4 were waited for; matrix products, arithmetic and copies ran while one was open for 0% of the time, Pallas kernels for 43%

profile of v6, /device:TPU:24, one launch (start us, length us, event | category | flops | bytes accessed | tf_op | source)
XLA Modules:
  0.0 151.1 jit_solution(2027911447606632992)
XLA Ops:
  0.7 1.8 %pack.1.refs_1_.refs_3_.refs_2_ = bf16[2,384,1536]{2,1,0:T(8,128)(2,1)S(1)} custom-call(bf16[384,1536]{1,0:T(8,128)(2,1)} %bitcast.26, bf16[384,1536]{1,0:T(8,128)(2,1)} %bitcast.27), custom_call_target="tpu_custom_call" | custom-call | bytes 4718592 | tf_op jit(solution)/shard_map/pack/pallas_call | solution.py:148
  2.4 0.1 collective-permute-start.2
  2.5 2.1 %collective-permute-start.5 = (bf16[2,384,1536]{2,1,0:T(8,128)(2,1)S(1)}, bf16[2,384,1536]{2,1,0:T(8,128)(2,1)}, u32[]{:S(2)}, u32[]{:S(2)}) collective-permute-start(bf16[2,384,1536]{2,1,0:T(8,128)(2,1)S(1)} %pack.1.refs_1_.refs_3_.refs_2_), channel_id=1, source_target_pairs={{0,0},{24,24},{8,16},{16,8},{1,1},{25,25},{9,17},{17,9},{2,2},{26,... | collective-permute-start | bytes 7077896 | tf_op jit(solution)/shard_map/ppermute | solution.py:392
  4.6 3.1 %prep.2.refs_0_.refs_1_ = bf16[800,512]{1,0:T(8,128)(2,1)} custom-call(s32[1]{0:T(128)} %bitcast.1.frame_ref, s32[1]{0:T(128)} %bitcast.2.row_ref, s32[9]{0:T(128)S(1)} %bitcast.15, bf16[384,1536]{1,0:T(8,128)(2,1)} %bitcast.20, bf16[384,1536]{1,0:T(8,128)(2,1)} %bitcast.22, bf16[384,1536]{1,0:T(8,128)(2,1)} %bitcast.24, f32[12,1,384]{2,1,0:T(1,128)S(1)} %bitcast.13), custom_call_target="tpu_custom_call" | custom-call | flops 393216 | bytes 1966080 | tf_op jit(solution)/shard_map/prep/pallas_call | solution.py:113
  7.7 1.5 collective-permute-start.1
  9.2 4.0 %prep.3 = (bf16[800,640]{1,0:T(8,128)(2,1)}, bf16[800,384]{1,0:T(8,128)(2,1)}) custom-call(s32[1]{0:T(128)} %bitcast.1.frame_ref, s32[1]{0:T(128)} %bitcast.2.row_ref, s32[9]{0:T(128)S(1)} %bitcast.16, bf16[384,1536]{1,0:T(8,128)(2,1)} %bitcast.21, bf16[384,1536]{1,0:T(8,128)(2,1)} %bitcast.23, bf16[384,1536]{1,0:T(8,128)(2,1)} %bitcast.25, ...), custom_call_target="tpu_custom_call" | custom-call | flops 786432 | bytes 3932160 | tf_op jit(solution)/shard_map/prep/pallas_call | solution.py:113
  13.2 0.5 collective-permute-start.4
  13.7 1.5 collective-permute-start
  15.2 0.0 collective-permute-done.2.refs_2_.refs_4_.refs_3_
  15.2 5.8 %pairs.9 = (f32[384,512]{1,0:T(8,128)S(1)}, f32[2,384,512]{2,1,0:T(8,128)S(1)}, f32[2,384,512]{2,1,0:T(8,128)S(1)}) custom-call(s32[1]{0:T(128)} %bitcast.far_ref, bf16[800,512]{1,0:T(8,128)(2,1)} %prep.2.refs_0_.refs_1_, bf16[2,384,1536]{2,1,0:T(8,128)(2,1)S(1)} %pack.1.refs_1_.refs_3_.refs_2_, ...), custom_call_target="tpu_custom_call" | custom-call | flops 6039797760 | bytes 3932160 | tf_op jit(solution)/shard_map/pairs/pallas_call | solution.py:297
  21.1 6.8 %pairs.10 = (f32[384,640]{1,0:T(8,128)S(1)}, f32[2,384,640]{2,1,0:T(8,128)S(1)}, f32[2,384,640]{2,1,0:T(8,128)S(1)}) custom-call(s32[1]{0:T(128)} %bitcast.far_ref, bf16[800,640]{1,0:T(8,128)(2,1)} %get-tuple-element.67.refs_0_.refs_1_, bf16[2,384,1536]{2,1,0:T(8,128)(2,1)S(1)} %pack.1.refs_1_.refs_3_.refs_2_, ...), custom_call_target="tpu_custom_call" | custom-call | flops 3774873600 | bytes 4915200 | tf_op jit(solution)/shard_map/pairs/pallas_call | solution.py:297
  27.9 4.5 %pairs.11 = (f32[384,384]{1,0:T(8,128)S(1)}, f32[2,384,384]{2,1,0:T(8,128)S(1)}, f32[2,384,384]{2,1,0:T(8,128)S(1)}) custom-call(s32[1]{0:T(128)} %bitcast.far_ref, bf16[800,384]{1,0:T(8,128)(2,1)} %get-tuple-element.70.refs_0_.refs_1_, bf16[2,384,1536]{2,1,0:T(8,128)(2,1)S(1)} %pack.1.refs_1_.refs_3_.refs_2_, ...), custom_call_target="tpu_custom_call" | custom-call | flops 2264924160 | bytes 2949120 | tf_op jit(solution)/shard_map/pairs/pallas_call | solution.py:297
  32.4 0.0 collective-permute-done.1.refs_0_.refs_2_
  32.4 0.3 collective-permute-start.3
  32.7 5.9 %pairs.12 = (f32[384,512]{1,0:T(8,128)S(1)}, f32[2,384,512]{2,1,0:T(8,128)S(1)}, f32[2,384,512]{2,1,0:T(8,128)S(1)}) custom-call(s32[1]{0:T(128)} %bitcast.far_ref, bf16[800,512]{1,0:T(8,128)(2,1)} %collective-permute-done.1.refs_0_.refs_2_, bf16[2,384,1536]{2,1,0:T(8,128)(2,1)S(1)} %pack.1.refs_1_.refs_3_.refs_2_, ...), custom_call_target="tpu_custom_call" | custom-call | flops 6039797760 | bytes 3932160 | tf_op jit(solution)/shard_map/pairs/pallas_call | solution.py:297
  38.6 12.0 %collective-permute-done.4.refs_0_ = bf16[800,640]{1,0:T(8,128)(2,1)S(1)} collective-permute-done((bf16[800,640]{1,0:T(8,128)(2,1)}, bf16[800,640]{1,0:T(8,128)(2,1)S(1)}, u32[]{:S(2)}, u32[]{:S(2)}) %collective-permute-start.4) | collective-permute-done | bytes 1024032 | tf_op jit(solution)/shard_map/ppermute | solution.py:456
  50.5 0.0 collective-permute-start.7
  50.5 0.0 collective-permute-done.5.refs_3_.refs_5_.refs_4_
  50.5 7.5 %pairs.13 = (bf16[384,640]{1,0:T(8,128)(2,1)S(1)}, f32[2,384,640]{2,1,0:T(8,128)S(1)}, f32[2,384,640]{2,1,0:T(8,128)S(1)}, f32[2,384,640]{2,1,0:T(8,128)S(1)}) custom-call(s32[1]{0:T(128)} %bitcast.far_ref, bf16[800,640]{1,0:T(8,128)(2,1)S(1)} %collective-permute-done.4.refs_0_, bf16[2,384,1536]{2,1,0:T(8,128)(2,1)S(1)} %pack.1.refs_1_.refs_3_.refs_2_, ...), custom_call_target="tpu_custom_call" | custom-call | flops 2831155200 | bytes 4915200 | tf_op jit(solution)/shard_map/pairs/pallas_call | solution.py:297
  58.0 2.0 %collective-permute-start.12 = (bf16[384,640]{1,0:T(8,128)(2,1)S(1)}, bf16[384,640]{1,0:T(8,128)(2,1)S(1)}, u32[]{:S(2)}, u32[]{:S(2)}) collective-permute-start(bf16[384,640]{1,0:T(8,128)(2,1)S(1)} %get-tuple-element.106), channel_id=1, source_target_pairs={{0,1},{1,0},{2,3},{3,2},{4,5},{5,4},{6,7},{7,6},{8,9},{9,8},{10,11... | collective-permute-start | bytes 1474568 | tf_op jit(solution)/shard_map/ppermute | solution.py:437
  60.0 0.0 collective-permute-done.3.refs_0_
  60.0 7.1 %pairs.14 = (bf16[384,512]{1,0:T(8,128)(2,1)S(1)}, f32[384,512]{1,0:T(8,128)S(1)}, bf16[384,512]{1,0:T(8,128)(2,1)S(1)}, f32[2,384,512]{2,1,0:T(8,128)S(1)}, bf1...) custom-call(s32[1]{0:T(128)} %bitcast.far_ref, bf16[800,512]{1,0:T(8,128)(2,1)S(1)} %collective-permute-done.3.refs_0_, ...), custom_call_target="tpu_custom_call" | custom-call | flops 7549747200 | bytes 3932160 | tf_op jit(solution)/shard_map/pairs/pallas_call | solution.py:297
  67.1 0.0 collective-permute-done.refs_0_
  67.1 3.5 %collective-permute-start.8 = (bf16[384,512]{1,0:T(8,128)(2,1)S(1)}, bf16[384,512]{1,0:T(8,128)(2,1)S(1)}, u32[]{:S(2)}, u32[]{:S(2)}) collective-permute-start(bf16[384,512]{1,0:T(8,128)(2,1)S(1)} %get-tuple-element.86), channel_id=1, source_target_pairs={{0,0},{7,7},{1,2},{2,1},{3,4},{4,3},{5,6},{6,5},{8,8},{15,15},{9,1... | collective-permute-start | bytes 1179656 | tf_op jit(solution)/shard_map/ppermute | solution.py:437
  70.6 9.3 %collective-permute-start.10 = (bf16[2,384,512]{2,1,0:T(8,128)(2,1)S(1)}, bf16[2,384,512]{2,1,0:T(8,128)(2,1)S(1)}, u32[]{:S(2)}, u32[]{:S(2)}) collective-permute-start(bf16[2,384,512]{2,1,0:T(8,128)(2,1)S(1)} %get-tuple-element.93), channel_id=1, source_target_pairs={{0,8},{8,0},{16,24},{24,16},{1,9},{9,1},{17,25},{25,17},{2,10},{10... | collective-permute-start | bytes 2359304 | tf_op jit(solution)/shard_map/ppermute | solution.py:437
  79.9 0.9 collective-permute-start.6
  80.8 4.8 %pairs.15 = (bf16[384,384]{1,0:T(8,128)(2,1)S(1)}, f32[2,384,384]{2,1,0:T(8,128)S(1)}, f32[2,384,384]{2,1,0:T(8,128)S(1)}, f32[2,384,384]{2,1,0:T(8,128)S(1)}) custom-call(s32[1]{0:T(128)} %bitcast.far_ref, bf16[800,384]{1,0:T(8,128)(2,1)} %collective-permute-done.refs_0_, bf16[2,384,1536]{2,1,0:T(8,128)(2,1)S(1)} %pack.1.refs_1_.refs_3_.refs_2_, ...), custom_call_target="tpu_custom_call" | custom-call | flops 6794772480 | bytes 2949120 | tf_op jit(solution)/shard_map/pairs/pallas_call | solution.py:297
  85.6 1.1 collective-permute-start.9
  86.7 0.7 collective-permute-start.11
  87.4 8.0 %pairs.16 = (bf16[384,640]{1,0:T(8,128)(2,1)S(1)}, f32[384,640]{1,0:T(8,128)S(1)}, f32[2,384,640]{2,1,0:T(8,128)S(1)}, bf16[2,384,640]{2,1,0:T(8,128)(2,1)S(1)}, bf16[2,384,640]{2,1,0:T(8,128)(2,1)S(1)}) custom-call(s32[1]{0:T(128)} %bitcast.far_ref, bf16[800,640]{1,0:T(8,128)(2,1)S(1)} %collective-permute-done.7.refs_0_, ...), custom_call_target="tpu_custom_call" | custom-call | flops 7549747200 | bytes 4915200 | tf_op jit(solution)/shard_map/pairs/pallas_call | solution.py:297
  95.5 2.5 %collective-permute-done.9.from_partner = bf16[384,512]{1,0:T(8,128)(2,1)S(1)} collective-permute-done((bf16[384,512]{1,0:T(8,128)(2,1)S(1)}, bf16[384,512]{1,0:T(8,128)(2,1)S(1)}, u32[]{:S(2)}, u32[]{:S(2)}) %collective-permute-start.9) | collective-permute-done | bytes 393248 | tf_op jit(solution)/shard_map/ppermute | solution.py:437
  97.9 19.4 %collective-permute-start.14 = (bf16[2,384,640]{2,1,0:T(8,128)(2,1)S(1)}, bf16[2,384,640]{2,1,0:T(8,128)(2,1)S(1)}, u32[]{:S(2)}, u32[]{:S(2)}) collective-permute-start(bf16[2,384,640]{2,1,0:T(8,128)(2,1)S(1)} %get-tuple-element.108), channel_id=1, source_target_pairs={{0,8},{8,0},{16,24},{24,16},{1,9},{9,1},{17,25},{25,17},{2,10},{10... | collective-permute-start | bytes 2949128 | tf_op jit(solution)/shard_map/ppermute | solution.py:437
  117.4 0.7 collective-permute-start.15
  118.1 1.9 %collective-permute-start.13 = (bf16[384,640]{1,0:T(8,128)(2,1)S(1)}, bf16[384,640]{1,0:T(8,128)(2,1)S(1)}, u32[]{:S(2)}, u32[]{:S(2)}) collective-permute-start(bf16[384,640]{1,0:T(8,128)(2,1)S(1)} %get-tuple-element.107), channel_id=1, source_target_pairs={{0,0},{7,7},{1,2},{2,1},{3,4},{4,3},{5,6},{6,5},{8,8},{15,15},{9,1... | collective-permute-start | bytes 1474568 | tf_op jit(solution)/shard_map/ppermute | solution.py:437
  120.0 5.2 %pairs.17 = (bf16[384,384]{1,0:T(8,128)(2,1)S(1)}, f32[384,384]{1,0:T(8,128)S(1)}, f32[2,384,384]{2,1,0:T(8,128)S(1)}, bf16[2,384,384]{2,1,0:T(8,128)(2,1)S(1)}, bf16[2,384,384]{2,1,0:T(8,128)(2,1)S(1)}) custom-call(s32[1]{0:T(128)} %bitcast.far_ref, bf16[800,384]{1,0:T(8,128)(2,1)S(1)} %collective-permute-done.6.refs_0_, ...), custom_call_target="tpu_custom_call" | custom-call | flops 9059696640 | bytes 2949120 | tf_op jit(solution)/shard_map/pairs/pallas_call | solution.py:297
  125.2 0.0 collective-permute-done.12.from_partner
  125.2 4.3 %collective-permute-start.18 = (bf16[2,384,384]{2,1,0:T(8,128)(2,1)S(1)}, bf16[2,384,384]{2,1,0:T(8,128)(2,1)S(1)}, u32[]{:S(2)}, u32[]{:S(2)}) collective-permute-start(bf16[2,384,384]{2,1,0:T(8,128)(2,1)S(1)} %get-tuple-element.116), channel_id=1, source_target_pairs={{0,8},{8,0},{16,24},{24,16},{1,9},{9,1},{17,25},{25,17},{2,10},{10... | collective-permute-start | bytes 1769480 | tf_op jit(solution)/shard_map/ppermute | solution.py:437
  129.5 0.0 collective-permute-done.11.far
  129.5 0.7 collective-permute-start.19
  130.2 4.5 %collective-permute-done.13.from_outer = bf16[384,640]{1,0:T(8,128)(2,1)S(1)} collective-permute-done((bf16[384,640]{1,0:T(8,128)(2,1)S(1)}, bf16[384,640]{1,0:T(8,128)(2,1)S(1)}, u32[]{:S(2)}, u32[]{:S(2)}) %collective-permute-start.13) | collective-permute-done | bytes 491552 | tf_op jit(solution)/shard_map/ppermute | solution.py:437
  134.7 1.9 %collective-permute-start.17 = (bf16[384,384]{1,0:T(8,128)(2,1)S(1)}, bf16[384,384]{1,0:T(8,128)(2,1)S(1)}, u32[]{:S(2)}, u32[]{:S(2)}) collective-permute-start(bf16[384,384]{1,0:T(8,128)(2,1)S(1)} %get-tuple-element.115), channel_id=1, source_target_pairs={{0,0},{7,7},{1,2},{2,1},{3,4},{4,3},{5,6},{6,5},{8,8},{15,15},{9,1... | collective-permute-start | bytes 884744 | tf_op jit(solution)/shard_map/ppermute | solution.py:437
  136.6 1.3 finish.3
  137.9 1.4 finish.4
  139.3 10.8 %collective-permute-done.16.from_partner = bf16[384,384]{1,0:T(8,128)(2,1)S(1)} collective-permute-done((bf16[384,384]{1,0:T(8,128)(2,1)S(1)}, bf16[384,384]{1,0:T(8,128)(2,1)S(1)}, u32[]{:S(2)}, u32[]{:S(2)}) %collective-permute-start.16) | collective-permute-done | bytes 294944 | tf_op jit(solution)/shard_map/ppermute | solution.py:437
  150.1 0.0 collective-permute-done.17.from_outer
  150.1 0.0 collective-permute-done.18.near
  150.1 0.0 collective-permute-done.19.far
  150.1 1.1 finish.5
  (11 shorter events, 0.0 us)
Async XLA Ops:
  0.6 4.0 %copy-start = (f32[1,1,12,384]{3,1,2,0:T(1,128)S(1)}, f32[1,1,12,384]{3,1,2,0:T(1,128)}, u32[]{:S(2)}) copy-start(f32[1,1,12,384]{3,1,2,0:T(1,128)} %param.12) | copy-start | bytes 55300
  0.6 4.0 %copy-start.1 = (s32[1,1,9]{2,1,0:T(1,128)S(1)}, s32[1,1,9]{2,1,0:T(1,128)}, u32[]{:S(2)}) copy-start(s32[1,1,9]{2,1,0:T(1,128)} %param.13) | copy-start | bytes 112
  2.4 12.8 %collective-permute-start.2 = (bf16[2,384,1536]{2,1,0:T(8,128)(2,1)S(1)}, bf16[2,384,1536]{2,1,0:T(8,128)(2,1)}, u32[]{:S(2)}, u32[]{:S(2)}) collective-permute-start(bf16[2,384,1536]{2,1,0:T(8,128)(2,1)S(1)} %pack.1.refs_1_.refs_3_.refs_2_), channel_id=1, source_target_pairs={{0,8},{8,0},{16,24},{24,16},{1,9},{9,1},{17,25},{25,17},{2,10},{10... | collective-permute-start | bytes 7077896 | tf_op jit(solution)/shard_map/ppermute | solution.py:391
  2.5 48.0 %collective-permute-start.5 = (bf16[2,384,1536]{2,1,0:T(8,128)(2,1)S(1)}, bf16[2,384,1536]{2,1,0:T(8,128)(2,1)}, u32[]{:S(2)}, u32[]{:S(2)}) collective-permute-start(bf16[2,384,1536]{2,1,0:T(8,128)(2,1)S(1)} %pack.1.refs_1_.refs_3_.refs_2_), channel_id=1, source_target_pairs={{0,0},{24,24},{8,16},{16,8},{1,1},{25,25},{9,17},{17,9},{2,2},{26,... | collective-permute-start | bytes 7077896 | tf_op jit(solution)/shard_map/ppermute | solution.py:392
  7.7 24.7 %collective-permute-start.1 = (bf16[800,512]{1,0:T(8,128)(2,1)}, bf16[800,512]{1,0:T(8,128)(2,1)}, u32[]{:S(2)}, u32[]{:S(2)}) collective-permute-start(bf16[800,512]{1,0:T(8,128)(2,1)} %prep.2.refs_0_.refs_1_), channel_id=1, source_target_pairs={{0,1},{1,0},{2,3},{3,2},{4,5},{5,4},{6,7},{7,6},{8,9},{9,8},{10,11... | collective-permute-start | bytes 2457608 | tf_op jit(solution)/shard_map/ppermute | solution.py:397
  13.2 37.3 %collective-permute-start.4 = (bf16[800,640]{1,0:T(8,128)(2,1)}, bf16[800,640]{1,0:T(8,128)(2,1)S(1)}, u32[]{:S(2)}, u32[]{:S(2)}) collective-permute-start(bf16[800,640]{1,0:T(8,128)(2,1)} %get-tuple-element.67.refs_0_.refs_1_), channel_id=1, source_target_pairs={{0,1},{1,0},{2,3},{3,2},{4,5},{5,4},{6,7},{7,6},{8,9},{9,8},{10,11... | collective-permute-start | bytes 3072008 | tf_op jit(solution)/shard_map/ppermute | solution.py:456
  13.7 53.4 %collective-permute-start = (bf16[800,384]{1,0:T(8,128)(2,1)}, bf16[800,384]{1,0:T(8,128)(2,1)}, u32[]{:S(2)}, u32[]{:S(2)}) collective-permute-start(bf16[800,384]{1,0:T(8,128)(2,1)} %get-tuple-element.70.refs_0_.refs_1_), channel_id=1, source_target_pairs={{0,1},{1,0},{2,3},{3,2},{4,5},{5,4},{6,7},{7,6},{8,9},{9,8},{10,11... | collective-permute-start | bytes 1843208 | tf_op jit(solution)/shard_map/ppermute | solution.py:456
  32.4 27.7 %collective-permute-start.3 = (bf16[800,512]{1,0:T(8,128)(2,1)}, bf16[800,512]{1,0:T(8,128)(2,1)S(1)}, u32[]{:S(2)}, u32[]{:S(2)}) collective-permute-start(bf16[800,512]{1,0:T(8,128)(2,1)} %collective-permute-done.1.refs_0_.refs_2_), channel_id=1, source_target_pairs={{0,2},{2,4},{4,6},{6,0},{1,7},{3,1},{5,3},{7,5},{8,10},{10,12},{12... | collective-permute-start | bytes 2457608 | tf_op jit(solution)/shard_map/ppermute | solution.py:443
  50.5 35.0 %collective-permute-start.7 = (bf16[800,640]{1,0:T(8,128)(2,1)S(1)}, bf16[800,640]{1,0:T(8,128)(2,1)S(1)}, u32[]{:S(2)}, u32[]{:S(2)}) collective-permute-start(bf16[800,640]{1,0:T(8,128)(2,1)S(1)} %collective-permute-done.4.refs_0_), channel_id=1, source_target_pairs={{0,2},{2,4},{4,6},{6,0},{1,7},{3,1},{5,3},{7,5},{8,10},{10,12},{12... | collective-permute-start | bytes 3072008 | tf_op jit(solution)/shard_map/ppermute | solution.py:443
  58.0 67.1 %collective-permute-start.12 = (bf16[384,640]{1,0:T(8,128)(2,1)S(1)}, bf16[384,640]{1,0:T(8,128)(2,1)S(1)}, u32[]{:S(2)}, u32[]{:S(2)}) collective-permute-start(bf16[384,640]{1,0:T(8,128)(2,1)S(1)} %get-tuple-element.106), channel_id=1, source_target_pairs={{0,1},{1,0},{2,3},{3,2},{4,5},{5,4},{6,7},{7,6},{8,9},{9,8},{10,11... | collective-permute-start | bytes 1474568 | tf_op jit(solution)/shard_map/ppermute | solution.py:437
  67.1 19.6 %collective-permute-start.8 = (bf16[384,512]{1,0:T(8,128)(2,1)S(1)}, bf16[384,512]{1,0:T(8,128)(2,1)S(1)}, u32[]{:S(2)}, u32[]{:S(2)}) collective-permute-start(bf16[384,512]{1,0:T(8,128)(2,1)S(1)} %get-tuple-element.86), channel_id=1, source_target_pairs={{0,0},{7,7},{1,2},{2,1},{3,4},{4,3},{5,6},{6,5},{8,8},{15,15},{9,1... | collective-permute-start | bytes 1179656 | tf_op jit(solution)/shard_map/ppermute | solution.py:437
  70.6 47.5 %collective-permute-start.10 = (bf16[2,384,512]{2,1,0:T(8,128)(2,1)S(1)}, bf16[2,384,512]{2,1,0:T(8,128)(2,1)S(1)}, u32[]{:S(2)}, u32[]{:S(2)}) collective-permute-start(bf16[2,384,512]{2,1,0:T(8,128)(2,1)S(1)} %get-tuple-element.93), channel_id=1, source_target_pairs={{0,8},{8,0},{16,24},{24,16},{1,9},{9,1},{17,25},{25,17},{2,10},{10... | collective-permute-start | bytes 2359304 | tf_op jit(solution)/shard_map/ppermute | solution.py:437
  79.9 37.5 %collective-permute-start.6 = (bf16[800,384]{1,0:T(8,128)(2,1)}, bf16[800,384]{1,0:T(8,128)(2,1)S(1)}, u32[]{:S(2)}, u32[]{:S(2)}) collective-permute-start(bf16[800,384]{1,0:T(8,128)(2,1)} %collective-permute-done.refs_0_), channel_id=1, source_target_pairs={{0,2},{2,4},{4,6},{6,0},{1,7},{3,1},{5,3},{7,5},{8,10},{10,12},{12... | collective-permute-start | bytes 1843208 | tf_op jit(solution)/shard_map/ppermute | solution.py:443
  85.6 12.3 %collective-permute-start.9 = (bf16[384,512]{1,0:T(8,128)(2,1)S(1)}, bf16[384,512]{1,0:T(8,128)(2,1)S(1)}, u32[]{:S(2)}, u32[]{:S(2)}) collective-permute-start(bf16[384,512]{1,0:T(8,128)(2,1)S(1)} %get-tuple-element.92), channel_id=1, source_target_pairs={{0,1},{1,0},{2,3},{3,2},{4,5},{5,4},{6,7},{7,6},{8,9},{9,8},{10,11... | collective-permute-start | bytes 1179656 | tf_op jit(solution)/shard_map/ppermute | solution.py:437
  86.7 42.8 %collective-permute-start.11 = (bf16[2,384,512]{2,1,0:T(8,128)(2,1)S(1)}, bf16[2,384,512]{2,1,0:T(8,128)(2,1)S(1)}, u32[]{:S(2)}, u32[]{:S(2)}) collective-permute-start(bf16[2,384,512]{2,1,0:T(8,128)(2,1)S(1)} %get-tuple-element.103), channel_id=1, source_target_pairs={{0,0},{24,24},{8,16},{16,8},{1,1},{25,25},{9,17},{17,9},{2,2},{26,... | collective-permute-start | bytes 2359304 | tf_op jit(solution)/shard_map/ppermute | solution.py:437
  97.9 36.8 %collective-permute-start.14 = (bf16[2,384,640]{2,1,0:T(8,128)(2,1)S(1)}, bf16[2,384,640]{2,1,0:T(8,128)(2,1)S(1)}, u32[]{:S(2)}, u32[]{:S(2)}) collective-permute-start(bf16[2,384,640]{2,1,0:T(8,128)(2,1)S(1)} %get-tuple-element.108), channel_id=1, source_target_pairs={{0,8},{8,0},{16,24},{24,16},{1,9},{9,1},{17,25},{25,17},{2,10},{10... | collective-permute-start | bytes 2949128 | tf_op jit(solution)/shard_map/ppermute | solution.py:437
  117.4 20.6 %collective-permute-start.15 = (bf16[2,384,640]{2,1,0:T(8,128)(2,1)S(1)}, bf16[2,384,640]{2,1,0:T(8,128)(2,1)S(1)}, u32[]{:S(2)}, u32[]{:S(2)}) collective-permute-start(bf16[2,384,640]{2,1,0:T(8,128)(2,1)S(1)} %get-tuple-element.109), channel_id=1, source_target_pairs={{0,0},{24,24},{8,16},{16,8},{1,1},{25,25},{9,17},{17,9},{2,2},{26,... | collective-permute-start | bytes 2949128 | tf_op jit(solution)/shard_map/ppermute | solution.py:437
  118.1 16.6 %collective-permute-start.13 = (bf16[384,640]{1,0:T(8,128)(2,1)S(1)}, bf16[384,640]{1,0:T(8,128)(2,1)S(1)}, u32[]{:S(2)}, u32[]{:S(2)}) collective-permute-start(bf16[384,640]{1,0:T(8,128)(2,1)S(1)} %get-tuple-element.107), channel_id=1, source_target_pairs={{0,0},{7,7},{1,2},{2,1},{3,4},{4,3},{5,6},{6,5},{8,8},{15,15},{9,1... | collective-permute-start | bytes 1474568 | tf_op jit(solution)/shard_map/ppermute | solution.py:437
  125.2 24.9 %collective-permute-start.18 = (bf16[2,384,384]{2,1,0:T(8,128)(2,1)S(1)}, bf16[2,384,384]{2,1,0:T(8,128)(2,1)S(1)}, u32[]{:S(2)}, u32[]{:S(2)}) collective-permute-start(bf16[2,384,384]{2,1,0:T(8,128)(2,1)S(1)} %get-tuple-element.116), channel_id=1, source_target_pairs={{0,8},{8,0},{16,24},{24,16},{1,9},{9,1},{17,25},{25,17},{2,10},{10... | collective-permute-start | bytes 1769480 | tf_op jit(solution)/shard_map/ppermute | solution.py:437
  129.5 20.6 %collective-permute-start.19 = (bf16[2,384,384]{2,1,0:T(8,128)(2,1)S(1)}, bf16[2,384,384]{2,1,0:T(8,128)(2,1)S(1)}, u32[]{:S(2)}, u32[]{:S(2)}) collective-permute-start(bf16[2,384,384]{2,1,0:T(8,128)(2,1)S(1)} %get-tuple-element.117), channel_id=1, source_target_pairs={{0,0},{24,24},{8,16},{16,8},{1,1},{25,25},{9,17},{17,9},{2,2},{26,... | collective-permute-start | bytes 1769480 | tf_op jit(solution)/shard_map/ppermute | solution.py:437
  134.7 15.3 %collective-permute-start.16 = (bf16[384,384]{1,0:T(8,128)(2,1)S(1)}, bf16[384,384]{1,0:T(8,128)(2,1)S(1)}, u32[]{:S(2)}, u32[]{:S(2)}) collective-permute-start(bf16[384,384]{1,0:T(8,128)(2,1)S(1)} %get-tuple-element.114), channel_id=1, source_target_pairs={{0,1},{1,0},{2,3},{3,2},{4,5},{5,4},{6,7},{7,6},{8,9},{9,8},{10,11... | collective-permute-start | bytes 884744 | tf_op jit(solution)/shard_map/ppermute | solution.py:437
  134.7 15.3 %collective-permute-start.17 = (bf16[384,384]{1,0:T(8,128)(2,1)S(1)}, bf16[384,384]{1,0:T(8,128)(2,1)S(1)}, u32[]{:S(2)}, u32[]{:S(2)}) collective-permute-start(bf16[384,384]{1,0:T(8,128)(2,1)S(1)} %get-tuple-element.115), channel_id=1, source_target_pairs={{0,0},{7,7},{1,2},{2,1},{3,4},{4,3},{5,6},{6,5},{8,8},{15,15},{9,1... | collective-permute-start | bytes 884744 | tf_op jit(solution)/shard_map/ppermute | solution.py:437
